TPU v7x, 256 devices: a whole 4x4x8 slice. The times are simulated.
256 devices in a mesh: train: 16 (over z_lo, x, core), feat: 16 (over y, z_hi).
Axes of the slice: x: 4, y: 4, z: 8 (z_hi: 4, z_lo: 2; z = z_hi * 2 + z_lo), core: 2. Of those that a mesh axis runs over, the one named last changes fastest.
Arguments:
- activations: bfloat16 [4096, 4096], P('train', 'feat'), may hold values from -6 to 6
- grad_outputs: bfloat16 [4096, 11008], P('train', 'feat'), may hold values from -6 to 6
- in_basis: bfloat16 [4096, 4096], P('train', 'feat'), may hold values from -0.09375 to 0.09375
- out_basis: bfloat16 [11008, 11008], P('train', 'feat'), may hold values from -0.0546875 to 0.0546875
- eigenvalues: float32 [4096, 11008], P(None, 'feat'), may hold values from 0.2 to 5
- query_left: bfloat16 [4096, 128], P('train'), may hold values from -0.032958984 to 0.032958984
- query_right: bfloat16 [11008, 128], P('train'), may hold values from -0.0017852783 to 0.0017852783
- lengths: int32 [16], P('train'), may hold values from 1 to 256, 2560 in all
Outputs:
- scores: float32 [16, 16], P('train', 'feat')
Inputs may be any that keep to these rules, and one draw needn't show every extreme that they name: lengths sum to 2560 and some sequence has 256.
All inputs are finite; a program needn't handle non-finite values. No bound on the sum of `lengths` on one device may be relied on, other than what follows from the above.
Results may differ from a plain program's by a relative error of at most 0.0049.
Values may be sent and summed in bfloat16 or wider, within the bound.
No kernel may reach another device: no remote copies, remote signals or barrier semaphores. Data moves between devices by JAX's collectives and lax.ppermute only.
A program may use at most 128 MiB of HBM per device.

v0:
```python
import jax
import jax.numpy as jnp
from jax import lax
from jax.sharding import PartitionSpec as P

SEQ_LEN = 256
RANK = 8


damping = 0.01
contract = (((0,), (0,)), ((), ()))


def local(
    activations, grad_outputs, in_basis, out_basis, eigenvalues, query_left, query_right, lengths
):
    seq_here = lengths.shape[0]
    out_cols = out_basis.shape[1]
    factor_cols = query_left.shape[1]
    queries = factor_cols // RANK
    act_full = lax.all_gather(activations, "feat", axis=1, tiled=True)
    basis_rows = lax.all_gather(in_basis, "train", axis=0, tiled=True)
    left_rows = lax.all_gather(query_left, "train", axis=0, tiled=True)
    columns = act_full
    first = jnp.dot(columns, basis_rows, preferred_element_type=jnp.float32)
    second = lax.dot_general(left_rows, basis_rows, contract, preferred_element_type=jnp.float32)
    in_acc = first
    left_acc = second
    grad_full = lax.all_gather(grad_outputs, "feat", axis=1, tiled=True)
    basis_rows = lax.all_gather(out_basis, "train", axis=0, tiled=True)
    right_rows = lax.all_gather(query_right, "train", axis=0, tiled=True)
    columns = grad_full
    first = jnp.dot(columns, basis_rows, preferred_element_type=jnp.float32)
    second = lax.dot_general(basis_rows, right_rows, contract, preferred_element_type=jnp.float32)
    in_flat = in_acc.astype(jnp.bfloat16)
    out_seq = first.astype(jnp.bfloat16).reshape(seq_here, SEQ_LEN, out_cols)
    left_rot = left_acc.astype(jnp.bfloat16)
    right_rot = second.astype(jnp.bfloat16)
    in_wide, left_wide = (
        lax.all_gather(in_flat, "feat", axis=1, tiled=True),
        lax.all_gather(left_rot, "feat", axis=1, tiled=True),
    )
    left_float = jnp.transpose(left_wide).astype(jnp.float32)
    positions = jnp.arange(SEQ_LEN, dtype=jnp.int32)
    keep = (positions[None, :] < lengths[:, None]).astype(jnp.bfloat16)
    out_seq = out_seq * keep[:, :, None]
    divisor = eigenvalues + damping
    grad = lax.dot_general(in_wide, out_seq[0], contract, preferred_element_type=jnp.float32)
    scaled = (grad / divisor).astype(jnp.bfloat16)
    mapped = jnp.dot(scaled, right_rot, preferred_element_type=jnp.float32)
    total_rows = mapped.shape[0]
    partials = [jnp.sum((mapped * left_float).reshape(total_rows, queries, RANK), axis=(0, 2))]
    partial_scores = jnp.stack(partials, axis=0)
    summed = lax.psum(partial_scores, "feat")
    share = queries // lax.axis_size("feat")
    return lax.dynamic_slice_in_dim(summed, lax.axis_index("feat") * share, share, 1)


def solution(mesh):
    in_specs = (
        P("train", "feat"),
        P("train", "feat"),
        P("train", "feat"),
        P("train", "feat"),
        P(None, "feat"),
        P("train", None),
        P("train", None),
        P("train"),
    )
    out_specs = P("train", "feat")
    return jax.shard_map(local, mesh=mesh, in_specs=in_specs, out_specs=out_specs, check_vma=False)
```

profile of v0, /device:TPU:4, one launch (start us, length us, event | category | flops | bytes accessed | tf_op | source)
XLA Modules:
  0.0 556.0 jit_solution(793794669088355312)
XLA Ops:
  6.5 0.7 all-gather.21.cloned.1.call-update
  7.3 0.0 all-gather.11.cloned.1.call-start
  7.3 0.7 all-gather.11.cloned.1.call-update
  8.0 0.0 all-gather.9.cloned.1.call-start
  8.1 0.7 all-gather.9.cloned.1.call-update
  8.7 0.0 all-gather.15.cloned.1.call-start
  8.8 0.5 all-gather.15.cloned.1.call-update
  9.3 0.0 all-gather.17.cloned.1.call-start
  9.4 0.5 all-gather.17.cloned.1.call-update
  9.9 0.0 all-gather.19.cloned.1.call-start
  9.9 0.5 all-gather.19.cloned.1.call-update
  10.5 0.0 all-gather.23.cloned.1.call-start
  10.5 35.7 %all-gather.21.cloned.1.call-done = bf16[4096,128]{1,0:T(8,128)(2,1)} async-done(((bf16[256,128]{1,0:T(8,128)(2,1)}), bf16[4096,128]{1,0:T(8,128)(2,1)}) %all-gather.21.cloned.1.call-update) | async-done | bytes 1048592 | tf_op jit(solution)/shard_map/all_gather | solution.py:23
  46.3 38.5 %all-gather.11.cloned.1.call-done = bf16[4096,256]{1,0:T(8,128)(2,1)} async-done(((bf16[256,256]{1,0:T(8,128)(2,1)}), bf16[4096,256]{1,0:T(8,128)(2,1)}) %all-gather.11.cloned.1.call-update) | async-done | bytes 2097168 | tf_op jit(solution)/shard_map/all_gather | solution.py:22
  84.8 3.6 convolution_convert_fusion.3
  88.4 0.0 all-gather.23.cloned.1.call-update
  88.4 0.0 all-gather.13.cloned.1.call-start
  88.5 62.6 %all-gather.9.cloned.1.call-done = bf16[256,4096]{1,0:T(8,128)(2,1)} async-done(((bf16[256,256]{1,0:T(8,128)(2,1)}), bf16[256,4096]{1,0:T(8,128)(2,1)}) %all-gather.9.cloned.1.call-update) | async-done | bytes 2097168 | tf_op jit(solution)/shard_map/all_gather | solution.py:21
  151.1 2.9 convolution_convert_fusion.2
  154.0 0.0 all-gather.13.cloned.1.call-update
  154.7 80.2 %all-gather.15.cloned.1.call-done = bf16[256,11008]{0,1:T(8,128)(2,1)} async-done(((bf16[256,688]{0,1:T(8,128)(2,1)}), bf16[256,11008]{0,1:T(8,128)(2,1)}) %all-gather.15.cloned.1.call-update) | async-done | bytes 5636112 | tf_op jit(solution)/shard_map/all_gather | solution.py:29
  234.9 102.2 %all-gather.17.cloned.1.call-done = bf16[11008,688]{1,0:T(8,128)(2,1)} async-done(((bf16[688,688]{1,0:T(8,128)(2,1)}), bf16[11008,688]{1,0:T(8,128)(2,1)}) %all-gather.17.cloned.1.call-update) | async-done | bytes 15147024 | tf_op jit(solution)/shard_map/all_gather | solution.py:30
  337.1 12.0 %fusion.5 = bf16[256,688]{1,0:T(8,128)(2,1)S(1)} fusion(bf16[256,11008]{0,1:T(8,128)(2,1)} %all-gather.15.cloned.1.call-done, bf16[11008,688]{1,0:T(8,128)(2,1)} %all-gather.17.cloned.1.call-done, bf16[256]{0:T(256)(128)(2,1)S(1)} %compare_convert_fusion), kind=kOutput, calls=%fused_computation.6 | convolution fusion | flops 3877986304 | bytes 21135872 | tf_op jit(solution)/shard_map/dot_general | solution.py:33
  349.1 27.9 %all-gather.19.cloned.1.call-done = bf16[11008,128]{1,0:T(8,128)(2,1)} async-done(((bf16[688,128]{1,0:T(8,128)(2,1)}), bf16[11008,128]{1,0:T(8,128)(2,1)}) %all-gather.19.cloned.1.call-update) | async-done | bytes 2818064 | tf_op jit(solution)/shard_map/all_gather | solution.py:31
  377.0 11.2 %convolution_convert_fusion.1 = bf16[688,128]{1,0:T(8,128)(2,1)S(1)} fusion(bf16[11008,688]{1,0:T(8,128)(2,1)} %all-gather.17.cloned.1.call-done, bf16[11008,128]{1,0:T(8,128)(2,1)} %all-gather.19.cloned.1.call-done), kind=kOutput, calls=%fused_computation.7 | convolution fusion | flops 1938905088 | bytes 18141184 | tf_op jit(solution)/shard_map/dot_general | solution.py:34
  388.2 46.2 %all-gather.23.cloned.1.call-done = bf16[128,4096]{0,1:T(8,128)(2,1)} async-done(((bf16[128,256]{0,1:T(8,128)(2,1)}), bf16[128,4096]{0,1:T(8,128)(2,1)}) %all-gather.23.cloned.1.call-update) | async-done | bytes 1048592 | tf_op jit(solution)/shard_map/all_gather | solution.py:41
  434.4 62.5 %all-gather.13.cloned.1.call-done = bf16[256,4096]{1,0:T(8,128)(2,1)} async-done(((bf16[256,256]{1,0:T(8,128)(2,1)}), bf16[256,4096]{1,0:T(8,128)(2,1)}) %all-gather.13.cloned.1.call-update) | async-done | bytes 2097168 | tf_op jit(solution)/shard_map/all_gather | solution.py:40
  496.9 8.8 %fusion.4 = f32[128]{0:T(128)S(1)} fusion(bf16[128,4096]{0,1:T(8,128)(2,1)} %all-gather.23.cloned.1.call-done, bf16[688,128]{1,0:T(8,128)(2,1)S(1)} %convolution_convert_fusion.1, f32[4096,688]{0,1:T(8,128)} %param.12, bf16[256,4096]{1,0:T(8,128)(2,1)} %all-gather.13.cloned.1.call-done, bf16[256,688]{1,0:T(8,128)(2,1)S(1)} %fusion.5), kind=kOutput, calls=%fused_computation.4 | convolution fusion | flops 2174287872 | bytes 14946816 | tf_op jit(solution)/shard_map/dot_general | solution.py:50
  505.7 0.1 reduce_sum.14
  505.8 0.1 reduce_sum.18
  505.9 42.7 %psum.7 = f32[1,16]{1,0:T(1,128)S(1)} all-reduce(f32[1,16]{1,0:T(1,128)S(1)} %bitcast.18), channel_id=1, replica_groups=mesh['train'=16,'feat'=16] {'feat'}, use_global_device_ids=true, to_apply=%region_2.3 | all-reduce | flops 16 | bytes 128 | tf_op jit(solution)/shard_map/psum | solution.py:54
  548.6 0.6 constant_dynamic-slice_fusion
  (4 shorter events, 0.0 us)
Async XLA Ops:
  6.5 39.7 %all-gather.21.cloned.1.call-start = ((), (), s32[]{:S(2)}) async-start(), calls=%async_computation.6 | async-start | bytes 1114112 | tf_op jit(solution)/shard_map/all_gather | solution.py:23
  7.3 77.5 %all-gather.11.cloned.1.call-start = ((), (), s32[]{:S(2)}) async-start(), calls=%async_computation.1 | async-start | bytes 2228224 | tf_op jit(solution)/shard_map/all_gather | solution.py:22
  8.0 143.1 %all-gather.9.cloned.1.call-start = ((), (), s32[]{:S(2)}) async-start(), calls=%async_computation | async-start | bytes 2228224 | tf_op jit(solution)/shard_map/all_gather | solution.py:21
  8.7 226.2 %all-gather.15.cloned.1.call-start = ((), (), s32[]{:S(2)}) async-start(), calls=%async_computation.3 | async-start | bytes 5988352 | tf_op jit(solution)/shard_map/all_gather | solution.py:29
  9.3 327.8 %all-gather.17.cloned.1.call-start = ((), (), s32[]{:S(2)}) async-start(), calls=%async_computation.4 | async-start | bytes 17965056 | tf_op jit(solution)/shard_map/all_gather | solution.py:30
  9.9 367.1 %all-gather.19.cloned.1.call-start = ((), (), s32[]{:S(2)}) async-start(), calls=%async_computation.5 | async-start | bytes 2994176 | tf_op jit(solution)/shard_map/all_gather | solution.py:31
  10.5 423.9 %all-gather.23.cloned.1.call-start = ((), (), s32[]{:S(2)}) async-start(), calls=%async_computation.7 | async-start | bytes 1114112 | tf_op jit(solution)/shard_map/all_gather | solution.py:41
  84.8 66.3 %copy-start = (bf16[4096,256]{1,0:T(8,128)(2,1)S(1)}, bf16[4096,256]{1,0:T(8,128)(2,1)}, u32[]{:S(2)}) copy-start(bf16[4096,256]{1,0:T(8,128)(2,1)} %all-gather.11.cloned.1.call-done) | copy-start | bytes 6291460
  88.4 408.5 %all-gather.13.cloned.1.call-start = ((), (), s32[]{:S(2)}) async-start(), calls=%async_computation.2 | async-start | bytes 2228224 | tf_op jit(solution)/shard_map/all_gather | solution.py:40
Sparse Core Ops, SparseCore 0:
  9.2 36.9 all-gather.20
  48.1 36.6 all-gather.10
  87.2 63.8 all-gather.8
  153.4 81.4 all-gather.14
  236.6 100.4 all-gather.16
  338.8 38.1 all-gather.18
  379.4 54.9 all-gather.22
  436.8 60.0 all-gather.12
where the time goes:
time: 556 us
  waiting for transfers between devices  460 us (83%)
  blocking collectives  42.7 us (8%)
  matrix products  38.6 us (7%)
  between operations  14.2 us (3%)
    all_gather x1, waiting for transfers between devices, local(): basis_rows = lax.all_gather(out_basis, 'train', axis=0, tiled=True)  102 us
    all_gather x1, waiting for transfers between devices, local(): grad_full = lax.all_gather(grad_outputs, 'feat', axis=1, tiled=True)  80.2 us
    all_gather x1, waiting for transfers between devices, local(): act_full = lax.all_gather(activations, 'feat', axis=1, tiled=True)  62.6 us
    all_gather x1, waiting for transfers between devices, local(): lax.all_gather(in_flat, 'feat', axis=1, tiled=True)  62.5 us
    all_gather x1, waiting for transfers between devices, local(): lax.all_gather(left_rot, 'feat', axis=1, tiled=True)  46.2 us
    psum x1, blocking collectives, local(): summed = lax.psum(partial_scores, 'feat')  42.7 us
    all_gather x1, waiting for transfers between devices, local(): basis_rows = lax.all_gather(in_basis, 'train', axis=0, tiled=True)  38.5 us
    all_gather x1, waiting for transfers between devices, local(): left_rows = lax.all_gather(query_left, 'train', axis=0, tiled=True)  35.7 us
  transfers between devices with their start and end apart: 8, of which 8 were waited for; matrix products, arithmetic and copies ran while one was open for 5% of the time, Pallas kernels for 0%

commit v1 on v0

v1 whole, which is shorter than its diff:
```python
import jax
import jax.numpy as jnp
from jax import lax
from jax.experimental import pallas as pl
from jax.experimental.pallas import tpu as pltpu
from jax.sharding import Mesh, PartitionSpec as P

SEQ_LEN = 256
RANK = 8
damping = 0.01
AXES = ("zlo", "x", "core", "y", "zhi")
SIZES = (2, 4, 2, 4, 4)
TRAIN = ("zlo", "x", "core")
FEAT = ("y", "zhi")
over_rows = (((0,), (0,)), ((), ()))


def shift(block, axis, step):
    size = SIZES[AXES.index(axis)]
    return lax.ppermute(block, axis, [(i, (i + step) % size) for i in range(size)])


def ring(block, axis, cut):
    one, three = shift(block, axis, 1), shift(block, axis, -1)
    two = jnp.concatenate([shift(one[:cut], axis, 1), shift(three[cut:], axis, -1)], axis=0)
    return [block, one, two, three]


def direct(block, axis):
    return [block] + [shift(block, axis, step) for step in (1, 2, 3)]


def rotate_kernel(order, lhs, rhs, out, acc):
    step = pl.program_id(0)

    @pl.when(step == 0)
    def _():
        acc[...] = jnp.zeros_like(acc)

    acc[...] += jnp.dot(lhs[0], rhs[0], preferred_element_type=jnp.float32)

    @pl.when(step == pl.num_programs(0) - 1)
    def _():
        out[...] = acc[...].astype(out.dtype)


def rotate_in(order, lhs, rhs):
    blocks, rows, depth = lhs.shape
    cols = rhs.shape[2]
    return pl.pallas_call(
        rotate_kernel,
        grid_spec=pltpu.PrefetchScalarGridSpec(
            num_scalar_prefetch=1,
            grid=(blocks,),
            in_specs=[
                pl.BlockSpec((1, rows, depth), lambda b, order: (b, 0, 0)),
                pl.BlockSpec((1, depth, cols), lambda b, order: (order[b], 0, 0)),
            ],
            out_specs=pl.BlockSpec((rows, cols), lambda b, order: (0, 0)),
            scratch_shapes=[pltpu.VMEM((rows, cols), jnp.float32)],
        ),
        out_shape=jax.ShapeDtypeStruct((rows, cols), jnp.bfloat16),
        compiler_params=pltpu.CompilerParams(vmem_limit_bytes=32 << 20),
    )(order, lhs, rhs)


def rotate_out_kernel(order, live, lhs, rhs, out, acc):
    step = pl.program_id(0)

    @pl.when(step == 0)
    def _():
        acc[...] = jnp.zeros_like(acc)

    acc[...] += lax.dot_general(lhs[0], rhs[0], over_rows, preferred_element_type=jnp.float32)

    @pl.when(step == pl.num_programs(0) - 1)
    def _():
        position = lax.broadcasted_iota(jnp.int32, acc.shape, 0)
        kept = jnp.where(position < live[0], acc[...], 0.0)
        out[...] = kept.T.astype(out.dtype)


def rotate_out(order, live, lhs, rhs):
    blocks, depth, rows = lhs.shape
    cols = rhs.shape[2]
    return pl.pallas_call(
        rotate_out_kernel,
        grid_spec=pltpu.PrefetchScalarGridSpec(
            num_scalar_prefetch=2,
            grid=(blocks,),
            in_specs=[
                pl.BlockSpec((1, depth, rows), lambda b, order, live: (b, 0, 0)),
                pl.BlockSpec((1, depth, cols), lambda b, order, live: (order[b], 0, 0)),
            ],
            out_specs=pl.BlockSpec((cols, rows), lambda b, order, live: (0, 0)),
            scratch_shapes=[pltpu.VMEM((rows, cols), jnp.float32)],
        ),
        out_shape=jax.ShapeDtypeStruct((cols, rows), jnp.bfloat16),
        compiler_params=pltpu.CompilerParams(vmem_limit_bytes=32 << 20),
    )(order, live, lhs, rhs)


def score_kernel(order, out_t, right, rows, eig, left, total, acc):
    step = pl.program_id(0)

    @pl.when(step == 0)
    def _():
        acc[...] = jnp.zeros_like(acc)

    grad = jnp.dot(out_t[...], rows[0], preferred_element_type=jnp.float32)
    scaled = (grad / (eig[...] + damping)).astype(jnp.bfloat16)
    mapped = jnp.dot(right[...], scaled, preferred_element_type=jnp.float32)
    acc[...] += mapped * left[0].astype(jnp.float32)

    @pl.when(step == pl.num_programs(0) - 1)
    def _():
        total[...] = acc[...]


def score(order, out_t, right, rows, eig_t, left):
    blocks, seq, width = rows.shape
    slab = out_t.shape[0]
    factors = right.shape[0]
    return pl.pallas_call(
        score_kernel,
        grid_spec=pltpu.PrefetchScalarGridSpec(
            num_scalar_prefetch=1,
            grid=(blocks,),
            in_specs=[
                pl.BlockSpec((slab, seq), lambda b, order: (0, 0)),
                pl.BlockSpec((factors, slab), lambda b, order: (0, 0)),
                pl.BlockSpec((1, seq, width), lambda b, order: (b, 0, 0)),
                pl.BlockSpec((slab, width), lambda b, order: (0, order[b])),
                pl.BlockSpec((1, factors, width), lambda b, order: (order[b], 0, 0)),
            ],
            out_specs=pl.BlockSpec((factors, width), lambda b, order: (0, 0)),
            scratch_shapes=[pltpu.VMEM((factors, width), jnp.float32)],
        ),
        out_shape=jax.ShapeDtypeStruct((factors, width), jnp.float32),
        compiler_params=pltpu.CompilerParams(vmem_limit_bytes=32 << 20),
    )(order, out_t, right, rows, eig_t, left)


def local(
    activations, grad_outputs, in_basis, out_basis, eigenvalues, query_left, query_right, lengths
):
    zlo, x, core = lax.axis_index("zlo"), lax.axis_index("x"), lax.axis_index("core")
    y, zhi = lax.axis_index("y"), lax.axis_index("zhi")
    bf16, f32 = jnp.bfloat16, jnp.float32
    trains, feats = 16, 16
    factors = query_left.shape[1]
    slab = out_basis.shape[1]
    width = in_basis.shape[1]

    basis = lax.all_gather(out_basis, TRAIN, axis=0, tiled=False)

    place = jnp.arange(feats, dtype=jnp.int32)
    block_y = lax.rem(y - place // 4 + 4, 4)
    block_z = lax.rem(zhi - place % 4 + 4, 4)
    order = (block_y * 4 + block_z).astype(jnp.int32)

    act_z = jnp.stack(direct(activations, "zhi"))
    act_all = jnp.stack(direct(act_z, "y")).reshape(feats, SEQ_LEN, width)

    u_x = jnp.stack(direct(in_basis, "x"))
    u_z = jnp.stack([u_x, shift(u_x, "zlo", 1)])
    u_all = jnp.stack([u_z, shift(u_z, "core", 1)]).reshape(trains, width, width)
    u_place = (
        lax.rem(core + order, 2) * 8
        + lax.rem(zlo + order // 8, 2) * 4
        + lax.rem(x - lax.rem(order // 2, 4) + 4, 4)
    ).astype(jnp.int32)

    grad_t = jnp.transpose(grad_outputs)
    cut = 352
    grad_z = ring(grad_t, "zhi", cut)
    grad_yz = [ring(block, "y", cut) for block in grad_z]
    grad_all = jnp.stack([grad_yz[z][k] for k in range(4) for z in range(4)])

    left_part = lax.dot_general(query_left, in_basis, over_rows, preferred_element_type=f32)
    right_part = lax.dot_general(query_right, out_basis, over_rows, preferred_element_type=f32)
    share = factors // trains
    parts = jnp.concatenate([right_part, left_part], axis=1).reshape(trains, share, slab + width)
    mine = jnp.sum(lax.all_to_all(parts, TRAIN, 0, 0), axis=0).astype(bf16)
    right_mine, left_mine = mine[:, :slab], mine[:, slab:]
    left_feat = lax.all_to_all(
        jnp.broadcast_to(left_mine[None], (feats, share, width)), FEAT, 0, 0
    )
    left_cols = jnp.transpose(left_feat, (1, 0, 2)).reshape(share, feats * width)
    both = jnp.concatenate([right_mine, left_cols], axis=1)
    both = lax.all_to_all(jnp.broadcast_to(both[None], (trains,) + both.shape), TRAIN, 0, 0)
    both = both.reshape(factors, slab + feats * width)
    right = both[:, :slab]
    left = jnp.transpose(both[:, slab:].reshape(factors, feats, width), (1, 0, 2))

    in_rot = rotate_in(u_place, act_all, u_all)
    in_z = jnp.stack(direct(in_rot, "zhi"))
    in_all = jnp.stack(direct(in_z, "y")).reshape(feats, SEQ_LEN, width)

    out_t = rotate_out(order, lengths, grad_all, basis)
    total = score(order, out_t, right, in_all, jnp.transpose(eigenvalues), left)
    queries = factors // RANK
    partial = jnp.sum(jnp.sum(total, axis=1).reshape(queries, RANK), axis=1)
    pieces = lax.all_to_all(partial.reshape(feats, 1, 1), FEAT, 0, 0)
    return jnp.sum(pieces, axis=0)


def solution(mesh):
    fine = Mesh(mesh.devices.reshape(SIZES), AXES)
    in_specs = (
        P(TRAIN, FEAT),
        P(TRAIN, FEAT),
        P(TRAIN, FEAT),
        P(TRAIN, FEAT),
        P(None, FEAT),
        P(TRAIN, None),
        P(TRAIN, None),
        P(TRAIN),
    )
    return jax.shard_map(
        local, mesh=fine, in_specs=in_specs, out_specs=P(TRAIN, FEAT), check_vma=False
    )
```

time: 556 us -> 274 us (0.49)
  waiting for transfers between devices: 460 us -> 57.2 us
  starting transfers between devices: 0.27 us -> 100 us
  local copies, waits for them, and re-layouts: 0.67 us -> 43.1 us
  matrix products: 38.6 us -> 2.95 us
  blocking collectives: 42.7 us -> 14.6 us
  Pallas kernels: 0 us -> 26.9 us
  other arithmetic: 0.13 us -> 9.81 us
    all_gather x8 -> x1, waiting for transfers between devices: 456 us -> 0.02 us  [local(): basis = lax.all_gather(out_basis, TRAIN, axis=0, tiled=False)]
    ppermute x0 -> x37, starting transfers between devices: none -> 73.4 us  [shift(): lax.ppermute(block, axis, [(i, (i + step) % size) for i in range(size)])]
    ppermute x0 -> x37, waiting for transfers between devices: none -> 47.1 us  [shift(): lax.ppermute(block, axis, [(i, (i + step) % size) for i in range(size)])]
    psum x1 -> x0, blocking collectives: 42.7 us -> none  [local(): summed = lax.psum(partial_scores, 'feat')]
    dot_general x5 -> x2, matrix products: 38.6 us -> 2.95 us  [the longest x1 1.79 us: local(): lax.dot_general(query_right, out_basis, over_rows, preferred_element_type...]
    pallas_call x0 -> x3, Pallas kernels: none -> 26.9 us  [the longest x1 13.6 us: rotate_out(): pl.pallas_call(rotate_out_kernel, grid_spec=pltpu.PrefetchScalarGridSpec(...]
    all_to_all x0 -> x3, starting transfers between devices: none -> 26.6 us  [the longest x1 12.2 us: local(): lax.all_to_all(jnp.broadcast_to(both[None], (trains,) + both.shape), TRAI...]
    unnamed x2 -> x46, local copies, waits for them, and re-layouts: 0.01 us -> 26.5 us
  transfers between devices with their start and end apart: 8 -> 41, of which waited for: 8 -> 14; matrix products, arithmetic and copies ran while one was open for 5% -> 15% of each run, Pallas kernels for 0% -> 1%
where the time goes in v1:
time: 274 us; the launch traced here: 269 us
  starting transfers between devices  100 us (36%)
  waiting for transfers between devices  57.2 us (21%)
  local copies, waits for them, and re-layouts  43.1 us (16%)
  Pallas kernels  26.9 us (10%)
  blocking collectives  14.6 us (5%)
  between operations  14.4 us (5%)
  other arithmetic  9.81 us (4%)
  matrix products  2.95 us (1%)
    ppermute x37, starting transfers between devices, shift(): lax.ppermute(block, axis, [(i, (i + step) % size) for i in range(size)])  73.4 us
    ppermute x37, waiting for transfers between devices, shift(): lax.ppermute(block, axis, [(i, (i + step) % size) for i in range(size)])  47.1 us
    unnamed x46, local copies, waits for them, and re-layouts  26.5 us
    all_to_all x1, blocking collectives, local(): pieces = lax.all_to_all(partial.reshape(feats, 1, 1), FEAT, 0, 0)  14.6 us
    pallas_call x1, Pallas kernels, rotate_out(): pl.pallas_call(rotate_out_kernel, grid_spec=pltpu.PrefetchScalarGridSpec(...  13.6 us
    all_to_all x1, starting transfers between devices, local(): lax.all_to_all(jnp.broadcast_to(both[None], (trains,) + both.shape), TRAI...  12.2 us
    pallas_call x1, Pallas kernels, score(): pl.pallas_call(score_kernel, grid_spec=pltpu.PrefetchScalarGridSpec(num_s...  9.48 us
    all_to_all x1, waiting for transfers between devices, local(): lax.all_to_all(jnp.broadcast_to(left_mine[None], (feats, share, width)),...  9.39 us
  transfers between devices with their start and end apart: 41, of which 14 were waited for; matrix products, arithmetic and copies ran while one was open for 15% of the time, Pallas kernels for 1%

profile of v1, /device:TPU:4, one launch (start us, length us, event | category | flops | bytes accessed | tf_op | source)
XLA Modules:
  0.0 269.0 jit_solution(13940574627418210706)
XLA Ops:
  7.3 3.3 %collective-permute-start = (bf16[688,256]{1,0:T(8,128)(2,1)}, bf16[688,256]{1,0:T(8,128)(2,1)S(1)}, u32[]{:S(2)}, u32[]{:S(2)}) collective-permute-start(bf16[688,256]{1,0:T(8,128)(2,1)} %bitcast.106), channel_id=1, source_target_pairs={{0,1},{1,2},{2,3},{3,0},{4,5},{5,6},{6,7},{7,4},{8,9},{9,10},{10,1... | collective-permute-start | bytes 1056776 | tf_op jit(solution)/shard_map/ppermute | solution.py:20
  10.6 3.1 %collective-permute-start.2 = (bf16[688,256]{1,0:T(8,128)(2,1)}, bf16[688,256]{1,0:T(8,128)(2,1)}, u32[]{:S(2)}, u32[]{:S(2)}) collective-permute-start(bf16[688,256]{1,0:T(8,128)(2,1)} %bitcast.107), channel_id=1, source_target_pairs={{0,3},{1,0},{2,1},{3,2},{4,7},{5,4},{6,5},{7,6},{8,11},{9,8},{10,9... | collective-permute-start | bytes 1056776 | tf_op jit(solution)/shard_map/ppermute | solution.py:20
  13.7 2.8 %collective-permute-start.22 = (bf16[256,256]{1,0:T(8,128)(2,1)}, bf16[256,256]{1,0:T(8,128)(2,1)S(1)}, u32[]{:S(2)}, u32[]{:S(2)}) collective-permute-start(bf16[256,256]{1,0:T(8,128)(2,1)} %param.8), channel_id=1, source_target_pairs={{0,3},{1,0},{2,1},{3,2},{4,7},{5,4},{6,5},{7,6},{8,11},{9,8},{10,9... | collective-permute-start | bytes 393224 | tf_op jit(solution)/shard_map/ppermute | solution.py:20
  16.6 2.1 collective-permute-start.21
  18.7 2.9 %collective-permute-start.20 = (bf16[256,256]{1,0:T(8,128)(2,1)}, bf16[256,256]{1,0:T(8,128)(2,1)S(1)}, u32[]{:S(2)}, u32[]{:S(2)}) collective-permute-start(bf16[256,256]{1,0:T(8,128)(2,1)} %param.8), channel_id=1, source_target_pairs={{0,1},{1,2},{2,3},{3,0},{4,5},{5,6},{6,7},{7,4},{8,9},{9,10},{10,1... | collective-permute-start | bytes 393224 | tf_op jit(solution)/shard_map/ppermute | solution.py:20
  25.6 5.3 %all-to-all-start = ((f32[16,8,944]{2,1,0:T(8,128)}), f32[16,8,944]{2,1,0:T(8,128)S(1)}, u32[]{:S(2)}, u32[]{:S(2)}) async-start(f32[16,8,944]{2,1,0:T(8,128)} %bitcast.18), calls=%async_computation | async-start | bytes 1048576 | tf_op jit(solution)/shard_map/all_to_all | solution.py:184
  31.7 8.4 %collective-permute-done.22 = bf16[256,256]{1,0:T(8,128)(2,1)S(1)} collective-permute-done((bf16[256,256]{1,0:T(8,128)(2,1)}, bf16[256,256]{1,0:T(8,128)(2,1)S(1)}, u32[]{:S(2)}, u32[]{:S(2)}) %collective-permute-start.22) | collective-permute-done | bytes 131104 | tf_op jit(solution)/shard_map/ppermute | solution.py:20
  41.2 6.5 %collective-permute-start.26 = (bf16[256,256]{1,0:T(8,128)(2,1)S(1)}, bf16[256,256]{1,0:T(8,128)(2,1)S(1)}, u32[]{:S(2)}, u32[]{:S(2)}) collective-permute-start(bf16[256,256]{1,0:T(8,128)(2,1)S(1)} %copy-done.14), channel_id=1, source_target_pairs={{0,32},{32,64},{64,96},{96,0},{1,33},{33,65},{65,97},{97,1},{2,34}... | collective-permute-start | bytes 393224 | tf_op jit(solution)/shard_map/ppermute | solution.py:20
  55.1 3.1 %collective-permute-start.25 = (bf16[4,256,256]{2,1,0:T(8,128)(2,1)S(1)}, bf16[4,256,256]{2,1,0:T(8,128)(2,1)S(1)}, u32[]{:S(2)}, u32[]{:S(2)}) collective-permute-start(bf16[4,256,256]{2,1,0:T(8,128)(2,1)S(1)} %get-tuple-element.14), channel_id=1, source_target_pairs={{0,12},{4,0},{8,4},{12,8},{1,13},{5,1},{9,5},{13,9},{2,14},{6,2},{... | collective-permute-start | bytes 1572872 | tf_op jit(solution)/shard_map/ppermute | solution.py:20
  58.3 2.7 %collective-permute-start.1 = (bf16[352,256]{1,0:T(8,128)(2,1)S(1)}, bf16[352,256]{1,0:T(8,128)(2,1)S(1)}, u32[]{:S(2)}, u32[]{:S(2)}) collective-permute-start(bf16[352,256]{1,0:T(8,128)(2,1)S(1)} %slice.56), channel_id=1, source_target_pairs={{0,1},{1,2},{2,3},{3,0},{4,5},{5,6},{6,7},{7,4},{8,9},{9,10},{10,1... | collective-permute-start | bytes 540680 | tf_op jit(solution)/shard_map/ppermute | solution.py:20
  62.0 2.7 collective-permute-start.3
  68.3 11.7 %collective-permute-start.29 = (bf16[4,256,256]{2,1,0:T(8,128)(2,1)S(1)}, bf16[4,256,256]{2,1,0:T(8,128)(2,1)S(1)}, u32[]{:S(2)}, u32[]{:S(2)}) collective-permute-start(bf16[4,256,256]{2,1,0:T(8,128)(2,1)S(1)} %get-tuple-element.12), channel_id=1, source_target_pairs={{0,128},{128,0},{1,129},{129,1},{2,130},{130,2},{3,131},{131,3},{4... | collective-permute-start | bytes 1572872 | tf_op jit(solution)/shard_map/ppermute | solution.py:20
  85.5 2.7 %collective-permute-start.12 = (bf16[688,256]{1,0:T(8,128)(2,1)S(1)}, bf16[688,256]{1,0:T(8,128)(2,1)S(1)}, u32[]{:S(2)}, u32[]{:S(2)}) collective-permute-start(bf16[688,256]{1,0:T(8,128)(2,1)S(1)} %collective-permute-done), channel_id=1, source_target_pairs={{0,12},{4,0},{8,4},{12,8},{1,13},{5,1},{9,5},{13,9},{2,14},{6,2},{... | collective-permute-start | bytes 1056776 | tf_op jit(solution)/shard_map/ppermute | solution.py:20
  88.2 1.9 collective-permute-start.18
  95.0 2.3 collective-permute-start.8
  100.3 2.2 collective-permute-start.15
  107.0 9.1 %all-to-all-start.1 = ((bf16[16,8,256]{2,1,0:T(8,128)(2,1)}), bf16[16,8,256]{2,1,0:T(8,128)(2,1)S(1)}, u32[]{:S(2)}, u32[]{:S(2)}) async-start(bf16[16,8,256]{2,1,0:T(8,128)(2,1)} %broadcast_in_dim.4), calls=%async_computation.1 | async-start | bytes 131072 | tf_op jit(solution)/shard_map/all_to_all | solution.py:186
  116.9 9.4 %all-to-all-done.1 = bf16[16,8,256]{2,1,0:T(8,128)(2,1)S(1)} async-done(((bf16[16,8,256]{2,1,0:T(8,128)(2,1)}), bf16[16,8,256]{2,1,0:T(8,128)(2,1)S(1)}, u32[]{:S(2)}, u32[]{:S(2)}) %all-to-all-start.1) | async-done | bytes 65568 | tf_op jit(solution)/shard_map/all_to_all | solution.py:186
  127.5 12.2 %all-to-all-start.2 = ((bf16[16,8,4784]{2,1,0:T(8,128)(2,1)}), bf16[16,8,4784]{2,1,0:T(8,128)(2,1)S(1)}, u32[]{:S(2)}, u32[]{:S(2)}) async-start(bf16[16,8,4784]{2,1,0:T(8,128)(2,1)} %broadcast_in_dim.5), calls=%async_computation.2 | async-start | bytes 2490368 | tf_op jit(solution)/shard_map/all_to_all | solution.py:191
  147.3 2.2 collective-permute-start.16
  151.2 3.2 %collective-permute-start.19 = (bf16[336,256]{1,0:T(8,128)(2,1)}, bf16[336,256]{1,0:T(8,128)(2,1)S(1)}, u32[]{:S(2)}, u32[]{:S(2)}) collective-permute-start(bf16[336,256]{1,0:T(8,128)(2,1)} %slice.65), channel_id=1, source_target_pairs={{0,12},{4,0},{8,4},{12,8},{1,13},{5,1},{9,5},{13,9},{2,14},{6,2},{... | collective-permute-start | bytes 516104 | tf_op jit(solution)/shard_map/ppermute | solution.py:20
  157.7 3.7 %collective-permute-done.17 = bf16[352,256]{1,0:T(8,128)(2,1)S(1)} collective-permute-done((bf16[352,256]{1,0:T(8,128)(2,1)}, bf16[352,256]{1,0:T(8,128)(2,1)S(1)}, u32[]{:S(2)}, u32[]{:S(2)}) %collective-permute-start.17) | collective-permute-done | bytes 180256 | tf_op jit(solution)/shard_map/ppermute | solution.py:20
  163.6 3.8 %shard_map.83 = bf16[256,256]{1,0:T(8,128)(2,1)S(1)} custom-call(s32[16]{0:T(128)S(1)} %get-tuple-element.5.order, bf16[16,256,256]{2,1,0:T(8,128)(2,1)S(1)} %bitcast.91, bf16[16,256,256]{2,1,0:T(8,128)(2,1)S(1)} %bitcast.92), custom_call_target="tpu_custom_call" | custom-call | tf_op jit(solution)/shard_map/pallas_call | solution.py:50
  168.1 3.7 %collective-permute-start.32 = (bf16[256,256]{1,0:T(8,128)(2,1)S(1)}, bf16[256,256]{1,0:T(8,128)(2,1)S(1)}, u32[]{:S(2)}, u32[]{:S(2)}) collective-permute-start(bf16[256,256]{1,0:T(8,128)(2,1)S(1)} %shard_map.83), channel_id=1, source_target_pairs={{0,2},{1,3},{2,0},{3,1},{4,6},{5,7},{6,4},{7,5},{8,10},{9,11},{10,... | collective-permute-start | bytes 393224 | tf_op jit(solution)/shard_map/ppermute | solution.py:20
  172.6 7.3 %collective-permute-done.33 = bf16[256,256]{1,0:T(8,128)(2,1)S(1)} collective-permute-done((bf16[256,256]{1,0:T(8,128)(2,1)S(1)}, bf16[256,256]{1,0:T(8,128)(2,1)S(1)}, u32[]{:S(2)}, u32[]{:S(2)}) %collective-permute-start.33) | collective-permute-done | bytes 131104 | tf_op jit(solution)/shard_map/ppermute | solution.py:20
  186.1 9.6 %collective-permute-done.36 = bf16[4,256,256]{2,1,0:T(8,128)(2,1)S(1)} collective-permute-done((bf16[4,256,256]{2,1,0:T(8,128)(2,1)S(1)}, bf16[4,256,256]{2,1,0:T(8,128)(2,1)S(1)}, u32[]{:S(2)}, u32[]{:S(2)}) %collective-permute-start.36) | collective-permute-done | bytes 524320 | tf_op jit(solution)/shard_map/ppermute | solution.py:20
  197.2 7.8 %collective-permute-done.34 = bf16[4,256,256]{2,1,0:T(8,128)(2,1)S(1)} collective-permute-done((bf16[4,256,256]{2,1,0:T(8,128)(2,1)S(1)}, bf16[4,256,256]{2,1,0:T(8,128)(2,1)S(1)}, u32[]{:S(2)}, u32[]{:S(2)}) %collective-permute-start.34) | collective-permute-done | bytes 524320 | tf_op jit(solution)/shard_map/ppermute | solution.py:20
  211.8 5.8 %copy-done.2 = bf16[11008,688]{1,0:T(8,128)(2,1)S(1)} copy-done((bf16[11008,688]{1,0:T(8,128)(2,1)S(1)}, bf16[11008,688]{1,0:T(8,128)(2,1)}, u32[]{:S(2)}) %copy-start.2) | copy-done | bytes 15147032
  217.6 13.6 %shard_map.82.out_t = bf16[688,256]{1,0:T(8,128)(2,1)S(1)} custom-call(s32[16]{0:T(128)S(1)} %get-tuple-element.6.order, s32[1]{0:T(128)S(6)} %copy.36.live, bf16[16,688,256]{2,1,0:T(8,128)(2,1)} %bitcast_dynamic-update-slice_fusion.1.lhs, bf16[16,688,688]{2,1,0:T(8,128)(2,1)S(1)} %bitcast.88), custom_call_target="tpu_custom_call" | custom-call | tf_op jit(solution)/shard_map/pallas_call | solution.py:86
  231.2 4.2 %copy-done.3 = f32[4096,688]{0,1:T(8,128)S(1)} copy-done((f32[4096,688]{0,1:T(8,128)S(1)}, f32[4096,688]{0,1:T(8,128)}, u32[]{:S(2)}) %copy-start.3) | copy-done | bytes 11272216
  235.5 9.5 %shard_map.84 = f32[128,256]{1,0:T(8,128)S(1)} custom-call(s32[16]{0:T(128)S(1)} %get-tuple-element.6.order, bf16[688,256]{1,0:T(8,128)(2,1)S(1)} %shard_map.82.out_t, bf16[128,688]{1,0:T(8,128)(2,1)S(1)} %slice.68.right, bf16[16,256,256]{2,1,0:T(8,128)(2,1)S(1)} %bitcast.90, f32[688,4096]{1,0:T(8,128)S(1)} %bitcast.89, bf16[16,128,256]{2,1,0:T(8,128)(2,1)S(1)} %bitcast.93), custom_call_target="tpu_custom_call" | custom-call | tf_op jit(solution)/shard_map/pallas_call | solution.py:124
  246.9 14.6 %all_to_all.20 = f32[16,1,1]{2,1,0:T(1,128)S(1)} all-to-all(f32[16,1,1]{2,1,0:T(1,128)S(1)} %copy.18), channel_id=1, replica_groups=mesh['zlo'=2,'x'=4,'core'=2,'y'=4,'zhi'=4] {'y','zhi'}, dimensions={0} | all-to-all | bytes 128 | tf_op jit(solution)/shard_map/all_to_all | solution.py:204
  (144 shorter events, 71.0 us)
Async XLA Ops:
  6.5 205.2 %all-gather.3.cloned.1.call-start = ((), (), s32[]{:S(2)}) async-start(), calls=%async_computation.4 | async-start | bytes 17965056 | tf_op jit(solution)/shard_map/all_gather | solution.py:155
  7.3 51.0 %collective-permute-start = (bf16[688,256]{1,0:T(8,128)(2,1)}, bf16[688,256]{1,0:T(8,128)(2,1)S(1)}, u32[]{:S(2)}, u32[]{:S(2)}) collective-permute-start(bf16[688,256]{1,0:T(8,128)(2,1)} %bitcast.106), channel_id=1, source_target_pairs={{0,1},{1,2},{2,3},{3,0},{4,5},{5,6},{6,7},{7,4},{8,9},{9,10},{10,1... | collective-permute-start | bytes 1056776 | tf_op jit(solution)/shard_map/ppermute | solution.py:20
  10.6 50.4 %collective-permute-start.2 = (bf16[688,256]{1,0:T(8,128)(2,1)}, bf16[688,256]{1,0:T(8,128)(2,1)}, u32[]{:S(2)}, u32[]{:S(2)}) collective-permute-start(bf16[688,256]{1,0:T(8,128)(2,1)} %bitcast.107), channel_id=1, source_target_pairs={{0,3},{1,0},{2,1},{3,2},{4,7},{5,4},{6,5},{7,6},{8,11},{9,8},{10,9... | collective-permute-start | bytes 1056776 | tf_op jit(solution)/shard_map/ppermute | solution.py:20
  13.7 26.3 %collective-permute-start.22 = (bf16[256,256]{1,0:T(8,128)(2,1)}, bf16[256,256]{1,0:T(8,128)(2,1)S(1)}, u32[]{:S(2)}, u32[]{:S(2)}) collective-permute-start(bf16[256,256]{1,0:T(8,128)(2,1)} %param.8), channel_id=1, source_target_pairs={{0,3},{1,0},{2,1},{3,2},{4,7},{5,4},{6,5},{7,6},{8,11},{9,8},{10,9... | collective-permute-start | bytes 393224 | tf_op jit(solution)/shard_map/ppermute | solution.py:20
  16.6 24.0 %collective-permute-start.21 = (bf16[256,256]{1,0:T(8,128)(2,1)}, bf16[256,256]{1,0:T(8,128)(2,1)S(1)}, u32[]{:S(2)}, u32[]{:S(2)}) collective-permute-start(bf16[256,256]{1,0:T(8,128)(2,1)} %param.8), channel_id=1, source_target_pairs={{0,2},{1,3},{2,0},{3,1},{4,6},{5,7},{6,4},{7,5},{8,10},{9,11},{10,... | collective-permute-start | bytes 393224 | tf_op jit(solution)/shard_map/ppermute | solution.py:20
  18.7 22.5 %collective-permute-start.20 = (bf16[256,256]{1,0:T(8,128)(2,1)}, bf16[256,256]{1,0:T(8,128)(2,1)S(1)}, u32[]{:S(2)}, u32[]{:S(2)}) collective-permute-start(bf16[256,256]{1,0:T(8,128)(2,1)} %param.8), channel_id=1, source_target_pairs={{0,1},{1,2},{2,3},{3,0},{4,5},{5,6},{6,7},{7,4},{8,9},{9,10},{10,1... | collective-permute-start | bytes 393224 | tf_op jit(solution)/shard_map/ppermute | solution.py:20
  25.6 80.6 %all-to-all-start = ((f32[16,8,944]{2,1,0:T(8,128)}), f32[16,8,944]{2,1,0:T(8,128)S(1)}, u32[]{:S(2)}, u32[]{:S(2)}) async-start(f32[16,8,944]{2,1,0:T(8,128)} %bitcast.18), calls=%async_computation | async-start | bytes 1048576 | tf_op jit(solution)/shard_map/all_to_all | solution.py:184
  41.2 13.9 %collective-permute-start.26 = (bf16[256,256]{1,0:T(8,128)(2,1)S(1)}, bf16[256,256]{1,0:T(8,128)(2,1)S(1)}, u32[]{:S(2)}, u32[]{:S(2)}) collective-permute-start(bf16[256,256]{1,0:T(8,128)(2,1)S(1)} %copy-done.14), channel_id=1, source_target_pairs={{0,32},{32,64},{64,96},{96,0},{1,33},{33,65},{65,97},{97,1},{2,34}... | collective-permute-start | bytes 393224 | tf_op jit(solution)/shard_map/ppermute | solution.py:20
  50.0 16.6 %collective-permute-start.4 = (bf16[688,256]{1,0:T(8,128)(2,1)S(1)}, bf16[688,256]{1,0:T(8,128)(2,1)S(1)}, u32[]{:S(2)}, u32[]{:S(2)}) collective-permute-start(bf16[688,256]{1,0:T(8,128)(2,1)S(1)} %bitcast.108), channel_id=1, source_target_pairs={{0,4},{4,8},{8,12},{12,0},{1,5},{5,9},{9,13},{13,1},{2,6},{6,10},{... | collective-permute-start | bytes 1056776 | tf_op jit(solution)/shard_map/ppermute | solution.py:20
  51.5 13.9 %collective-permute-start.9 = (bf16[688,256]{1,0:T(8,128)(2,1)S(1)}, bf16[688,256]{1,0:T(8,128)(2,1)S(1)}, u32[]{:S(2)}, u32[]{:S(2)}) collective-permute-start(bf16[688,256]{1,0:T(8,128)(2,1)S(1)} %bitcast.109), channel_id=1, source_target_pairs={{0,12},{4,0},{8,4},{12,8},{1,13},{5,1},{9,5},{13,9},{2,14},{6,2},{... | collective-permute-start | bytes 1056776 | tf_op jit(solution)/shard_map/ppermute | solution.py:20
  55.1 29.8 %collective-permute-start.25 = (bf16[4,256,256]{2,1,0:T(8,128)(2,1)S(1)}, bf16[4,256,256]{2,1,0:T(8,128)(2,1)S(1)}, u32[]{:S(2)}, u32[]{:S(2)}) collective-permute-start(bf16[4,256,256]{2,1,0:T(8,128)(2,1)S(1)} %get-tuple-element.14), channel_id=1, source_target_pairs={{0,12},{4,0},{8,4},{12,8},{1,13},{5,1},{9,5},{13,9},{2,14},{6,2},{... | collective-permute-start | bytes 1572872 | tf_op jit(solution)/shard_map/ppermute | solution.py:20
  62.0 18.7 %collective-permute-start.3 = (bf16[336,256]{1,0:T(8,128)(2,1)S(1)}, bf16[336,256]{1,0:T(8,128)(2,1)S(1)}, u32[]{:S(2)}, u32[]{:S(2)}) collective-permute-start(bf16[336,256]{1,0:T(8,128)(2,1)S(1)} %slice.57), channel_id=1, source_target_pairs={{0,3},{1,0},{2,1},{3,2},{4,7},{5,4},{6,5},{7,6},{8,11},{9,8},{10,9... | collective-permute-start | bytes 516104 | tf_op jit(solution)/shard_map/ppermute | solution.py:20
  65.4 20.0 %collective-permute-start.24 = (bf16[4,256,256]{2,1,0:T(8,128)(2,1)S(1)}, bf16[4,256,256]{2,1,0:T(8,128)(2,1)S(1)}, u32[]{:S(2)}, u32[]{:S(2)}) collective-permute-start(bf16[4,256,256]{2,1,0:T(8,128)(2,1)S(1)} %get-tuple-element.14), channel_id=1, source_target_pairs={{0,8},{4,12},{8,0},{12,4},{1,9},{5,13},{9,1},{13,5},{2,10},{6,14},... | collective-permute-start | bytes 1572872 | tf_op jit(solution)/shard_map/ppermute | solution.py:20
  66.6 25.8 %collective-permute-start.23 = (bf16[4,256,256]{2,1,0:T(8,128)(2,1)S(1)}, bf16[4,256,256]{2,1,0:T(8,128)(2,1)S(1)}, u32[]{:S(2)}, u32[]{:S(2)}) collective-permute-start(bf16[4,256,256]{2,1,0:T(8,128)(2,1)S(1)} %get-tuple-element.14), channel_id=1, source_target_pairs={{0,4},{4,8},{8,12},{12,0},{1,5},{5,9},{9,13},{13,1},{2,6},{6,10},{... | collective-permute-start | bytes 1572872 | tf_op jit(solution)/shard_map/ppermute | solution.py:20
  68.3 19.9 %collective-permute-start.29 = (bf16[4,256,256]{2,1,0:T(8,128)(2,1)S(1)}, bf16[4,256,256]{2,1,0:T(8,128)(2,1)S(1)}, u32[]{:S(2)}, u32[]{:S(2)}) collective-permute-start(bf16[4,256,256]{2,1,0:T(8,128)(2,1)S(1)} %get-tuple-element.12), channel_id=1, source_target_pairs={{0,128},{128,0},{1,129},{129,1},{2,130},{130,2},{3,131},{131,3},{4... | collective-permute-start | bytes 1572872 | tf_op jit(solution)/shard_map/ppermute | solution.py:20
  80.7 17.4 %collective-permute-start.5 = (bf16[688,256]{1,0:T(8,128)(2,1)S(1)}, bf16[688,256]{1,0:T(8,128)(2,1)S(1)}, u32[]{:S(2)}, u32[]{:S(2)}) collective-permute-start(bf16[688,256]{1,0:T(8,128)(2,1)S(1)} %collective-permute-done), channel_id=1, source_target_pairs={{0,4},{4,8},{8,12},{12,0},{1,5},{5,9},{9,13},{13,1},{2,6},{6,10},{... | collective-permute-start | bytes 1056776 | tf_op jit(solution)/shard_map/ppermute | solution.py:20
  84.8 20.0 %collective-permute-start.7 = (bf16[688,256]{1,0:T(8,128)(2,1)}, bf16[688,256]{1,0:T(8,128)(2,1)S(1)}, u32[]{:S(2)}, u32[]{:S(2)}) collective-permute-start(bf16[688,256]{1,0:T(8,128)(2,1)} %collective-permute-done.2), channel_id=1, source_target_pairs={{0,4},{4,8},{8,12},{12,0},{1,5},{5,9},{9,13},{13,1},{2,6},{6,10},{... | collective-permute-start | bytes 1056776 | tf_op jit(solution)/shard_map/ppermute | solution.py:20
  88.2 12.1 %collective-permute-start.18 = (bf16[688,256]{1,0:T(8,128)(2,1)}, bf16[688,256]{1,0:T(8,128)(2,1)S(1)}, u32[]{:S(2)}, u32[]{:S(2)}) collective-permute-start(bf16[688,256]{1,0:T(8,128)(2,1)} %collective-permute-done.2), channel_id=1, source_target_pairs={{0,12},{4,0},{8,4},{12,8},{1,13},{5,1},{9,5},{13,9},{2,14},{6,2},{... | collective-permute-start | bytes 1056776 | tf_op jit(solution)/shard_map/ppermute | solution.py:20
  92.4 54.8 %collective-permute-start.10 = (bf16[336,256]{1,0:T(8,128)(2,1)}, bf16[336,256]{1,0:T(8,128)(2,1)}, u32[]{:S(2)}, u32[]{:S(2)}) collective-permute-start(bf16[336,256]{1,0:T(8,128)(2,1)} %slice.59), channel_id=1, source_target_pairs={{0,12},{4,0},{8,4},{12,8},{1,13},{5,1},{9,5},{13,9},{2,14},{6,2},{... | collective-permute-start | bytes 516104 | tf_op jit(solution)/shard_map/ppermute | solution.py:20
  95.0 54.4 %collective-permute-start.8 = (bf16[352,256]{1,0:T(8,128)(2,1)}, bf16[352,256]{1,0:T(8,128)(2,1)}, u32[]{:S(2)}, u32[]{:S(2)}) collective-permute-start(bf16[352,256]{1,0:T(8,128)(2,1)} %slice.58), channel_id=1, source_target_pairs={{0,4},{4,8},{8,12},{12,0},{1,5},{5,9},{9,13},{13,1},{2,6},{6,10},{... | collective-permute-start | bytes 540680 | tf_op jit(solution)/shard_map/ppermute | solution.py:20
  98.0 41.7 %collective-permute-start.6 = (bf16[688,256]{1,0:T(8,128)(2,1)}, bf16[688,256]{1,0:T(8,128)(2,1)}, u32[]{:S(2)}, u32[]{:S(2)}) collective-permute-start(bf16[688,256]{1,0:T(8,128)(2,1)} %constant_dynamic-update-slice_fusion), channel_id=1, source_target_pairs={{0,4},{4,8},{8,12},{12,0},{1,5},{5,9},{9,13},{13,1},{2,6},{6,10},{... | collective-permute-start | bytes 1056776 | tf_op jit(solution)/shard_map/ppermute | solution.py:20
  100.3 42.1 %collective-permute-start.15 = (bf16[688,256]{1,0:T(8,128)(2,1)}, bf16[688,256]{1,0:T(8,128)(2,1)}, u32[]{:S(2)}, u32[]{:S(2)}) collective-permute-start(bf16[688,256]{1,0:T(8,128)(2,1)} %constant_dynamic-update-slice_fusion), channel_id=1, source_target_pairs={{0,12},{4,0},{8,4},{12,8},{1,13},{5,1},{9,5},{13,9},{2,14},{6,2},{... | collective-permute-start | bytes 1056776 | tf_op jit(solution)/shard_map/ppermute | solution.py:20
  104.8 57.3 %collective-permute-start.30 = (bf16[2,4,256,256]{3,2,1,0:T(8,128)(2,1)}, bf16[2,4,256,256]{3,2,1,0:T(8,128)(2,1)}, u32[]{:S(2)}, u32[]{:S(2)}) collective-permute-start(bf16[2,4,256,256]{3,2,1,0:T(8,128)(2,1)} %get-tuple-element.8), channel_id=1, source_target_pairs={{0,16},{16,0},{1,17},{17,1},{2,18},{18,2},{3,19},{19,3},{4,20},{20... | collective-permute-start | bytes 3145736 | tf_op jit(solution)/shard_map/ppermute | solution.py:20
  107.0 19.3 %all-to-all-start.1 = ((bf16[16,8,256]{2,1,0:T(8,128)(2,1)}), bf16[16,8,256]{2,1,0:T(8,128)(2,1)S(1)}, u32[]{:S(2)}, u32[]{:S(2)}) async-start(bf16[16,8,256]{2,1,0:T(8,128)(2,1)} %broadcast_in_dim.4), calls=%async_computation.1 | async-start | bytes 131072 | tf_op jit(solution)/shard_map/all_to_all | solution.py:186
  127.5 77.8 %all-to-all-start.2 = ((bf16[16,8,4784]{2,1,0:T(8,128)(2,1)}), bf16[16,8,4784]{2,1,0:T(8,128)(2,1)S(1)}, u32[]{:S(2)}, u32[]{:S(2)}) async-start(bf16[16,8,4784]{2,1,0:T(8,128)(2,1)} %broadcast_in_dim.5), calls=%async_computation.2 | async-start | bytes 2490368 | tf_op jit(solution)/shard_map/all_to_all | solution.py:191
  139.8 11.4 %collective-permute-start.13 = (bf16[336,256]{1,0:T(8,128)(2,1)}, bf16[336,256]{1,0:T(8,128)(2,1)S(1)}, u32[]{:S(2)}, u32[]{:S(2)}) collective-permute-start(bf16[336,256]{1,0:T(8,128)(2,1)} %slice.61), channel_id=1, source_target_pairs={{0,12},{4,0},{8,4},{12,8},{1,13},{5,1},{9,5},{13,9},{2,14},{6,2},{... | collective-permute-start | bytes 516104 | tf_op jit(solution)/shard_map/ppermute | solution.py:20
  142.4 12.0 %collective-permute-start.11 = (bf16[352,256]{1,0:T(8,128)(2,1)}, bf16[352,256]{1,0:T(8,128)(2,1)S(1)}, u32[]{:S(2)}, u32[]{:S(2)}) collective-permute-start(bf16[352,256]{1,0:T(8,128)(2,1)} %slice.60), channel_id=1, source_target_pairs={{0,4},{4,8},{8,12},{12,0},{1,5},{5,9},{9,13},{13,1},{2,6},{6,10},{... | collective-permute-start | bytes 540680 | tf_op jit(solution)/shard_map/ppermute | solution.py:20
  167.4 12.5 %collective-permute-start.33 = (bf16[256,256]{1,0:T(8,128)(2,1)S(1)}, bf16[256,256]{1,0:T(8,128)(2,1)S(1)}, u32[]{:S(2)}, u32[]{:S(2)}) collective-permute-start(bf16[256,256]{1,0:T(8,128)(2,1)S(1)} %shard_map.83), channel_id=1, source_target_pairs={{0,3},{1,0},{2,1},{3,2},{4,7},{5,4},{6,5},{7,6},{8,11},{9,8},{10,9... | collective-permute-start | bytes 393224 | tf_op jit(solution)/shard_map/ppermute | solution.py:20
  168.1 11.8 %collective-permute-start.32 = (bf16[256,256]{1,0:T(8,128)(2,1)S(1)}, bf16[256,256]{1,0:T(8,128)(2,1)S(1)}, u32[]{:S(2)}, u32[]{:S(2)}) collective-permute-start(bf16[256,256]{1,0:T(8,128)(2,1)S(1)} %shard_map.83), channel_id=1, source_target_pairs={{0,2},{1,3},{2,0},{3,1},{4,6},{5,7},{6,4},{7,5},{8,10},{9,11},{10,... | collective-permute-start | bytes 393224 | tf_op jit(solution)/shard_map/ppermute | solution.py:20
  180.7 14.9 %collective-permute-start.36 = (bf16[4,256,256]{2,1,0:T(8,128)(2,1)S(1)}, bf16[4,256,256]{2,1,0:T(8,128)(2,1)S(1)}, u32[]{:S(2)}, u32[]{:S(2)}) collective-permute-start(bf16[4,256,256]{2,1,0:T(8,128)(2,1)S(1)} %get-tuple-element.10), channel_id=1, source_target_pairs={{0,12},{4,0},{8,4},{12,8},{1,13},{5,1},{9,5},{13,9},{2,14},{6,2},{... | collective-permute-start | bytes 1572872 | tf_op jit(solution)/shard_map/ppermute | solution.py:20
  180.9 16.4 %collective-permute-start.35 = (bf16[4,256,256]{2,1,0:T(8,128)(2,1)S(1)}, bf16[4,256,256]{2,1,0:T(8,128)(2,1)S(1)}, u32[]{:S(2)}, u32[]{:S(2)}) collective-permute-start(bf16[4,256,256]{2,1,0:T(8,128)(2,1)S(1)} %get-tuple-element.10), channel_id=1, source_target_pairs={{0,8},{4,12},{8,0},{12,4},{1,9},{5,13},{9,1},{13,5},{2,10},{6,14},... | collective-permute-start | bytes 1572872 | tf_op jit(solution)/shard_map/ppermute | solution.py:20
  181.9 23.2 %collective-permute-start.34 = (bf16[4,256,256]{2,1,0:T(8,128)(2,1)S(1)}, bf16[4,256,256]{2,1,0:T(8,128)(2,1)S(1)}, u32[]{:S(2)}, u32[]{:S(2)}) collective-permute-start(bf16[4,256,256]{2,1,0:T(8,128)(2,1)S(1)} %get-tuple-element.10), channel_id=1, source_target_pairs={{0,4},{4,8},{8,12},{12,0},{1,5},{5,9},{9,13},{13,1},{2,6},{6,10},{... | collective-permute-start | bytes 1572872 | tf_op jit(solution)/shard_map/ppermute | solution.py:20
  (26 other events, 375.2 us)
Sparse Core Ops, SparseCore 0:
  9.2 133.1 all-gather.2

commit v2 on v1

v2 whole, which is shorter than its diff:
```python
import functools

import jax
import jax.numpy as jnp
from jax import lax
from jax.experimental import pallas as pl
from jax.experimental.pallas import tpu as pltpu
from jax.sharding import Mesh, PartitionSpec as P

SEQ_LEN = 256
RANK = 8
damping = 0.01
AXES = ("zlo", "x", "core", "y", "zhi")
SIZES = (2, 4, 2, 4, 4)
TRAIN = ("zlo", "x", "core")
FEAT = ("y", "zhi")
PART = SEQ_LEN // 4
HALF_SCALE = 128.0
over_rows = (((0,), (0,)), ((), ()))


def shift(block, axis, step):
    size = SIZES[AXES.index(axis)]
    return lax.ppermute(block, axis, [(i, (i + step) % size) for i in range(size)])


def ring(block, axis):
    one, three = shift(block, axis, 1), shift(block, axis, -1)
    two = jnp.concatenate([shift(one[:2], axis, 1), shift(three[2:], axis, -1)], axis=0)
    return jnp.stack([block, one, two, three])


def direct(block, axis):
    return jnp.stack([block] + [shift(block, axis, step) for step in (1, 2, 3)])


def to_basis_rows(parts):
    x = lax.axis_index("x")
    got = []
    for k in range(4):
        pairs = []
        for zlo in range(2):
            for sx in range(4):
                for core in range(2):
                    for y in range(4):
                        for zhi in range(4):
                            source = (((zlo * 4 + sx) * 2 + core) * 4 + y) * 4 + zhi
                            dest_x = 2 * (y % 2) + zhi // 2
                            dest = (((y // 2) * 4 + dest_x) * 2 + core) * 4 + (sx + k) % 4
                            pairs.append((source, dest * 4 + 2 * zlo + zhi % 2))
        piece = lax.dynamic_index_in_dim(parts, lax.rem(x + k, 4), 0, keepdims=False)
        got.append(lax.ppermute(piece, AXES, pairs))
    return jnp.stack(got)


def partial_kernel(scale, place, lhs0, lhs1, rhs0, rhs1, out):
    rows = 4 * PART
    depth = lhs0.shape[3]
    result = jnp.dot(lhs0[0].reshape(rows, depth), rhs0[0, 0], preferred_element_type=jnp.float32)
    result += jnp.dot(lhs1[0].reshape(rows, depth), rhs1[0, 0], preferred_element_type=jnp.float32)
    result = (result * scale).astype(out.dtype)
    for k in range(4):
        out[place[4 + k], 0] = result[k * PART : (k + 1) * PART]


def partial_rotation(place, lhs, rhs, out_type, scale):
    depth, cols = rhs.shape[2:]
    return pl.pallas_call(
        functools.partial(partial_kernel, scale),
        grid_spec=pltpu.PrefetchScalarGridSpec(
            num_scalar_prefetch=1,
            grid=(4, 2),
            in_specs=[
                pl.BlockSpec((1, 4, PART, depth), lambda y, z, place: (place[2 * z], 0, 0, 0)),
                pl.BlockSpec((1, 4, PART, depth), lambda y, z, place: (place[2 * z + 1], 0, 0, 0)),
                pl.BlockSpec((1, 1, depth, cols), lambda y, z, place: (0, y, 0, 0)),
                pl.BlockSpec((1, 1, depth, cols), lambda y, z, place: (1, y, 0, 0)),
            ],
            out_specs=pl.BlockSpec((4, 1, PART, cols), lambda y, z, place: (z, y, 0, 0)),
        ),
        out_shape=jax.ShapeDtypeStruct((8, 4, PART, cols), out_type),
        compiler_params=pltpu.CompilerParams(vmem_limit_bytes=40 << 20),
    )(place, lhs, lhs, rhs, rhs)


def score_kernel(place, live, out_ref, right, rows, eig, left, total, acc, out_t):
    step = pl.program_id(0)
    slab = out_ref.shape[2]
    seq, width = 4 * PART, rows.shape[4]

    @pl.when(step == 0)
    def _():
        acc[...] = jnp.zeros_like(acc)
        row = lax.broadcasted_iota(jnp.int32, (PART, slab), 0)
        for k in range(4):
            quarter = place[4 + k]
            kept = jnp.where(row + quarter * PART < live[0], out_ref[quarter].astype(jnp.float32), 0.0)
            out_t[:, k * PART : (k + 1) * PART] = kept.T.astype(out_t.dtype)

    rotated = rows[...].reshape(seq, width)
    grad = jnp.dot(out_t[...], rotated, preferred_element_type=jnp.float32)
    scaled = (grad / (eig[...] + damping)).astype(jnp.bfloat16)
    mapped = jnp.dot(right[...], scaled, preferred_element_type=jnp.float32)
    acc[...] += mapped * left[...].reshape(acc.shape)

    @pl.when(step == pl.num_programs(0) - 1)
    def _():
        total[...] = acc[...]


def score(place, live, out, right, rows, eig_t, left):
    width = rows.shape[4]
    slab = out.shape[2]
    trains, share = left.shape[:2]
    factors = trains * share

    def slab_of(b, place):
        return (b // 4) * 4 + place[8 + b % 4]

    return pl.pallas_call(
        score_kernel,
        grid_spec=pltpu.PrefetchScalarGridSpec(
            num_scalar_prefetch=2,
            grid=(16,),
            in_specs=[
                pl.BlockSpec((4, PART, slab), lambda b, place, live: (0, 0, 0)),
                pl.BlockSpec((factors, slab), lambda b, place, live: (0, 0)),
                pl.BlockSpec((4, 1, 1, PART, width), lambda b, place, live: (0, b % 4, b // 4, 0, 0)),
                pl.BlockSpec((slab, width), lambda b, place, live: (0, slab_of(b, place))),
                pl.BlockSpec((trains, share, width), lambda b, place, live: (0, 0, slab_of(b, place))),
            ],
            out_specs=pl.BlockSpec((factors, width), lambda b, place, live: (0, 0)),
            scratch_shapes=[
                pltpu.VMEM((factors, width), jnp.float32),
                pltpu.VMEM((slab, 4 * PART), jnp.bfloat16),
            ],
        ),
        out_shape=jax.ShapeDtypeStruct((factors, width), jnp.float32),
        compiler_params=pltpu.CompilerParams(vmem_limit_bytes=40 << 20),
    )(place, live, out, right, rows, eig_t, left)


def local(
    activations, grad_outputs, in_basis, out_basis, eigenvalues, query_left, query_right, lengths
):
    y, zhi = lax.axis_index("y"), lax.axis_index("zhi")
    bf16, f32 = jnp.bfloat16, jnp.float32
    trains, feats = 16, 16
    factors = query_left.shape[1]
    slab = out_basis.shape[1]
    width = in_basis.shape[1]

    basis = lax.all_gather(out_basis, ("core", "y"), axis=0, tiled=False).reshape(2, 4, slab, slab)

    four = jnp.arange(4, dtype=jnp.int32)
    step_of_z = lax.rem(zhi - four + 4, 4)
    place = jnp.concatenate([step_of_z, lax.rem(y - four + 4, 4), step_of_z]).astype(jnp.int32)

    u_y = direct(in_basis, "y")
    u_other = shift(u_y, "core", 1)
    core = lax.axis_index("core")
    u_both = jnp.where(core == 0, jnp.stack([u_y, u_other]), jnp.stack([u_other, u_y]))
    u_all = u_both

    act_part = to_basis_rows(activations.reshape(4, PART, width))
    grad_part = to_basis_rows(grad_outputs.reshape(4, PART, slab))
    act_all = direct(act_part, "zhi")
    grad_all = ring(grad_part, "zhi")

    left_part = lax.dot_general(query_left, in_basis, over_rows, preferred_element_type=f32)
    right_part = lax.dot_general(query_right, out_basis, over_rows, preferred_element_type=f32)
    share = factors // trains
    parts = jnp.concatenate([left_part, right_part], axis=1).reshape(trains, share, slab + width)
    mine = jnp.sum(lax.all_to_all(parts, TRAIN, 0, 0), axis=0).astype(bf16)
    left_mine, right_mine = mine[:, :width], mine[:, width:]
    left_feat = lax.all_to_all(
        jnp.broadcast_to(left_mine[None], (feats, share, width)), FEAT, 0, 0
    )
    left_cols = jnp.transpose(left_feat, (1, 0, 2)).reshape(share, feats * width)
    both = jnp.concatenate([left_cols, right_mine], axis=1)
    both = lax.all_to_all(jnp.broadcast_to(both[None], (trains,) + both.shape), TRAIN, 0, 0)
    left = both[:, :, : feats * width].astype(f32)
    right = both[:, :, feats * width :].reshape(factors, slab)

    u_all = jnp.stack([lax.dynamic_index_in_dim(u_all, place[4 + k], 1, keepdims=False) for k in range(4)], axis=1)
    in_part = partial_rotation(place, act_all, u_all, f32, 1.0)
    in_sum = jnp.sum(lax.all_to_all(in_part, ("zlo", "x"), 0, 0, tiled=True), axis=0).astype(bf16)
    in_all = ring(direct(in_sum, "zhi"), "y")

    out_part = partial_rotation(place, grad_all, basis, f32, HALF_SCALE).astype(jnp.float16)
    out_got = lax.all_to_all(out_part, ("zlo", "x"), 0, 0, tiled=True)
    out_sum = (jnp.sum(out_got.astype(f32), axis=0) * (1.0 / HALF_SCALE)).astype(bf16)
    out_rot = lax.all_to_all(out_sum, "y", 0, 0, tiled=True)

    total = score(place, lengths, out_rot, right, in_all, jnp.transpose(eigenvalues), left)
    queries = factors // RANK
    partial = jnp.sum(jnp.sum(total, axis=1).reshape(queries, RANK), axis=1)
    pieces = lax.all_to_all(partial.reshape(feats, 1, 1), FEAT, 0, 0)
    return jnp.sum(pieces, axis=0)


def solution(mesh):
    fine = Mesh(mesh.devices.reshape(SIZES), AXES)
    in_specs = (
        P(TRAIN, FEAT),
        P(TRAIN, FEAT),
        P(TRAIN, FEAT),
        P(TRAIN, FEAT),
        P(None, FEAT),
        P(TRAIN, None),
        P(TRAIN, None),
        P(TRAIN),
    )
    return jax.shard_map(
        local, mesh=fine, in_specs=in_specs, out_specs=P(TRAIN, FEAT), check_vma=False
    )
```

time: 274 us -> 332 us (1.21); the launches traced: 269 us -> 331 us
  waiting for transfers between devices: 57.2 us -> 101 us
  local copies, waits for them, and re-layouts: 43.1 us -> 8.71 us
  starting transfers between devices: 100 us -> 124 us
  blocking collectives: 14.6 us -> 25.9 us
  between operations: 14.4 us -> 22 us
  other arithmetic: 9.81 us -> 15 us
  Pallas kernels: 26.9 us -> 30.8 us
    ppermute x0 -> x8, starting transfers between devices: none -> 36.1 us  [to_basis_rows(): got.append(lax.ppermute(piece, AXES, pairs))]
    ppermute x37 -> x18, starting transfers between devices: 73.4 us -> 43.9 us  [shift(): lax.ppermute(block, axis, [(i, (i + step) % size) for i in range(size)])]
    unnamed x46 -> x19, local copies, waits for them, and re-layouts: 26.5 us -> 3.4 us
    ppermute x37 -> x18, waiting for transfers between devices: 47.1 us -> 69.2 us  [shift(): lax.ppermute(block, axis, [(i, (i + step) % size) for i in range(size)])]
    all_to_all x1 -> x3, starting transfers between devices: 5.27 us -> 26.8 us  [the longest x1 16 us: local(): out_got = lax.all_to_all(out_part, ('zlo', 'x'), 0, 0, tiled=True)]
    ppermute x0 -> x8, waiting for transfers between devices: none -> 16.9 us  [to_basis_rows(): got.append(lax.ppermute(piece, AXES, pairs))]
    all_to_all x0 -> x1, blocking collectives: none -> 13.1 us  [local(): mine = jnp.sum(lax.all_to_all(parts, TRAIN, 0, 0), axis=0).astype(bf16)]
    slice x15 -> x7, local copies, waits for them, and re-layouts: 10.8 us -> 2.16 us  [the longest x2 0.75 us: ring(): one[:2]]
  transfers between devices with their start and end apart: 41 -> 32, of which waited for: 14 -> 10; matrix products, arithmetic and copies ran while one was open for 15% -> 7% of each run, Pallas kernels for 1% -> 5%
where the time goes in v2:
time: 332 us; the launch traced here: 331 us
  starting transfers between devices  124 us (37%)
  waiting for transfers between devices  101 us (30%)
  Pallas kernels  30.8 us (9%)
  blocking collectives  25.9 us (8%)
  between operations  22 us (7%)
  other arithmetic  15 us (5%)
  local copies, waits for them, and re-layouts  8.71 us (3%)
    ppermute x18, waiting for transfers between devices, shift(): lax.ppermute(block, axis, [(i, (i + step) % size) for i in range(size)])  69.2 us
    ppermute x18, starting transfers between devices, shift(): lax.ppermute(block, axis, [(i, (i + step) % size) for i in range(size)])  43.9 us
    ppermute x8, starting transfers between devices, to_basis_rows(): got.append(lax.ppermute(piece, AXES, pairs))  36.1 us
    ppermute x8, waiting for transfers between devices, to_basis_rows(): got.append(lax.ppermute(piece, AXES, pairs))  16.9 us
    all_to_all x1, starting transfers between devices, local(): out_got = lax.all_to_all(out_part, ('zlo', 'x'), 0, 0, tiled=True)  16 us
    pallas_call x2, Pallas kernels, partial_rotation(): pl.pallas_call(functools.partial(partial_kernel, scale), grid_spec=pltpu....  15.7 us
    pallas_call x1, Pallas kernels, score(): pl.pallas_call(score_kernel, grid_spec=pltpu.PrefetchScalarGridSpec(num_s...  15.1 us
    all_to_all x1, blocking collectives, local(): mine = jnp.sum(lax.all_to_all(parts, TRAIN, 0, 0), axis=0).astype(bf16)  13.1 us
  transfers between devices with their start and end apart: 32, of which 10 were waited for; matrix products, arithmetic and copies ran while one was open for 7% of the time, Pallas kernels for 5%

profile of v2, /device:TPU:4, one launch (start us, length us, event | category | flops | bytes accessed | tf_op | source)
XLA Modules:
  0.0 330.5 jit_solution(10592100432584176279)
XLA Ops:
  10.5 13.1 %all_to_all.35 = f32[16,8,944]{2,1,0:T(8,128)S(1)} all-to-all(f32[16,8,944]{2,1,0:T(8,128)S(1)} %bitcast.75), channel_id=1, replica_groups=mesh['zlo'=2,'x'=4,'core'=2,'y'=4,'zhi'=4] {'zlo','x','core'}, dimensions={0} | all-to-all | bytes 966656 | tf_op jit(solution)/shard_map/all_to_all | solution.py:174
  24.2 10.4 %all-to-all-start.3 = ((bf16[16,8,256]{2,1,0:T(8,128)(2,1)}), bf16[16,8,256]{2,1,0:T(8,128)(2,1)S(1)}, u32[]{:S(2)}, u32[]{:S(2)}) async-start(bf16[16,8,256]{2,1,0:T(8,128)(2,1)} %broadcast_in_dim.4), calls=%async_computation.3 | async-start | bytes 131072 | tf_op jit(solution)/shard_map/all_to_all | solution.py:176
  34.7 10.4 %all-to-all-done.3 = bf16[16,8,256]{2,1,0:T(8,128)(2,1)S(1)} async-done(((bf16[16,8,256]{2,1,0:T(8,128)(2,1)}), bf16[16,8,256]{2,1,0:T(8,128)(2,1)S(1)}, u32[]{:S(2)}, u32[]{:S(2)}) %all-to-all-start.3) | async-done | bytes 65568 | tf_op jit(solution)/shard_map/all_to_all | solution.py:176
  46.2 7.2 %all-to-all-start.4 = ((bf16[16,8,4784]{2,1,0:T(8,128)(2,1)}), bf16[16,8,4784]{2,1,0:T(8,128)(2,1)S(1)}, u32[]{:S(2)}, u32[]{:S(2)}) async-start(bf16[16,8,4784]{2,1,0:T(8,128)(2,1)} %broadcast_in_dim.5), calls=%async_computation.4 | async-start | bytes 2490368 | tf_op jit(solution)/shard_map/all_to_all | solution.py:181
  56.0 3.6 %collective-permute-start.11 = (bf16[64,256]{1,0:T(8,128)(2,1)S(1)}, bf16[64,256]{1,0:T(8,128)(2,1)S(1)}, u32[]{:S(2)}, u32[]{:S(2)}) collective-permute-start(bf16[64,256]{1,0:T(8,128)(2,1)S(1)} %get-tuple-element.22), channel_id=1, source_target_pairs={{0,12},{1,13},{2,44},{3,45},{4,76},{5,77},{6,108},{7,109},{8,140},... | collective-permute-start | bytes 98312 | tf_op jit(solution)/shard_map/ppermute | solution.py:52
  62.6 5.6 %collective-permute-start.9 = (bf16[64,256]{1,0:T(8,128)(2,1)S(1)}, bf16[64,256]{1,0:T(8,128)(2,1)S(1)}, u32[]{:S(2)}, u32[]{:S(2)}) collective-permute-start(bf16[64,256]{1,0:T(8,128)(2,1)S(1)} %get-tuple-element.24), channel_id=1, source_target_pairs={{0,4},{1,5},{2,36},{3,37},{4,68},{5,69},{6,100},{7,101},{8,132},{9... | collective-permute-start | bytes 98312 | tf_op jit(solution)/shard_map/ppermute | solution.py:52
  68.2 7.0 %collective-permute-start.8 = (bf16[64,256]{1,0:T(8,128)(2,1)S(1)}, bf16[64,256]{1,0:T(8,128)(2,1)S(1)}, u32[]{:S(2)}, u32[]{:S(2)}) collective-permute-start(bf16[64,256]{1,0:T(8,128)(2,1)S(1)} %get-tuple-element.21), channel_id=1, source_target_pairs={{0,0},{1,1},{2,32},{3,33},{4,64},{5,65},{6,96},{7,97},{8,128},{9,1... | collective-permute-start | bytes 98312 | tf_op jit(solution)/shard_map/ppermute | solution.py:52
  76.8 8.5 %collective-permute-start.14 = (bf16[4,64,256]{2,1,0:T(8,128)(2,1)S(1)}, bf16[4,64,256]{2,1,0:T(8,128)(2,1)S(1)}, u32[]{:S(2)}, u32[]{:S(2)}) collective-permute-start(bf16[4,64,256]{2,1,0:T(8,128)(2,1)S(1)} %get-tuple-element.20), channel_id=1, source_target_pairs={{0,3},{1,0},{2,1},{3,2},{4,7},{5,4},{6,5},{7,6},{8,11},{9,8},{10,9... | collective-permute-start | bytes 393224 | tf_op jit(solution)/shard_map/ppermute | solution.py:24
  85.3 2.6 collective-permute-start.12
  97.6 4.6 %shard_map.83 = f32[8,4,64,256]{3,2,1,0:T(8,128)} custom-call(s32[12]{0:T(128)S(1)} %pad_add_fusion.place, bf16[4,4,64,256]{3,2,1,0:T(8,128)(2,1)S(1)} %pad_maximum_fusion.3.lhs0.lhs1, bf16[4,4,64,256]{3,2,1,0:T(8,128)(2,1)S(1)} %pad_maximum_fusion.3.lhs0.lhs1, bf16[2,4,256,256]{3,2,1,0:T(8,128)(2,1)S(1)} %pad_maximum_fusion.2.rhs0.rhs1, ...), custom_call_target="tpu_custom_call" | custom-call | tf_op jit(solution)/shard_map/pallas_call | solution.py:68
  102.2 7.4 %all-to-all-start.5 = ((f32[8,4,64,256]{3,2,1,0:T(8,128)}), f32[8,4,64,256]{3,2,1,0:T(8,128)}, u32[]{:S(2)}, u32[]{:S(2)}) async-start(f32[8,4,64,256]{3,2,1,0:T(8,128)} %shard_map.83), calls=%async_computation.5 | async-start | bytes 4194304 | tf_op jit(solution)/shard_map/all_to_all | solution.py:187
  111.7 4.0 %collective-permute-start.2 = (bf16[64,688]{1,0:T(8,128)(2,1)S(1)}, bf16[64,688]{1,0:T(8,128)(2,1)S(1)}, u32[]{:S(2)}, u32[]{:S(2)}) collective-permute-start(bf16[64,688]{1,0:T(8,128)(2,1)S(1)} %get-tuple-element.17), channel_id=1, source_target_pairs={{0,8},{1,9},{2,40},{3,41},{4,72},{5,73},{6,104},{7,105},{8,136},{9... | collective-permute-start | bytes 264200 | tf_op jit(solution)/shard_map/ppermute | solution.py:52
  115.7 7.5 %collective-permute-start.1 = (bf16[64,688]{1,0:T(8,128)(2,1)S(1)}, bf16[64,688]{1,0:T(8,128)(2,1)S(1)}, u32[]{:S(2)}, u32[]{:S(2)}) collective-permute-start(bf16[64,688]{1,0:T(8,128)(2,1)S(1)} %get-tuple-element.18), channel_id=1, source_target_pairs={{0,4},{1,5},{2,36},{3,37},{4,68},{5,69},{6,100},{7,101},{8,132},{9... | collective-permute-start | bytes 264200 | tf_op jit(solution)/shard_map/ppermute | solution.py:52
  123.2 4.6 %collective-permute-start = (bf16[64,688]{1,0:T(8,128)(2,1)S(1)}, bf16[64,688]{1,0:T(8,128)(2,1)S(1)}, u32[]{:S(2)}, u32[]{:S(2)}) collective-permute-start(bf16[64,688]{1,0:T(8,128)(2,1)S(1)} %get-tuple-element.15), channel_id=1, source_target_pairs={{0,0},{1,1},{2,32},{3,33},{4,64},{5,65},{6,96},{7,97},{8,128},{9,1... | collective-permute-start | bytes 264200 | tf_op jit(solution)/shard_map/ppermute | solution.py:52
  127.9 15.6 %collective-permute-done.3 = bf16[64,688]{1,0:T(8,128)(2,1)S(1)} collective-permute-done((bf16[64,688]{1,0:T(8,128)(2,1)S(1)}, bf16[64,688]{1,0:T(8,128)(2,1)S(1)}, u32[]{:S(2)}, u32[]{:S(2)}) %collective-permute-start.3) | collective-permute-done | bytes 88096 | tf_op jit(solution)/shard_map/ppermute | solution.py:52
  143.5 13.1 %collective-permute-start.6 = (bf16[4,64,688]{2,1,0:T(8,128)(2,1)S(1)}, bf16[4,64,688]{2,1,0:T(8,128)(2,1)S(1)}, u32[]{:S(2)}, u32[]{:S(2)}) collective-permute-start(bf16[4,64,688]{2,1,0:T(8,128)(2,1)S(1)} %get-tuple-element.14), channel_id=1, source_target_pairs={{0,3},{1,0},{2,1},{3,2},{4,7},{5,4},{6,5},{7,6},{8,11},{9,8},{10,9... | collective-permute-start | bytes 1056776 | tf_op jit(solution)/shard_map/ppermute | solution.py:24
  156.6 7.3 %collective-permute-done.6 = bf16[4,64,688]{2,1,0:T(8,128)(2,1)S(1)} collective-permute-done((bf16[4,64,688]{2,1,0:T(8,128)(2,1)S(1)}, bf16[4,64,688]{2,1,0:T(8,128)(2,1)S(1)}, u32[]{:S(2)}, u32[]{:S(2)}) %collective-permute-start.6) | collective-permute-done | bytes 352288 | tf_op jit(solution)/shard_map/ppermute | solution.py:24
  163.9 4.9 %collective-permute-start.7 = (bf16[2,64,688]{2,1,0:T(8,128)(2,1)S(1)}, bf16[2,64,688]{2,1,0:T(8,128)(2,1)S(1)}, u32[]{:S(2)}, u32[]{:S(2)}) collective-permute-start(bf16[2,64,688]{2,1,0:T(8,128)(2,1)S(1)} %slice.49), channel_id=1, source_target_pairs={{0,3},{1,0},{2,1},{3,2},{4,7},{5,4},{6,5},{7,6},{8,11},{9,8},{10,9... | collective-permute-start | bytes 528392 | tf_op jit(solution)/shard_map/ppermute | solution.py:24
  169.0 11.5 %collective-permute-done.7 = bf16[2,64,688]{2,1,0:T(8,128)(2,1)S(1)} collective-permute-done((bf16[2,64,688]{2,1,0:T(8,128)(2,1)S(1)}, bf16[2,64,688]{2,1,0:T(8,128)(2,1)S(1)}, u32[]{:S(2)}, u32[]{:S(2)}) %collective-permute-start.7) | collective-permute-done | bytes 176160 | tf_op jit(solution)/shard_map/ppermute | solution.py:24
  180.5 4.0 %collective-permute-done.5 = bf16[2,64,688]{2,1,0:T(8,128)(2,1)S(1)} collective-permute-done((bf16[2,64,688]{2,1,0:T(8,128)(2,1)S(1)}, bf16[2,64,688]{2,1,0:T(8,128)(2,1)S(1)}, u32[]{:S(2)}, u32[]{:S(2)}) %collective-permute-start.5) | collective-permute-done | bytes 176160 | tf_op jit(solution)/shard_map/ppermute | solution.py:24
  184.8 11.2 %shard_map.82 = f32[8,4,64,688]{3,2,1,0:T(8,128)S(1)} custom-call(s32[12]{0:T(128)S(1)} %pad_add_fusion.place, bf16[4,4,64,688]{3,2,1,0:T(8,128)(2,1)S(1)} %pad_maximum_fusion.1.lhs0.lhs1, bf16[4,4,64,688]{3,2,1,0:T(8,128)(2,1)S(1)} %pad_maximum_fusion.1.lhs0.lhs1, bf16[2,4,688,688]{3,2,1,0:T(8,128)(2,1)} %bitcast.72, bf16[2,4,688,688]{3,2,1,0:T(8,128)(2,1)} %bitcast.73), custom_call_target="tpu_custom_call" | custom-call | tf_op jit(solution)/shard_map/pallas_call | solution.py:68
  198.2 16.0 %all-to-all-start = ((f16[8,4,64,688]{3,2,1,0:T(8,128)(2,1)}), f16[8,4,64,688]{3,2,1,0:T(8,128)(2,1)}, u32[]{:S(2)}, u32[]{:S(2)}) async-start(f16[8,4,64,688]{3,2,1,0:T(8,128)(2,1)} %convert_element_type.28), calls=%async_computation | async-start | bytes 6291456 | tf_op jit(solution)/shard_map/all_to_all | solution.py:191
  218.2 2.9 collective-permute-start.20
  221.1 2.8 collective-permute-start.19
  224.6 36.4 %collective-permute-done.20 = bf16[4,64,256]{2,1,0:T(8,128)(2,1)S(1)} collective-permute-done((bf16[4,64,256]{2,1,0:T(8,128)(2,1)S(1)}, bf16[4,64,256]{2,1,0:T(8,128)(2,1)S(1)}, u32[]{:S(2)}, u32[]{:S(2)}) %collective-permute-start.20) | collective-permute-done | bytes 131104 | tf_op jit(solution)/shard_map/ppermute | solution.py:24
  265.1 8.8 %collective-permute-done.24 = bf16[4,4,64,256]{3,2,1,0:T(8,128)(2,1)S(1)} collective-permute-done((bf16[4,4,64,256]{3,2,1,0:T(8,128)(2,1)S(1)}, bf16[4,4,64,256]{3,2,1,0:T(8,128)(2,1)S(1)}, u32[]{:S(2)}, u32[]{:S(2)}) %collective-permute-start.24) | collective-permute-done | bytes 524320 | tf_op jit(solution)/shard_map/ppermute | solution.py:24
  279.0 2.5 convert_reduce_fusion
  282.3 3.5 %all-to-all-start.1 = ((bf16[4,64,688]{2,1,0:T(8,128)(2,1)}), bf16[4,64,688]{2,1,0:T(8,128)(2,1)S(1)}, u32[]{:S(2)}, u32[]{:S(2)}) async-start(bf16[4,64,688]{2,1,0:T(8,128)(2,1)} %multiply_convert_fusion), calls=%async_computation.1 | async-start | bytes 786432 | tf_op jit(solution)/shard_map/all_to_all | solution.py:193
  286.9 2.8 pad_maximum_fusion.rows
  289.7 3.4 %all-to-all-done.1.out_ref = bf16[4,64,688]{2,1,0:T(8,128)(2,1)S(1)} async-done(((bf16[4,64,688]{2,1,0:T(8,128)(2,1)}), bf16[4,64,688]{2,1,0:T(8,128)(2,1)S(1)}, u32[]{:S(2)}, u32[]{:S(2)}) %all-to-all-start.1) | async-done | bytes 352288 | tf_op jit(solution)/shard_map/all_to_all | solution.py:193
  294.7 15.1 %shard_map.84 = f32[128,256]{1,0:T(8,128)S(1)} custom-call(s32[12]{0:T(128)S(1)} %pad_add_fusion.place, s32[1]{0:T(128)S(6)} %copy.22.live, bf16[4,64,688]{2,1,0:T(8,128)(2,1)S(1)} %all-to-all-done.1.out_ref, bf16[128,688]{1,0:T(8,128)(2,1)S(1)} %slice_bitcast_fusion.right, bf16[4,4,4,64,256]{4,3,2,1,0:T(8,128)(2,1)S(1)} %copy-done.1, f32[688,4096]{1,0:T(8,128)} %bitcast.74, ...), custom_call_target="tpu_custom_call" | custom-call | tf_op jit(solution)/shard_map/pallas_call | solution.py:120
  310.3 12.8 %all_to_all.36 = f32[16,1,1]{2,1,0:T(1,128)S(1)} all-to-all(f32[16,1,1]{2,1,0:T(1,128)S(1)} %copy.20), channel_id=1, replica_groups=mesh['zlo'=2,'x'=4,'core'=2,'y'=4,'zhi'=4] {'y','zhi'}, dimensions={0} | all-to-all | bytes 128 | tf_op jit(solution)/shard_map/all_to_all | solution.py:198
  (99 shorter events, 37.5 us)
Async XLA Ops:
  6.5 178.3 %all-gather.3.cloned.1.call-start = ((), (), s32[]{:S(2)}) async-start(), calls=%async_computation.7 | async-start | bytes 9510912 | tf_op jit(solution)/shard_map/all_gather | solution.py:153
  24.2 20.8 %all-to-all-start.3 = ((bf16[16,8,256]{2,1,0:T(8,128)(2,1)}), bf16[16,8,256]{2,1,0:T(8,128)(2,1)S(1)}, u32[]{:S(2)}, u32[]{:S(2)}) async-start(bf16[16,8,256]{2,1,0:T(8,128)(2,1)} %broadcast_in_dim.4), calls=%async_computation.3 | async-start | bytes 131072 | tf_op jit(solution)/shard_map/all_to_all | solution.py:176
  46.2 56.0 %all-to-all-start.4 = ((bf16[16,8,4784]{2,1,0:T(8,128)(2,1)}), bf16[16,8,4784]{2,1,0:T(8,128)(2,1)S(1)}, u32[]{:S(2)}, u32[]{:S(2)}) async-start(bf16[16,8,4784]{2,1,0:T(8,128)(2,1)} %broadcast_in_dim.5), calls=%async_computation.4 | async-start | bytes 2490368 | tf_op jit(solution)/shard_map/all_to_all | solution.py:181
  53.3 9.2 %collective-permute-start.17 = (bf16[256,256]{1,0:T(8,128)(2,1)S(1)}, bf16[256,256]{1,0:T(8,128)(2,1)S(1)}, u32[]{:S(2)}, u32[]{:S(2)}) collective-permute-start(bf16[256,256]{1,0:T(8,128)(2,1)S(1)} %copy-done.6), channel_id=1, source_target_pairs={{0,12},{4,0},{8,4},{12,8},{1,13},{5,1},{9,5},{13,9},{2,14},{6,2},{... | collective-permute-start | bytes 393224 | tf_op jit(solution)/shard_map/ppermute | solution.py:24
  54.5 13.7 %collective-permute-start.16 = (bf16[256,256]{1,0:T(8,128)(2,1)S(1)}, bf16[256,256]{1,0:T(8,128)(2,1)S(1)}, u32[]{:S(2)}, u32[]{:S(2)}) collective-permute-start(bf16[256,256]{1,0:T(8,128)(2,1)S(1)} %copy-done.6), channel_id=1, source_target_pairs={{0,8},{4,12},{8,0},{12,4},{1,9},{5,13},{9,1},{13,5},{2,10},{6,14},... | collective-permute-start | bytes 393224 | tf_op jit(solution)/shard_map/ppermute | solution.py:24
  56.0 19.2 %collective-permute-start.15 = (bf16[256,256]{1,0:T(8,128)(2,1)S(1)}, bf16[256,256]{1,0:T(8,128)(2,1)S(1)}, u32[]{:S(2)}, u32[]{:S(2)}) collective-permute-start(bf16[256,256]{1,0:T(8,128)(2,1)S(1)} %copy-done.6), channel_id=1, source_target_pairs={{0,4},{4,8},{8,12},{12,0},{1,5},{5,9},{9,13},{13,1},{2,6},{6,10},{... | collective-permute-start | bytes 393224 | tf_op jit(solution)/shard_map/ppermute | solution.py:24
  56.0 19.4 %collective-permute-start.11 = (bf16[64,256]{1,0:T(8,128)(2,1)S(1)}, bf16[64,256]{1,0:T(8,128)(2,1)S(1)}, u32[]{:S(2)}, u32[]{:S(2)}) collective-permute-start(bf16[64,256]{1,0:T(8,128)(2,1)S(1)} %get-tuple-element.22), channel_id=1, source_target_pairs={{0,12},{1,13},{2,44},{3,45},{4,76},{5,77},{6,108},{7,109},{8,140},... | collective-permute-start | bytes 98312 | tf_op jit(solution)/shard_map/ppermute | solution.py:52
  59.6 15.9 %collective-permute-start.10 = (bf16[64,256]{1,0:T(8,128)(2,1)S(1)}, bf16[64,256]{1,0:T(8,128)(2,1)S(1)}, u32[]{:S(2)}, u32[]{:S(2)}) collective-permute-start(bf16[64,256]{1,0:T(8,128)(2,1)S(1)} %get-tuple-element.23), channel_id=1, source_target_pairs={{0,8},{1,9},{2,40},{3,41},{4,72},{5,73},{6,104},{7,105},{8,136},{9... | collective-permute-start | bytes 98312 | tf_op jit(solution)/shard_map/ppermute | solution.py:52
  62.6 12.9 %collective-permute-start.9 = (bf16[64,256]{1,0:T(8,128)(2,1)S(1)}, bf16[64,256]{1,0:T(8,128)(2,1)S(1)}, u32[]{:S(2)}, u32[]{:S(2)}) collective-permute-start(bf16[64,256]{1,0:T(8,128)(2,1)S(1)} %get-tuple-element.24), channel_id=1, source_target_pairs={{0,4},{1,5},{2,36},{3,37},{4,68},{5,69},{6,100},{7,101},{8,132},{9... | collective-permute-start | bytes 98312 | tf_op jit(solution)/shard_map/ppermute | solution.py:52
  68.2 8.6 %collective-permute-start.8 = (bf16[64,256]{1,0:T(8,128)(2,1)S(1)}, bf16[64,256]{1,0:T(8,128)(2,1)S(1)}, u32[]{:S(2)}, u32[]{:S(2)}) collective-permute-start(bf16[64,256]{1,0:T(8,128)(2,1)S(1)} %get-tuple-element.21), channel_id=1, source_target_pairs={{0,0},{1,1},{2,32},{3,33},{4,64},{5,65},{6,96},{7,97},{8,128},{9,1... | collective-permute-start | bytes 98312 | tf_op jit(solution)/shard_map/ppermute | solution.py:52
  75.3 21.9 %collective-permute-start.18 = (bf16[4,256,256]{2,1,0:T(8,128)(2,1)S(1)}, bf16[4,256,256]{2,1,0:T(8,128)(2,1)S(1)}, u32[]{:S(2)}, u32[]{:S(2)}) collective-permute-start(bf16[4,256,256]{2,1,0:T(8,128)(2,1)S(1)} %get-tuple-element.12), channel_id=1, source_target_pairs={{0,16},{16,0},{1,17},{17,1},{2,18},{18,2},{3,19},{19,3},{4,20},{20... | collective-permute-start | bytes 1572872 | tf_op jit(solution)/shard_map/ppermute | solution.py:24
  76.8 19.4 %collective-permute-start.14 = (bf16[4,64,256]{2,1,0:T(8,128)(2,1)S(1)}, bf16[4,64,256]{2,1,0:T(8,128)(2,1)S(1)}, u32[]{:S(2)}, u32[]{:S(2)}) collective-permute-start(bf16[4,64,256]{2,1,0:T(8,128)(2,1)S(1)} %get-tuple-element.20), channel_id=1, source_target_pairs={{0,3},{1,0},{2,1},{3,2},{4,7},{5,4},{6,5},{7,6},{8,11},{9,8},{10,9... | collective-permute-start | bytes 393224 | tf_op jit(solution)/shard_map/ppermute | solution.py:24
  85.3 10.9 %collective-permute-start.13 = (bf16[4,64,256]{2,1,0:T(8,128)(2,1)S(1)}, bf16[4,64,256]{2,1,0:T(8,128)(2,1)S(1)}, u32[]{:S(2)}, u32[]{:S(2)}) collective-permute-start(bf16[4,64,256]{2,1,0:T(8,128)(2,1)S(1)} %get-tuple-element.20), channel_id=1, source_target_pairs={{0,2},{1,3},{2,0},{3,1},{4,6},{5,7},{6,4},{7,5},{8,10},{9,11},{10,... | collective-permute-start | bytes 393224 | tf_op jit(solution)/shard_map/ppermute | solution.py:24
  85.3 10.9 %collective-permute-start.12 = (bf16[4,64,256]{2,1,0:T(8,128)(2,1)S(1)}, bf16[4,64,256]{2,1,0:T(8,128)(2,1)}, u32[]{:S(2)}, u32[]{:S(2)}) collective-permute-start(bf16[4,64,256]{2,1,0:T(8,128)(2,1)S(1)} %get-tuple-element.20), channel_id=1, source_target_pairs={{0,1},{1,2},{2,3},{3,0},{4,5},{5,6},{6,7},{7,4},{8,9},{9,10},{10,1... | collective-permute-start | bytes 393224 | tf_op jit(solution)/shard_map/ppermute | solution.py:24
  102.2 96.0 %all-to-all-start.5 = ((f32[8,4,64,256]{3,2,1,0:T(8,128)}), f32[8,4,64,256]{3,2,1,0:T(8,128)}, u32[]{:S(2)}, u32[]{:S(2)}) async-start(f32[8,4,64,256]{3,2,1,0:T(8,128)} %shard_map.83), calls=%async_computation.5 | async-start | bytes 4194304 | tf_op jit(solution)/shard_map/all_to_all | solution.py:187
  109.8 33.6 %collective-permute-start.3 = (bf16[64,688]{1,0:T(8,128)(2,1)S(1)}, bf16[64,688]{1,0:T(8,128)(2,1)S(1)}, u32[]{:S(2)}, u32[]{:S(2)}) collective-permute-start(bf16[64,688]{1,0:T(8,128)(2,1)S(1)} %get-tuple-element.16), channel_id=1, source_target_pairs={{0,12},{1,13},{2,44},{3,45},{4,76},{5,77},{6,108},{7,109},{8,140},... | collective-permute-start | bytes 264200 | tf_op jit(solution)/shard_map/ppermute | solution.py:52
  111.7 31.7 %collective-permute-start.2 = (bf16[64,688]{1,0:T(8,128)(2,1)S(1)}, bf16[64,688]{1,0:T(8,128)(2,1)S(1)}, u32[]{:S(2)}, u32[]{:S(2)}) collective-permute-start(bf16[64,688]{1,0:T(8,128)(2,1)S(1)} %get-tuple-element.17), channel_id=1, source_target_pairs={{0,8},{1,9},{2,40},{3,41},{4,72},{5,73},{6,104},{7,105},{8,136},{9... | collective-permute-start | bytes 264200 | tf_op jit(solution)/shard_map/ppermute | solution.py:52
  115.7 27.7 %collective-permute-start.1 = (bf16[64,688]{1,0:T(8,128)(2,1)S(1)}, bf16[64,688]{1,0:T(8,128)(2,1)S(1)}, u32[]{:S(2)}, u32[]{:S(2)}) collective-permute-start(bf16[64,688]{1,0:T(8,128)(2,1)S(1)} %get-tuple-element.18), channel_id=1, source_target_pairs={{0,4},{1,5},{2,36},{3,37},{4,68},{5,69},{6,100},{7,101},{8,132},{9... | collective-permute-start | bytes 264200 | tf_op jit(solution)/shard_map/ppermute | solution.py:52
  123.2 20.2 %collective-permute-start = (bf16[64,688]{1,0:T(8,128)(2,1)S(1)}, bf16[64,688]{1,0:T(8,128)(2,1)S(1)}, u32[]{:S(2)}, u32[]{:S(2)}) collective-permute-start(bf16[64,688]{1,0:T(8,128)(2,1)S(1)} %get-tuple-element.15), channel_id=1, source_target_pairs={{0,0},{1,1},{2,32},{3,33},{4,64},{5,65},{6,96},{7,97},{8,128},{9,1... | collective-permute-start | bytes 264200 | tf_op jit(solution)/shard_map/ppermute | solution.py:52
  143.5 20.4 %collective-permute-start.6 = (bf16[4,64,688]{2,1,0:T(8,128)(2,1)S(1)}, bf16[4,64,688]{2,1,0:T(8,128)(2,1)S(1)}, u32[]{:S(2)}, u32[]{:S(2)}) collective-permute-start(bf16[4,64,688]{2,1,0:T(8,128)(2,1)S(1)} %get-tuple-element.14), channel_id=1, source_target_pairs={{0,3},{1,0},{2,1},{3,2},{4,7},{5,4},{6,5},{7,6},{8,11},{9,8},{10,9... | collective-permute-start | bytes 1056776 | tf_op jit(solution)/shard_map/ppermute | solution.py:24
  156.6 12.3 %collective-permute-start.4 = (bf16[4,64,688]{2,1,0:T(8,128)(2,1)S(1)}, bf16[4,64,688]{2,1,0:T(8,128)(2,1)S(1)}, u32[]{:S(2)}, u32[]{:S(2)}) collective-permute-start(bf16[4,64,688]{2,1,0:T(8,128)(2,1)S(1)} %get-tuple-element.14), channel_id=1, source_target_pairs={{0,1},{1,2},{2,3},{3,0},{4,5},{5,6},{6,7},{7,4},{8,9},{9,10},{10,1... | collective-permute-start | bytes 1056776 | tf_op jit(solution)/shard_map/ppermute | solution.py:24
  163.9 16.5 %collective-permute-start.7 = (bf16[2,64,688]{2,1,0:T(8,128)(2,1)S(1)}, bf16[2,64,688]{2,1,0:T(8,128)(2,1)S(1)}, u32[]{:S(2)}, u32[]{:S(2)}) collective-permute-start(bf16[2,64,688]{2,1,0:T(8,128)(2,1)S(1)} %slice.49), channel_id=1, source_target_pairs={{0,3},{1,0},{2,1},{3,2},{4,7},{5,4},{6,5},{7,6},{8,11},{9,8},{10,9... | collective-permute-start | bytes 528392 | tf_op jit(solution)/shard_map/ppermute | solution.py:24
  168.9 15.6 %collective-permute-start.5 = (bf16[2,64,688]{2,1,0:T(8,128)(2,1)S(1)}, bf16[2,64,688]{2,1,0:T(8,128)(2,1)S(1)}, u32[]{:S(2)}, u32[]{:S(2)}) collective-permute-start(bf16[2,64,688]{2,1,0:T(8,128)(2,1)S(1)} %slice.48), channel_id=1, source_target_pairs={{0,1},{1,2},{2,3},{3,0},{4,5},{5,6},{6,7},{7,4},{8,9},{9,10},{10,1... | collective-permute-start | bytes 528392 | tf_op jit(solution)/shard_map/ppermute | solution.py:24
  198.2 80.8 %all-to-all-start = ((f16[8,4,64,688]{3,2,1,0:T(8,128)(2,1)}), f16[8,4,64,688]{3,2,1,0:T(8,128)(2,1)}, u32[]{:S(2)}, u32[]{:S(2)}) async-start(f16[8,4,64,688]{3,2,1,0:T(8,128)(2,1)} %convert_element_type.28), calls=%async_computation | async-start | bytes 6291456 | tf_op jit(solution)/shard_map/all_to_all | solution.py:191
  216.0 8.6 %collective-permute-start.21 = (bf16[4,64,256]{2,1,0:T(8,128)(2,1)S(1)}, bf16[4,64,256]{2,1,0:T(8,128)(2,1)S(1)}, u32[]{:S(2)}, u32[]{:S(2)}) collective-permute-start(bf16[4,64,256]{2,1,0:T(8,128)(2,1)S(1)} %reduce_sum.58), channel_id=1, source_target_pairs={{0,3},{1,0},{2,1},{3,2},{4,7},{5,4},{6,5},{7,6},{8,11},{9,8},{10,9... | collective-permute-start | bytes 393224 | tf_op jit(solution)/shard_map/ppermute | solution.py:24
  218.2 42.8 %collective-permute-start.20 = (bf16[4,64,256]{2,1,0:T(8,128)(2,1)S(1)}, bf16[4,64,256]{2,1,0:T(8,128)(2,1)S(1)}, u32[]{:S(2)}, u32[]{:S(2)}) collective-permute-start(bf16[4,64,256]{2,1,0:T(8,128)(2,1)S(1)} %reduce_sum.58), channel_id=1, source_target_pairs={{0,2},{1,3},{2,0},{3,1},{4,6},{5,7},{6,4},{7,5},{8,10},{9,11},{10,... | collective-permute-start | bytes 393224 | tf_op jit(solution)/shard_map/ppermute | solution.py:24
  221.1 39.9 %collective-permute-start.19 = (bf16[4,64,256]{2,1,0:T(8,128)(2,1)S(1)}, bf16[4,64,256]{2,1,0:T(8,128)(2,1)S(1)}, u32[]{:S(2)}, u32[]{:S(2)}) collective-permute-start(bf16[4,64,256]{2,1,0:T(8,128)(2,1)S(1)} %reduce_sum.58), channel_id=1, source_target_pairs={{0,1},{1,2},{2,3},{3,0},{4,5},{5,6},{6,7},{7,4},{8,9},{9,10},{10,1... | collective-permute-start | bytes 393224 | tf_op jit(solution)/shard_map/ppermute | solution.py:24
  261.9 12.0 %collective-permute-start.24 = (bf16[4,4,64,256]{3,2,1,0:T(8,128)(2,1)S(1)}, bf16[4,4,64,256]{3,2,1,0:T(8,128)(2,1)S(1)}, u32[]{:S(2)}, u32[]{:S(2)}) collective-permute-start(bf16[4,4,64,256]{3,2,1,0:T(8,128)(2,1)S(1)} %get-tuple-element.10), channel_id=1, source_target_pairs={{0,12},{4,0},{8,4},{12,8},{1,13},{5,1},{9,5},{13,9},{2,14},{6,2},{... | collective-permute-start | bytes 1572872 | tf_op jit(solution)/shard_map/ppermute | solution.py:24
  261.9 13.7 %collective-permute-start.22 = (bf16[4,4,64,256]{3,2,1,0:T(8,128)(2,1)S(1)}, bf16[4,4,64,256]{3,2,1,0:T(8,128)(2,1)S(1)}, u32[]{:S(2)}, u32[]{:S(2)}) collective-permute-start(bf16[4,4,64,256]{3,2,1,0:T(8,128)(2,1)S(1)} %get-tuple-element.10), channel_id=1, source_target_pairs={{0,4},{4,8},{8,12},{12,0},{1,5},{5,9},{9,13},{13,1},{2,6},{6,10},{... | collective-permute-start | bytes 1572872 | tf_op jit(solution)/shard_map/ppermute | solution.py:24
  275.4 10.4 %collective-permute-start.25 = (bf16[2,4,64,256]{3,2,1,0:T(8,128)(2,1)}, bf16[2,4,64,256]{3,2,1,0:T(8,128)(2,1)}, u32[]{:S(2)}, u32[]{:S(2)}) collective-permute-start(bf16[2,4,64,256]{3,2,1,0:T(8,128)(2,1)} %slice.54), channel_id=1, source_target_pairs={{0,12},{4,0},{8,4},{12,8},{1,13},{5,1},{9,5},{13,9},{2,14},{6,2},{... | collective-permute-start | bytes 786440 | tf_op jit(solution)/shard_map/ppermute | solution.py:24
  277.2 8.6 %collective-permute-start.23 = (bf16[2,4,64,256]{3,2,1,0:T(8,128)(2,1)}, bf16[2,4,64,256]{3,2,1,0:T(8,128)(2,1)}, u32[]{:S(2)}, u32[]{:S(2)}) collective-permute-start(bf16[2,4,64,256]{3,2,1,0:T(8,128)(2,1)} %slice.53), channel_id=1, source_target_pairs={{0,4},{4,8},{8,12},{12,0},{1,5},{5,9},{9,13},{13,1},{2,6},{6,10},{... | collective-permute-start | bytes 786440 | tf_op jit(solution)/shard_map/ppermute | solution.py:24
  282.3 10.8 %all-to-all-start.1 = ((bf16[4,64,688]{2,1,0:T(8,128)(2,1)}), bf16[4,64,688]{2,1,0:T(8,128)(2,1)S(1)}, u32[]{:S(2)}, u32[]{:S(2)}) async-start(bf16[4,64,688]{2,1,0:T(8,128)(2,1)} %multiply_convert_fusion), calls=%async_computation.1 | async-start | bytes 786432 | tf_op jit(solution)/shard_map/all_to_all | solution.py:193
  (9 other events, 241.1 us)
Sparse Core Ops, SparseCore 0:
  9.2 64.9 all-gather.2

commit v3 on v0

v3 whole, which is shorter than its diff:
```python
import functools

import jax
import jax.numpy as jnp
from jax import lax
from jax.experimental import pallas as pl
from jax.experimental.pallas import tpu as pltpu
from jax.sharding import Mesh, PartitionSpec as P

SEQ_LEN = 256
RANK = 8
VMEM_LIMIT = 16 << 20
SCORE_LIMIT = 54 << 20
GROUPS = ((0,), (1, 3), (2,))
PIECES = 15
damping = 0.01
AXES = ("zlo", "x", "core", "y", "zhi")
SIZES = (2, 4, 2, 4, 4)
TRAIN = ("zlo", "x", "core")
FEAT = ("y", "zhi")
over_rows = (((0,), (0,)), ((), ()))


def shift(block, axis, step):
    size = SIZES[AXES.index(axis)]
    return lax.ppermute(block, axis, [(i, (i + step) % size) for i in range(size)])


def sides(block, axis):
    return shift(block, axis, 1), shift(block, axis, -1)


def opposite(one, three, axis):
    cut = one.shape[-2] // 2
    return shift(one[..., :cut, :], axis, 1), shift(three[..., cut:, :], axis, -1)


def direct(block, axis):
    return [block] + [shift(block, axis, step) for step in (1, 2, 3)]


def after(value, *earlier):
    return lax.optimization_barrier((value, *earlier))[0]


def everyone(block, axes, size):
    return lax.all_to_all(jnp.broadcast_to(block[None], (size,) + block.shape), axes, 0, 0)


def rotate_in_kernel(order, lhs, rhs, out, acc, acc_left):
    step = pl.program_id(0)
    width = lhs.shape[2]
    half = acc_left.shape[0]

    @pl.when(step == 0)
    def _():
        acc[...] = jnp.zeros_like(acc)
        acc_left[...] = jnp.zeros_like(acc_left)

    basis = rhs[0, :, :width]
    acc[...] += jnp.dot(lhs[0], basis, preferred_element_type=jnp.float32)
    acc_left[...] += lax.dot_general(
        rhs[0, :, width:], basis, over_rows, preferred_element_type=jnp.float32
    )

    @pl.when(step == pl.num_programs(0) - 1)
    def _():
        rows = acc.shape[0]
        out[:rows] = acc[...].astype(out.dtype)
        core = order[pl.num_programs(0)]
        mine = jnp.where(core == 0, acc_left[:half // 2], acc_left[half // 2 :])
        out[rows:] = mine.astype(out.dtype)


def rotate_in(order, lhs, rhs):
    blocks, rows, depth = lhs.shape
    cols = depth
    factors = rhs.shape[2] - cols
    return pl.pallas_call(
        rotate_in_kernel,
        grid_spec=pltpu.PrefetchScalarGridSpec(
            num_scalar_prefetch=1,
            grid=(blocks,),
            in_specs=[
                pl.BlockSpec((1, rows, depth), lambda b, order: (b, 0, 0)),
                pl.BlockSpec((1, depth, cols + factors), lambda b, order: (order[b], 0, 0)),
            ],
            out_specs=pl.BlockSpec((rows + factors // 2, cols), lambda b, order: (0, 0)),
            scratch_shapes=[
                pltpu.VMEM((rows, cols), jnp.float32),
                pltpu.VMEM((factors, cols), jnp.float32),
            ],
        ),
        out_shape=jax.ShapeDtypeStruct((rows + factors // 2, cols), jnp.bfloat16),
        compiler_params=pltpu.CompilerParams(vmem_limit_bytes=VMEM_LIMIT),
    )(order, lhs, rhs)


def score_kernel(order, columns, live, *refs):
    lhs, rest = refs[:PIECES], refs[PIECES:]
    right, rows, left, eig_hbm, near, far, out, met, acc, eig, held, lhs_sems, eig_sems, sems = rest
    slots = held.shape[0]
    ahead, width = eig.shape[0], eig.shape[2]

    def bring(number):
        start = pl.multiple_of(columns[number] * width, width)
        return pltpu.make_async_copy(
            eig_hbm.at[:, pl.ds(start, width)], eig.at[number % ahead], eig_sems.at[number % ahead]
        )

    for number in range(ahead - 1):
        bring(number).start()
    half = near.shape[0]
    moves, first = [], 0
    for base, count in ((0, 1), (5, 2), (10, 1)):
        cut = lhs[base + 2].shape[1]
        for piece, row in ((base, 0), (base + 1, 0), (base + 4, 0), (base + 2, 0), (base + 3, cut)):
            target = met.at[pl.ds(first, count), pl.ds(row, lhs[piece].shape[1])]
            moves.append((first, pltpu.make_async_copy(lhs[piece], target, lhs_sems.at[piece])))
            if piece != base + 2:
                first += count
    for _, move in moves:
        move.start()

    def fetch(number, act):
        slot = number % slots

        @pl.when(order[number] < half)
        def _():
            act(pltpu.make_async_copy(near.at[jnp.minimum(order[number], half - 1)], held.at[slot], sems.at[slot]))

        @pl.when(order[number] >= half)
        def _():
            act(pltpu.make_async_copy(far.at[jnp.maximum(order[number] - half, 0)], held.at[slot], sems.at[slot]))

    for number in range(slots - 1):
        fetch(number, lambda copy: copy.start())
    depth = near.shape[1]
    for number in range(met.shape[0]):
        if number + slots - 1 < met.shape[0]:
            fetch(number + slots - 1, lambda copy: copy.start())
        fetch(number, lambda copy: copy.wait())
        for first, move in moves:
            if first == number:
                move.wait()
        term = jnp.dot(
            met[number, :, :depth], held[number % slots], preferred_element_type=jnp.float32
        )
        if number == 0:
            acc[...] = term
        else:
            acc[...] += term
    position = lax.broadcasted_iota(jnp.int32, acc.shape, 0)
    out_t = jnp.where(position < live[0], acc[...], 0.0).astype(jnp.bfloat16).T
    seq = acc.shape[0]
    total = jnp.zeros(out.shape, jnp.float32)
    for i in range(rows.shape[0]):
        if i + ahead - 1 < rows.shape[0]:
            bring(i + ahead - 1).start()
        grad = jnp.dot(out_t, rows[i, :seq], preferred_element_type=jnp.float32)
        bring(i).wait()
        scaled = (grad / (eig[i % ahead] + damping)).astype(jnp.bfloat16)
        mapped = jnp.dot(right[...], scaled, preferred_element_type=jnp.float32)
        factors = jnp.concatenate([rows[i, seq:], left[i]], axis=0)
        total += mapped * factors.astype(jnp.float32)
    out[...] = total


def score(order, columns, live, lhs, near, far, right, rows, eig_t, left):
    (height, padded), cols = lhs[0].shape[1:], near.shape[2]
    factors, width = right.shape[0], rows.shape[2]
    vmem, smem = pl.BlockSpec(memory_space=pltpu.VMEM), pl.BlockSpec(memory_space=pltpu.SMEM)
    hbm = pl.BlockSpec(memory_space=pltpu.HBM)
    return pl.pallas_call(
        score_kernel,
        in_specs=[smem] * 3 + [hbm] * PIECES + [vmem] * 3 + [hbm] * 3,
        out_specs=vmem,
        scratch_shapes=[
            pltpu.VMEM((16, height, padded), jnp.bfloat16),
            pltpu.VMEM((height, cols), jnp.float32),
            pltpu.VMEM((4, cols, width), jnp.float32),
            pltpu.VMEM((4,) + near.shape[1:], jnp.bfloat16),
            pltpu.SemaphoreType.DMA((PIECES,)),
            pltpu.SemaphoreType.DMA((4,)),
            pltpu.SemaphoreType.DMA((4,)),
        ],
        out_shape=jax.ShapeDtypeStruct((factors, width), jnp.float32),
        compiler_params=pltpu.CompilerParams(vmem_limit_bytes=SCORE_LIMIT),
    )(order, columns, live, *lhs, right, rows, left, eig_t, near, far)


def local(
    activations, grad_outputs, in_basis, out_basis, eigenvalues, query_left, query_right, lengths
):
    zlo, x, core = lax.axis_index("zlo"), lax.axis_index("x"), lax.axis_index("core")
    y, zhi = lax.axis_index("y"), lax.axis_index("zhi")
    bf16, f32 = jnp.bfloat16, jnp.float32
    trains, feats = 16, 16
    factors = query_left.shape[1]
    share = factors // trains
    slab = out_basis.shape[1]
    width = in_basis.shape[1]

    u_own = jnp.concatenate([in_basis, query_left], axis=1)
    u_far = shift(u_own, "zlo", 1)
    u_all = lax.all_gather(jnp.stack([u_own, u_far]), ("x", "core"), axis=0, tiled=True)
    near = lax.all_gather(after(out_basis, u_far), ("x", "core"), axis=0, tiled=False)
    block = jnp.arange(feats, dtype=jnp.int32)
    u_place = lax.rem(block, 8) * 2 + lax.rem(zlo + block // 8, 2)

    right_part = lax.dot_general(query_right, out_basis, over_rows, preferred_element_type=f32)
    half = factors // 2
    low, high = right_part[:half], right_part[half:]
    right_core = jnp.where(core == 0, low, high) + shift(jnp.where(core == 0, high, low), "core", 1)
    right_pair = right_core + shift(right_core, "zlo", 1)
    right_x = right_pair + lax.ppermute(right_pair, "x", [(i, i ^ 1) for i in range(4)])
    right_sum = right_x + lax.ppermute(right_x, "x", [(i, i ^ 2) for i in range(4)])
    right_own = right_sum.astype(bf16)

    act_z = everyone(after(activations, u_far), "zhi", 4)
    padding = -slab % 256
    own = jnp.pad(grad_outputs, ((0, 0), (0, padding)))[None]
    own_1, own_3 = sides(own, "y")

    act_all = everyone(after(act_z, own_1, own_3, right_core), "y", 4).reshape(feats, SEQ_LEN, width)
    z_1, z_3 = sides(after(own, act_z), "zhi")
    own_2 = opposite(own_1, own_3, "y")
    in_rot = rotate_in(
        jnp.concatenate([u_place, core[None].astype(jnp.int32)]),
        after(act_all, z_1, z_3, *own_2, right_pair),
        u_all,
    )

    pair = jnp.concatenate([z_1, z_3], axis=0)
    pair_1, pair_3 = sides(pair, "y")
    v_far = shift(after(out_basis, z_1, z_3), "zlo", 1)
    in_z = everyone(after(in_rot, right_x), "zhi", 4)
    z_2 = jnp.concatenate(opposite(after(z_1, right_own), after(z_3, right_own), "zhi"), axis=-2)
    far = lax.all_gather(after(v_far, in_z, pair_1, pair_3), ("x", "core"), axis=0, tiled=False)

    in_all = everyone(after(in_z, pair_1, pair_3), "y", 4)
    in_all = in_all.reshape(feats, SEQ_LEN + factors // 2, width)
    pair_2 = opposite(pair_1, pair_3, "y")
    far_1, far_3 = sides(z_2, "y")
    far_2 = opposite(far_1, far_3, "y")

    left_other = shift(in_all[:, SEQ_LEN:], "core", 1)

    pieces = (own, own_1, *own_2, own_3, pair, pair_1, *pair_2, pair_3, z_2, far_1, *far_2, far_3)
    steps = [(k, z) for group in GROUPS for k in (0, 1, 3, 2) for z in group]
    y_steps, z_steps = (jnp.array(v, jnp.int32) for v in zip(*steps))
    numbers = lax.rem(y - y_steps + 4, 4) * 4 + lax.rem(zhi - z_steps + 4, 4)
    numbers = lax.rem(numbers - zlo * 8 + 16, 16).astype(jnp.int32)

    right_here = jnp.concatenate([right_own, shift(right_own, "core", 1)], axis=0)
    eig_t = jnp.transpose(eigenvalues)
    total = score(
        numbers, block, lengths, pieces, near, far, right_here, in_all, eig_t, left_other
    )
    sums = jnp.sum(total, axis=1)
    sums = jnp.where(core == 0, sums, jnp.concatenate([sums[half:], sums[:half]]))
    queries = factors // RANK
    partial = jnp.sum(sums.reshape(queries, RANK), axis=1)
    pieces = lax.all_to_all(partial.reshape(feats, 1, 1), FEAT, 0, 0)
    return jnp.sum(pieces, axis=0)


def solution(mesh):
    fine = Mesh(mesh.devices.reshape(SIZES), AXES)
    in_specs = (
        P(TRAIN, FEAT),
        P(TRAIN, FEAT),
        P(TRAIN, FEAT),
        P(TRAIN, FEAT),
        P(None, FEAT),
        P(TRAIN, None),
        P(TRAIN, None),
        P(TRAIN),
    )
    return jax.shard_map(
        local, mesh=fine, in_specs=in_specs, out_specs=P(TRAIN, FEAT), check_vma=False
    )
```

time: 556 us -> 225 us (0.40)
  waiting for transfers between devices: 460 us -> 76.9 us
  starting transfers between devices: 0.27 us -> 60.8 us
  matrix products: 38.6 us -> 0.35 us
  Pallas kernels: 0 us -> 26.4 us
  blocking collectives: 42.7 us -> 16.4 us
  local copies, waits for them, and re-layouts: 0.67 us -> 23.2 us
  other arithmetic: 0.13 us -> 5.86 us
    all_gather x8 -> x3, waiting for transfers between devices: 456 us -> 0.04 us  [the longest x1 0.02 us: local(): lax.all_gather(after(out_basis, u_far), ('x', 'core'), axis=0, tiled=False)]
    ppermute x0 -> x24, waiting for transfers between devices: none -> 67.3 us  [the longest x22 57.6 us: shift(): lax.ppermute(block, axis, [(i, (i + step) % size) for i in range(size)])]
    psum x1 -> x0, blocking collectives: 42.7 us -> none  [local(): summed = lax.psum(partial_scores, 'feat')]
    dot_general x5 -> x1, matrix products: 38.6 us -> 0.35 us  [local(): lax.dot_general(query_right, out_basis, over_rows, preferred_element_type...]
    ppermute x0 -> x24, starting transfers between devices: none -> 36 us  [the longest x22 34.1 us: shift(): lax.ppermute(block, axis, [(i, (i + step) % size) for i in range(size)])]
    pallas_call x0 -> x2, Pallas kernels: none -> 26.4 us  [the longest x1 22 us: score(): pl.pallas_call(score_kernel, in_specs=[smem] * 3 + [hbm] * PIECES + [vmem...]
    all_to_all x0 -> x4, starting transfers between devices: none -> 24.7 us  [everyone(): lax.all_to_all(jnp.broadcast_to(block[None], (size,) + block.shape), axes...]
    all_to_all x0 -> x1, blocking collectives: none -> 16.4 us  [local(): pieces = lax.all_to_all(partial.reshape(feats, 1, 1), FEAT, 0, 0)]
  transfers between devices with their start and end apart: 8 -> 31, of which waited for: 8 -> 13; matrix products, arithmetic and copies ran while one was open for 5% -> 9% of each run, Pallas kernels for 0% -> 2%
where the time goes in v3:
time: 225 us; the launch traced here: 224 us
  waiting for transfers between devices  76.9 us (34%)
  starting transfers between devices  60.8 us (27%)
  Pallas kernels  26.4 us (12%)
  local copies, waits for them, and re-layouts  23.2 us (10%)
  blocking collectives  16.4 us (7%)
  between operations  14.1 us (6%)
  other arithmetic  5.86 us (3%)
    ppermute x22, waiting for transfers between devices, shift(): lax.ppermute(block, axis, [(i, (i + step) % size) for i in range(size)])  57.6 us
    ppermute x22, starting transfers between devices, shift(): lax.ppermute(block, axis, [(i, (i + step) % size) for i in range(size)])  34.1 us
    all_to_all x4, starting transfers between devices, everyone(): lax.all_to_all(jnp.broadcast_to(block[None], (size,) + block.shape), axes...  24.7 us
    pallas_call x1, Pallas kernels, score(): pl.pallas_call(score_kernel, in_specs=[smem] * 3 + [hbm] * PIECES + [vmem...  22 us
    all_to_all x1, blocking collectives, local(): pieces = lax.all_to_all(partial.reshape(feats, 1, 1), FEAT, 0, 0)  16.4 us
    all_to_all x4, waiting for transfers between devices, everyone(): lax.all_to_all(jnp.broadcast_to(block[None], (size,) + block.shape), axes...  8.86 us
    ppermute x1, waiting for transfers between devices, local(): lax.ppermute(right_x, 'x', [(i, i ^ 2) for i in range(4)])  6.54 us
    unnamed x36, local copies, waits for them, and re-layouts  6.32 us
  transfers between devices with their start and end apart: 31, of which 13 were waited for; matrix products, arithmetic and copies ran while one was open for 9% of the time, Pallas kernels for 2%

profile of v3, /device:TPU:4, one launch (start us, length us, event | category | flops | bytes accessed | tf_op | source)
XLA Modules:
  0.0 224.1 jit_solution(13250262729832344594)
XLA Ops:
  8.5 2.0 collective-permute-start.4
  10.5 4.9 %collective-permute-done.4 = bf16[256,384]{1,0:T(8,128)(2,1)S(1)} collective-permute-done((bf16[256,384]{1,0:T(8,128)(2,1)S(1)}, bf16[256,384]{1,0:T(8,128)(2,1)S(1)}, u32[]{:S(2)}, u32[]{:S(2)}) %collective-permute-start.4) | collective-permute-done | bytes 196640 | tf_op jit(solution)/shard_map/ppermute | solution.py:26
  17.8 8.3 %all-to-all-start = ((bf16[4,256,256]{2,1,0:T(8,128)(2,1)}), bf16[4,256,256]{2,1,0:T(8,128)(2,1)S(1)}, u32[]{:S(2)}, u32[]{:S(2)}) async-start(bf16[4,256,256]{2,1,0:T(8,128)(2,1)} %broadcast_in_dim.13), calls=%async_computation | async-start | bytes 1048576 | tf_op jit(solution)/shard_map/all_to_all | solution.py:47
  26.8 1.7 collective-permute-start
  28.5 1.7 collective-permute-start.2
  30.2 9.5 %collective-permute-done.refs_1_ = bf16[1,256,768]{2,1,0:T(8,128)(2,1)S(1)} collective-permute-done((bf16[1,256,768]{2,1,0:T(8,128)(2,1)S(1)}, bf16[1,256,768]{2,1,0:T(8,128)(2,1)S(1)}, u32[]{:S(2)}, u32[]{:S(2)}) %collective-permute-start) | collective-permute-done | bytes 393248 | tf_op jit(solution)/shard_map/ppermute | solution.py:26
  42.5 4.5 %all-to-all-start.1 = ((bf16[4,4,256,256]{3,2,1,0:T(8,128)(2,1)}), bf16[4,4,256,256]{3,2,1,0:T(8,128)(2,1)S(1)}, u32[]{:S(2)}, u32[]{:S(2)}) async-start(bf16[4,4,256,256]{3,2,1,0:T(8,128)(2,1)} %broadcast_in_dim.15), calls=%async_computation.1 | async-start | bytes 4194304 | tf_op jit(solution)/shard_map/all_to_all | solution.py:47
  46.9 2.0 collective-permute-start.12
  49.9 3.2 %collective-permute-start.6 = (bf16[1,256,768]{2,1,0:T(8,128)(2,1)}, bf16[1,256,768]{2,1,0:T(8,128)(2,1)}, u32[]{:S(2)}, u32[]{:S(2)}) collective-permute-start(bf16[1,256,768]{2,1,0:T(8,128)(2,1)} %copy-done.7), channel_id=1, source_target_pairs={{0,3},{1,0},{2,1},{3,2},{4,7},{5,4},{6,5},{7,6},{8,11},{9,8},{10,9... | collective-permute-start | bytes 1179656 | tf_op jit(solution)/shard_map/ppermute | solution.py:26
  53.1 9.5 %collective-permute-done.12 = f32[64,688]{1,0:T(8,128)} collective-permute-done((f32[64,688]{1,0:T(8,128)S(1)}, f32[64,688]{1,0:T(8,128)}, u32[]{:S(2)}, u32[]{:S(2)}) %collective-permute-start.12) | collective-permute-done | bytes 176160 | tf_op jit(solution)/shard_map/ppermute | solution.py:26
  65.8 2.0 collective-permute-start.1
  70.2 3.2 %collective-permute-done.13 = f32[64,688]{1,0:T(8,128)S(1)} collective-permute-done((f32[64,688]{1,0:T(8,128)S(1)}, f32[64,688]{1,0:T(8,128)S(1)}, u32[]{:S(2)}, u32[]{:S(2)}) %collective-permute-start.13) | collective-permute-done | bytes 176160 | tf_op jit(solution)/shard_map/ppermute | solution.py:216
  73.5 2.5 %collective-permute-start.23 = (bf16[688,688]{1,0:T(8,128)(2,1)S(1)}, bf16[688,688]{1,0:T(8,128)(2,1)}, u32[]{:S(2)}, u32[]{:S(2)}) collective-permute-start(bf16[688,688]{1,0:T(8,128)(2,1)S(1)} %copy-done.3), channel_id=1, source_target_pairs={{0,128},{128,0},{1,129},{129,1},{2,130},{130,2},{3,131},{131,3},{4... | collective-permute-start | bytes 2840072 | tf_op jit(solution)/shard_map/ppermute | solution.py:26
  76.9 1.9 copy-done.1
  78.8 4.3 %shard_map.100 = bf16[320,256]{1,0:T(8,128)(2,1)S(1)} custom-call(s32[17]{0:T(128)S(1)} %pad_add_fusion.order, bf16[16,256,256]{2,1,0:T(8,128)(2,1)S(1)} %bitcast.14, bf16[16,256,384]{2,1,0:T(8,128)(2,1)S(1)} %copy-done.1), custom_call_target="tpu_custom_call" | custom-call | tf_op jit(solution)/shard_map/pallas_call | solution.py:79
  84.0 7.7 %all-to-all-start.2 = ((bf16[4,320,256]{2,1,0:T(8,128)(2,1)}), bf16[4,320,256]{2,1,0:T(8,128)(2,1)S(1)}, u32[]{:S(2)}, u32[]{:S(2)}) async-start(bf16[4,320,256]{2,1,0:T(8,128)(2,1)} %broadcast_in_dim.16), calls=%async_computation.2 | async-start | bytes 1310720 | tf_op jit(solution)/shard_map/all_to_all | solution.py:47
  93.8 3.2 %collective-permute-start.9 = (bf16[2,256,768]{2,1,0:T(8,128)(2,1)S(1)}, bf16[2,256,768]{2,1,0:T(8,128)(2,1)}, u32[]{:S(2)}, u32[]{:S(2)}) collective-permute-start(bf16[2,256,768]{2,1,0:T(8,128)(2,1)S(1)} %constant_dynamic-update-slice_fusion.2.refs_5_), channel_id=1, source_target_pairs={{0,12},{4,0},{8,4},{12,8},{1,13},{5,1},{9,5},{13,9},{2,14},{6,2},{... | collective-permute-start | bytes 2359304 | tf_op jit(solution)/shard_map/ppermute | solution.py:26
  97.0 17.2 %collective-permute-done.7.refs_6_ = bf16[2,256,768]{2,1,0:T(8,128)(2,1)S(1)} collective-permute-done((bf16[2,256,768]{2,1,0:T(8,128)(2,1)S(1)}, bf16[2,256,768]{2,1,0:T(8,128)(2,1)S(1)}, u32[]{:S(2)}, u32[]{:S(2)}) %collective-permute-start.7) | collective-permute-done | bytes 786464 | tf_op jit(solution)/shard_map/ppermute | solution.py:26
  114.3 1.7 broadcast_in_dim.17
  116.0 4.3 %all-to-all-start.3 = ((bf16[4,4,320,256]{3,2,1,0:T(8,128)(2,1)}), bf16[4,4,320,256]{3,2,1,0:T(8,128)(2,1)S(1)}, u32[]{:S(2)}, u32[]{:S(2)}) async-start(bf16[4,4,320,256]{3,2,1,0:T(8,128)(2,1)} %broadcast_in_dim.17), calls=%async_computation.3 | async-start | bytes 5242880 | tf_op jit(solution)/shard_map/all_to_all | solution.py:47
  121.0 6.5 %collective-permute-done.14 = f32[64,688]{1,0:T(8,128)S(1)} collective-permute-done((f32[64,688]{1,0:T(8,128)S(1)}, f32[64,688]{1,0:T(8,128)S(1)}, u32[]{:S(2)}, u32[]{:S(2)}) %collective-permute-start.14) | collective-permute-done | bytes 176160 | tf_op jit(solution)/shard_map/ppermute | solution.py:217
  128.5 2.8 %collective-permute-start.15 = (bf16[1,128,768]{2,1,0:T(8,128)(2,1)S(1)}, bf16[1,128,768]{2,1,0:T(8,128)(2,1)S(1)}, u32[]{:S(2)}, u32[]{:S(2)}) collective-permute-start(bf16[1,128,768]{2,1,0:T(8,128)(2,1)S(1)} %slice.59), channel_id=1, source_target_pairs={{0,1},{1,2},{2,3},{3,0},{4,5},{5,6},{6,7},{7,4},{8,9},{9,10},{10,1... | collective-permute-start | bytes 589832 | tf_op jit(solution)/shard_map/ppermute | solution.py:26
  132.3 1.7 collective-permute-start.16
  134.0 2.7 %collective-permute-done.15 = bf16[1,128,768]{2,1,0:T(8,128)(2,1)S(1)} collective-permute-done((bf16[1,128,768]{2,1,0:T(8,128)(2,1)S(1)}, bf16[1,128,768]{2,1,0:T(8,128)(2,1)S(1)}, u32[]{:S(2)}, u32[]{:S(2)}) %collective-permute-start.15) | collective-permute-done | bytes 196640 | tf_op jit(solution)/shard_map/ppermute | solution.py:26
  137.3 4.0 %collective-permute-done.16 = bf16[1,128,768]{2,1,0:T(8,128)(2,1)S(1)} collective-permute-done((bf16[1,128,768]{2,1,0:T(8,128)(2,1)S(1)}, bf16[1,128,768]{2,1,0:T(8,128)(2,1)S(1)}, u32[]{:S(2)}, u32[]{:S(2)}) %collective-permute-start.16) | collective-permute-done | bytes 196640 | tf_op jit(solution)/shard_map/ppermute | solution.py:26
  142.1 2.3 %collective-permute-start.17 = (bf16[1,256,768]{2,1,0:T(8,128)(2,1)}, bf16[1,256,768]{2,1,0:T(8,128)(2,1)S(1)}, u32[]{:S(2)}, u32[]{:S(2)}) collective-permute-start(bf16[1,256,768]{2,1,0:T(8,128)(2,1)} %constant_dynamic-update-slice_fusion.4.refs_10_), channel_id=1, source_target_pairs={{0,4},{4,8},{8,12},{12,0},{1,5},{5,9},{9,13},{13,1},{2,6},{6,10},{... | collective-permute-start | bytes 1179656 | tf_op jit(solution)/shard_map/ppermute | solution.py:26
  145.3 8.5 %all-to-all-done.3 = bf16[4,4,320,256]{3,2,1,0:T(8,128)(2,1)S(1)} async-done(((bf16[4,4,320,256]{3,2,1,0:T(8,128)(2,1)}), bf16[4,4,320,256]{3,2,1,0:T(8,128)(2,1)S(1)}, u32[]{:S(2)}, u32[]{:S(2)}) %all-to-all-start.3) | async-done | bytes 2621472 | tf_op jit(solution)/shard_map/all_to_all | solution.py:47
  155.2 1.8 slice.69
  161.4 3.0 %collective-permute-start.20 = (bf16[1,128,768]{2,1,0:T(8,128)(2,1)S(1)}, bf16[1,128,768]{2,1,0:T(8,128)(2,1)}, u32[]{:S(2)}, u32[]{:S(2)}) collective-permute-start(bf16[1,128,768]{2,1,0:T(8,128)(2,1)S(1)} %slice.73), channel_id=1, source_target_pairs={{0,12},{4,0},{8,4},{12,8},{1,13},{5,1},{9,5},{13,9},{2,14},{6,2},{... | collective-permute-start | bytes 589832 | tf_op jit(solution)/shard_map/ppermute | solution.py:26
  167.2 9.0 %collective-permute-done.18.refs_12_ = bf16[1,128,768]{2,1,0:T(8,128)(2,1)S(1)} collective-permute-done((bf16[1,128,768]{2,1,0:T(8,128)(2,1)S(1)}, bf16[1,128,768]{2,1,0:T(8,128)(2,1)S(1)}, u32[]{:S(2)}, u32[]{:S(2)}) %collective-permute-start.18) | collective-permute-done | bytes 196640 | tf_op jit(solution)/shard_map/ppermute | solution.py:26
  176.9 22.0 %shard_map.101 = f32[128,256]{1,0:T(8,128)} custom-call(s32[16]{0:T(128)} %compare_select_fusion.2.order, s32[16]{0:T(128)} %iota.7.columns, s32[1]{0:T(128)S(6)} %copy.25.live, bf16[1,256,768]{2,1,0:T(8,128)(2,1)} %copy-done.7, bf16[1,256,768]{2,1,0:T(8,128)(2,1)} %copy-done.8, bf16[1,128,768]{2,1,0:T(8,128)(2,1)} %copy-done.11, ...), custom_call_target="tpu_custom_call" | custom-call | tf_op jit(solution)/shard_map/pallas_call | solution.py:174
  200.5 16.4 %all_to_all.25 = f32[16,1,1]{2,1,0:T(1,128)S(1)} all-to-all(f32[16,1,1]{2,1,0:T(1,128)S(1)} %copy.20), channel_id=1, replica_groups=mesh['zlo'=2,'x'=4,'core'=2,'y'=4,'zhi'=4] {'y','zhi'}, dimensions={0} | all-to-all | bytes 128 | tf_op jit(solution)/shard_map/all_to_all | solution.py:264
  (109 shorter events, 33.8 us)
Async XLA Ops:
  6.5 70.3 %all-gather.6.cloned.1.call-start = ((), (), s32[]{:S(2)}) async-start(), calls=%async_computation.5 | async-start | bytes 3538944 | tf_op jit(solution)/shard_map/all_gather | solution.py:206
  8.5 6.9 %collective-permute-start.4 = (bf16[256,384]{1,0:T(8,128)(2,1)S(1)}, bf16[256,384]{1,0:T(8,128)(2,1)S(1)}, u32[]{:S(2)}, u32[]{:S(2)}) collective-permute-start(bf16[256,384]{1,0:T(8,128)(2,1)S(1)} %constant_dynamic-update-slice_fusion), channel_id=1, source_target_pairs={{0,128},{128,0},{1,129},{129,1},{2,130},{130,2},{3,131},{131,3},{4... | collective-permute-start | bytes 589832 | tf_op jit(solution)/shard_map/ppermute | solution.py:26
  16.2 160.0 %all-gather.8.cloned.1.call-start = ((), (), s32[]{:S(2)}) async-start(), calls=%async_computation.6 | async-start | bytes 9510912 | tf_op jit(solution)/shard_map/all_gather | solution.py:207
  17.8 23.1 %all-to-all-start = ((bf16[4,256,256]{2,1,0:T(8,128)(2,1)}), bf16[4,256,256]{2,1,0:T(8,128)(2,1)S(1)}, u32[]{:S(2)}, u32[]{:S(2)}) async-start(bf16[4,256,256]{2,1,0:T(8,128)(2,1)} %broadcast_in_dim.13), calls=%async_computation | async-start | bytes 1048576 | tf_op jit(solution)/shard_map/all_to_all | solution.py:47
  26.5 3.7 %collective-permute-start.11 = (f32[64,688]{1,0:T(8,128)S(1)}, f32[64,688]{1,0:T(8,128)S(1)}, u32[]{:S(2)}, u32[]{:S(2)}) collective-permute-start(f32[64,688]{1,0:T(8,128)S(1)} %slice_select_fusion), channel_id=1, source_target_pairs={{0,16},{16,0},{1,17},{17,1},{2,18},{18,2},{3,19},{19,3},{4,20},{20... | collective-permute-start | bytes 528392 | tf_op jit(solution)/shard_map/ppermute | solution.py:26
  26.8 12.9 %collective-permute-start = (bf16[1,256,768]{2,1,0:T(8,128)(2,1)S(1)}, bf16[1,256,768]{2,1,0:T(8,128)(2,1)S(1)}, u32[]{:S(2)}, u32[]{:S(2)}) collective-permute-start(bf16[1,256,768]{2,1,0:T(8,128)(2,1)S(1)} %pad_bitcast_fusion.refs_0_), channel_id=1, source_target_pairs={{0,4},{4,8},{8,12},{12,0},{1,5},{5,9},{9,13},{13,1},{2,6},{6,10},{... | collective-permute-start | bytes 1179656 | tf_op jit(solution)/shard_map/ppermute | solution.py:26
  28.5 12.0 %collective-permute-start.2 = (bf16[1,256,768]{2,1,0:T(8,128)(2,1)S(1)}, bf16[1,256,768]{2,1,0:T(8,128)(2,1)}, u32[]{:S(2)}, u32[]{:S(2)}) collective-permute-start(bf16[1,256,768]{2,1,0:T(8,128)(2,1)S(1)} %pad_bitcast_fusion.refs_0_), channel_id=1, source_target_pairs={{0,12},{4,0},{8,4},{12,8},{1,13},{5,1},{9,5},{13,9},{2,14},{6,2},{... | collective-permute-start | bytes 1179656 | tf_op jit(solution)/shard_map/ppermute | solution.py:26
  42.5 34.4 %all-to-all-start.1 = ((bf16[4,4,256,256]{3,2,1,0:T(8,128)(2,1)}), bf16[4,4,256,256]{3,2,1,0:T(8,128)(2,1)S(1)}, u32[]{:S(2)}, u32[]{:S(2)}) async-start(bf16[4,4,256,256]{3,2,1,0:T(8,128)(2,1)} %broadcast_in_dim.15), calls=%async_computation.1 | async-start | bytes 4194304 | tf_op jit(solution)/shard_map/all_to_all | solution.py:47
  46.9 15.7 %collective-permute-start.12 = (f32[64,688]{1,0:T(8,128)S(1)}, f32[64,688]{1,0:T(8,128)}, u32[]{:S(2)}, u32[]{:S(2)}) collective-permute-start(f32[64,688]{1,0:T(8,128)S(1)} %select_add_fusion), channel_id=1, source_target_pairs={{0,128},{128,0},{1,129},{129,1},{2,130},{130,2},{3,131},{131,3},{4... | collective-permute-start | bytes 528392 | tf_op jit(solution)/shard_map/ppermute | solution.py:26
  49.0 24.5 %collective-permute-start.5 = (bf16[1,256,768]{2,1,0:T(8,128)(2,1)}, bf16[1,256,768]{2,1,0:T(8,128)(2,1)}, u32[]{:S(2)}, u32[]{:S(2)}) collective-permute-start(bf16[1,256,768]{2,1,0:T(8,128)(2,1)} %copy-done.7), channel_id=1, source_target_pairs={{0,1},{1,2},{2,3},{3,0},{4,5},{5,6},{6,7},{7,4},{8,9},{9,10},{10,1... | collective-permute-start | bytes 1179656 | tf_op jit(solution)/shard_map/ppermute | solution.py:26
  49.9 23.6 %collective-permute-start.6 = (bf16[1,256,768]{2,1,0:T(8,128)(2,1)}, bf16[1,256,768]{2,1,0:T(8,128)(2,1)}, u32[]{:S(2)}, u32[]{:S(2)}) collective-permute-start(bf16[1,256,768]{2,1,0:T(8,128)(2,1)} %copy-done.7), channel_id=1, source_target_pairs={{0,3},{1,0},{2,1},{3,2},{4,7},{5,4},{6,5},{7,6},{8,11},{9,8},{10,9... | collective-permute-start | bytes 1179656 | tf_op jit(solution)/shard_map/ppermute | solution.py:26
  63.6 9.8 %collective-permute-start.13 = (f32[64,688]{1,0:T(8,128)S(1)}, f32[64,688]{1,0:T(8,128)S(1)}, u32[]{:S(2)}, u32[]{:S(2)}) collective-permute-start(f32[64,688]{1,0:T(8,128)S(1)} %add.41), channel_id=1, source_target_pairs={{0,32},{32,0},{64,96},{96,64},{1,33},{33,1},{65,97},{97,65},{2,34}... | collective-permute-start | bytes 528392 | tf_op jit(solution)/shard_map/ppermute | solution.py:216
  65.8 10.3 %collective-permute-start.1 = (bf16[1,128,768]{2,1,0:T(8,128)(2,1)S(1)}, bf16[1,128,768]{2,1,0:T(8,128)(2,1)S(1)}, u32[]{:S(2)}, u32[]{:S(2)}) collective-permute-start(bf16[1,128,768]{2,1,0:T(8,128)(2,1)S(1)} %slice.66), channel_id=1, source_target_pairs={{0,4},{4,8},{8,12},{12,0},{1,5},{5,9},{9,13},{13,1},{2,6},{6,10},{... | collective-permute-start | bytes 589832 | tf_op jit(solution)/shard_map/ppermute | solution.py:26
  68.8 8.0 %collective-permute-start.3 = (bf16[1,128,768]{2,1,0:T(8,128)(2,1)S(1)}, bf16[1,128,768]{2,1,0:T(8,128)(2,1)}, u32[]{:S(2)}, u32[]{:S(2)}) collective-permute-start(bf16[1,128,768]{2,1,0:T(8,128)(2,1)S(1)} %slice.67), channel_id=1, source_target_pairs={{0,12},{4,0},{8,4},{12,8},{1,13},{5,1},{9,5},{13,9},{2,14},{6,2},{... | collective-permute-start | bytes 589832 | tf_op jit(solution)/shard_map/ppermute | solution.py:26
  73.5 40.8 %collective-permute-start.23 = (bf16[688,688]{1,0:T(8,128)(2,1)S(1)}, bf16[688,688]{1,0:T(8,128)(2,1)}, u32[]{:S(2)}, u32[]{:S(2)}) collective-permute-start(bf16[688,688]{1,0:T(8,128)(2,1)S(1)} %copy-done.3), channel_id=1, source_target_pairs={{0,128},{128,0},{1,129},{129,1},{2,130},{130,2},{3,131},{131,3},{4... | collective-permute-start | bytes 2840072 | tf_op jit(solution)/shard_map/ppermute | solution.py:26
  84.0 30.3 %all-to-all-start.2 = ((bf16[4,320,256]{2,1,0:T(8,128)(2,1)}), bf16[4,320,256]{2,1,0:T(8,128)(2,1)S(1)}, u32[]{:S(2)}, u32[]{:S(2)}) async-start(bf16[4,320,256]{2,1,0:T(8,128)(2,1)} %broadcast_in_dim.16), calls=%async_computation.2 | async-start | bytes 1310720 | tf_op jit(solution)/shard_map/all_to_all | solution.py:47
  91.6 84.7 %all-gather.10.cloned.1.call-start = ((), (), s32[]{:S(2)}) async-start(), calls=%async_computation.7 | async-start | bytes 9510912 | tf_op jit(solution)/shard_map/all_gather | solution.py:239
  93.7 20.6 %collective-permute-start.7 = (bf16[2,256,768]{2,1,0:T(8,128)(2,1)S(1)}, bf16[2,256,768]{2,1,0:T(8,128)(2,1)S(1)}, u32[]{:S(2)}, u32[]{:S(2)}) collective-permute-start(bf16[2,256,768]{2,1,0:T(8,128)(2,1)S(1)} %constant_dynamic-update-slice_fusion.2.refs_5_), channel_id=1, source_target_pairs={{0,4},{4,8},{8,12},{12,0},{1,5},{5,9},{9,13},{13,1},{2,6},{6,10},{... | collective-permute-start | bytes 2359304 | tf_op jit(solution)/shard_map/ppermute | solution.py:26
  93.8 20.5 %collective-permute-start.9 = (bf16[2,256,768]{2,1,0:T(8,128)(2,1)S(1)}, bf16[2,256,768]{2,1,0:T(8,128)(2,1)}, u32[]{:S(2)}, u32[]{:S(2)}) collective-permute-start(bf16[2,256,768]{2,1,0:T(8,128)(2,1)S(1)} %constant_dynamic-update-slice_fusion.2.refs_5_), channel_id=1, source_target_pairs={{0,12},{4,0},{8,4},{12,8},{1,13},{5,1},{9,5},{13,9},{2,14},{6,2},{... | collective-permute-start | bytes 2359304 | tf_op jit(solution)/shard_map/ppermute | solution.py:26
  116.0 37.8 %all-to-all-start.3 = ((bf16[4,4,320,256]{3,2,1,0:T(8,128)(2,1)}), bf16[4,4,320,256]{3,2,1,0:T(8,128)(2,1)S(1)}, u32[]{:S(2)}, u32[]{:S(2)}) async-start(bf16[4,4,320,256]{3,2,1,0:T(8,128)(2,1)} %broadcast_in_dim.17), calls=%async_computation.3 | async-start | bytes 5242880 | tf_op jit(solution)/shard_map/all_to_all | solution.py:47
  120.3 7.2 %collective-permute-start.14 = (f32[64,688]{1,0:T(8,128)S(1)}, f32[64,688]{1,0:T(8,128)S(1)}, u32[]{:S(2)}, u32[]{:S(2)}) collective-permute-start(f32[64,688]{1,0:T(8,128)S(1)} %add.42), channel_id=1, source_target_pairs={{0,64},{32,96},{64,0},{96,32},{1,65},{33,97},{65,1},{97,33},{2,66}... | collective-permute-start | bytes 528392 | tf_op jit(solution)/shard_map/ppermute | solution.py:217
  128.5 8.1 %collective-permute-start.15 = (bf16[1,128,768]{2,1,0:T(8,128)(2,1)S(1)}, bf16[1,128,768]{2,1,0:T(8,128)(2,1)S(1)}, u32[]{:S(2)}, u32[]{:S(2)}) collective-permute-start(bf16[1,128,768]{2,1,0:T(8,128)(2,1)S(1)} %slice.59), channel_id=1, source_target_pairs={{0,1},{1,2},{2,3},{3,0},{4,5},{5,6},{6,7},{7,4},{8,9},{9,10},{10,1... | collective-permute-start | bytes 589832 | tf_op jit(solution)/shard_map/ppermute | solution.py:26
  132.3 32.1 %copy-start.14 = (s32[16]{0:T(128)S(1)}, s32[16]{0:T(128)}, u32[]{:S(2)}) copy-start(s32[16]{0:T(128)} %constant.66) | copy-start | bytes 196
  132.3 9.1 %collective-permute-start.16 = (bf16[1,128,768]{2,1,0:T(8,128)(2,1)S(1)}, bf16[1,128,768]{2,1,0:T(8,128)(2,1)S(1)}, u32[]{:S(2)}, u32[]{:S(2)}) collective-permute-start(bf16[1,128,768]{2,1,0:T(8,128)(2,1)S(1)} %slice.60), channel_id=1, source_target_pairs={{0,3},{1,0},{2,1},{3,2},{4,7},{5,4},{6,5},{7,6},{8,11},{9,8},{10,9... | collective-permute-start | bytes 589832 | tf_op jit(solution)/shard_map/ppermute | solution.py:26
  142.1 17.4 %collective-permute-start.17 = (bf16[1,256,768]{2,1,0:T(8,128)(2,1)}, bf16[1,256,768]{2,1,0:T(8,128)(2,1)S(1)}, u32[]{:S(2)}, u32[]{:S(2)}) collective-permute-start(bf16[1,256,768]{2,1,0:T(8,128)(2,1)} %constant_dynamic-update-slice_fusion.4.refs_10_), channel_id=1, source_target_pairs={{0,4},{4,8},{8,12},{12,0},{1,5},{5,9},{9,13},{13,1},{2,6},{6,10},{... | collective-permute-start | bytes 1179656 | tf_op jit(solution)/shard_map/ppermute | solution.py:26
  144.4 15.5 %collective-permute-start.19 = (bf16[1,256,768]{2,1,0:T(8,128)(2,1)}, bf16[1,256,768]{2,1,0:T(8,128)(2,1)}, u32[]{:S(2)}, u32[]{:S(2)}) collective-permute-start(bf16[1,256,768]{2,1,0:T(8,128)(2,1)} %constant_dynamic-update-slice_fusion.4.refs_10_), channel_id=1, source_target_pairs={{0,12},{4,0},{8,4},{12,8},{1,13},{5,1},{9,5},{13,9},{2,14},{6,2},{... | collective-permute-start | bytes 1179656 | tf_op jit(solution)/shard_map/ppermute | solution.py:26
  154.6 21.6 %collective-permute-start.22 = (bf16[16,64,256]{2,1,0:T(8,128)(2,1)}, bf16[16,64,256]{2,1,0:T(8,128)(2,1)}, u32[]{:S(2)}, u32[]{:S(2)}) collective-permute-start(bf16[16,64,256]{2,1,0:T(8,128)(2,1)} %slice.74), channel_id=1, source_target_pairs={{0,16},{16,0},{1,17},{17,1},{2,18},{18,2},{3,19},{19,3},{4,20},{20... | collective-permute-start | bytes 1572872 | tf_op jit(solution)/shard_map/ppermute | solution.py:26
  154.6 6.7 %collective-permute-start.21 = (bf16[64,688]{1,0:T(8,128)(2,1)S(1)}, bf16[64,688]{1,0:T(8,128)(2,1)}, u32[]{:S(2)}, u32[]{:S(2)}) collective-permute-start(bf16[64,688]{1,0:T(8,128)(2,1)S(1)} %add_convert_fusion), channel_id=1, source_target_pairs={{0,16},{16,0},{1,17},{17,1},{2,18},{18,2},{3,19},{19,3},{4,20},{20... | collective-permute-start | bytes 264200 | tf_op jit(solution)/shard_map/ppermute | solution.py:26
  157.0 19.2 %collective-permute-start.10 = (bf16[2,128,768]{2,1,0:T(8,128)(2,1)}, bf16[2,128,768]{2,1,0:T(8,128)(2,1)}, u32[]{:S(2)}, u32[]{:S(2)}) collective-permute-start(bf16[2,128,768]{2,1,0:T(8,128)(2,1)} %slice.69), channel_id=1, source_target_pairs={{0,12},{4,0},{8,4},{12,8},{1,13},{5,1},{9,5},{13,9},{2,14},{6,2},{... | collective-permute-start | bytes 1179656 | tf_op jit(solution)/shard_map/ppermute | solution.py:26
  159.5 16.7 %collective-permute-start.8 = (bf16[2,128,768]{2,1,0:T(8,128)(2,1)}, bf16[2,128,768]{2,1,0:T(8,128)(2,1)}, u32[]{:S(2)}, u32[]{:S(2)}) collective-permute-start(bf16[2,128,768]{2,1,0:T(8,128)(2,1)} %slice.68), channel_id=1, source_target_pairs={{0,4},{4,8},{8,12},{12,0},{1,5},{5,9},{9,13},{13,1},{2,6},{6,10},{... | collective-permute-start | bytes 1179656 | tf_op jit(solution)/shard_map/ppermute | solution.py:26
  159.8 16.4 %collective-permute-start.18 = (bf16[1,128,768]{2,1,0:T(8,128)(2,1)S(1)}, bf16[1,128,768]{2,1,0:T(8,128)(2,1)S(1)}, u32[]{:S(2)}, u32[]{:S(2)}) collective-permute-start(bf16[1,128,768]{2,1,0:T(8,128)(2,1)S(1)} %slice.72), channel_id=1, source_target_pairs={{0,4},{4,8},{8,12},{12,0},{1,5},{5,9},{9,13},{13,1},{2,6},{6,10},{... | collective-permute-start | bytes 589832 | tf_op jit(solution)/shard_map/ppermute | solution.py:26
  161.4 14.8 %collective-permute-start.20 = (bf16[1,128,768]{2,1,0:T(8,128)(2,1)S(1)}, bf16[1,128,768]{2,1,0:T(8,128)(2,1)}, u32[]{:S(2)}, u32[]{:S(2)}) collective-permute-start(bf16[1,128,768]{2,1,0:T(8,128)(2,1)S(1)} %slice.73), channel_id=1, source_target_pairs={{0,12},{4,0},{8,4},{12,8},{1,13},{5,1},{9,5},{13,9},{2,14},{6,2},{... | collective-permute-start | bytes 589832 | tf_op jit(solution)/shard_map/ppermute | solution.py:26
  (15 other events, 174.3 us)
Sparse Core Ops, SparseCore 0:
  16.3 31.8 all-gather.5
  50.0 54.8 all-gather.7
  114.4 52.6 all-gather.9

commit v4 on v3

--- a/solution.py
+++ b/solution.py
@@ -12,7 +12,7 @@
 VMEM_LIMIT = 16 << 20
 SCORE_LIMIT = 54 << 20
 GROUPS = ((0,), (1, 3), (2,))
-PIECES = 15
+PIECES = 20
 damping = 0.01
 AXES = ("zlo", "x", "core", "y", "zhi")
 SIZES = (2, 4, 2, 4, 4)
@@ -98,7 +98,7 @@
 
 def score_kernel(order, columns, live, *refs):
     lhs, rest = refs[:PIECES], refs[PIECES:]
-    right, rows, left, eig_hbm, near, far, out, met, acc, eig, held, lhs_sems, eig_sems, sems = rest
+    right, left, eig_hbm, near, far, out, met, rows, acc, eig, held, lhs_sems, eig_sems, sems = rest
     slots = held.shape[0]
     ahead, width = eig.shape[0], eig.shape[2]
 
@@ -111,16 +111,18 @@
     for number in range(ahead - 1):
         bring(number).start()
     half = near.shape[0]
-    moves, first = [], 0
-    for base, count in ((0, 1), (5, 2), (10, 1)):
-        cut = lhs[base + 2].shape[1]
-        for piece, row in ((base, 0), (base + 1, 0), (base + 4, 0), (base + 2, 0), (base + 3, cut)):
-            target = met.at[pl.ds(first, count), pl.ds(row, lhs[piece].shape[1])]
-            moves.append((first, pltpu.make_async_copy(lhs[piece], target, lhs_sems.at[piece])))
-            if piece != base + 2:
-                first += count
-    for _, move in moves:
-        move.start()
+    moves = {}
+    for held_in, bases in ((met, ((0, 1), (5, 2), (10, 1))), (rows, ((15, 4),))):
+        first = 0
+        for base, count in bases:
+            cut = lhs[base + 2].shape[1]
+            for piece, row in ((base, 0), (base + 1, 0), (base + 4, 0), (base + 2, 0), (base + 3, cut)):
+                target = held_in.at[pl.ds(first, count), pl.ds(row, lhs[piece].shape[1])]
+                move = pltpu.make_async_copy(lhs[piece], target, lhs_sems.at[piece])
+                moves.setdefault((held_in is met, first), []).append(move)
+                move.start()
+                if piece != base + 2:
+                    first += count
 
     def fetch(number, act):
         slot = number % slots
@@ -140,9 +142,8 @@
         if number + slots - 1 < met.shape[0]:
             fetch(number + slots - 1, lambda copy: copy.start())
         fetch(number, lambda copy: copy.wait())
-        for first, move in moves:
-            if first == number:
-                move.wait()
+        for move in moves.get((True, number), ()):
+            move.wait()
         term = jnp.dot(
             met[number, :, :depth], held[number % slots], preferred_element_type=jnp.float32
         )
@@ -157,6 +158,8 @@
     for i in range(rows.shape[0]):
         if i + ahead - 1 < rows.shape[0]:
             bring(i + ahead - 1).start()
+        for move in moves.get((False, i), ()):
+            move.wait()
         grad = jnp.dot(out_t, rows[i, :seq], preferred_element_type=jnp.float32)
         bring(i).wait()
         scaled = (grad / (eig[i % ahead] + damping)).astype(jnp.bfloat16)
@@ -166,17 +169,18 @@
     out[...] = total
 
 
-def score(order, columns, live, lhs, near, far, right, rows, eig_t, left):
+def score(order, columns, live, lhs, rows, near, far, right, eig_t, left):
     (height, padded), cols = lhs[0].shape[1:], near.shape[2]
-    factors, width = right.shape[0], rows.shape[2]
+    factors, width = right.shape[0], rows[0].shape[2]
     vmem, smem = pl.BlockSpec(memory_space=pltpu.VMEM), pl.BlockSpec(memory_space=pltpu.SMEM)
     hbm = pl.BlockSpec(memory_space=pltpu.HBM)
     return pl.pallas_call(
         score_kernel,
-        in_specs=[smem] * 3 + [hbm] * PIECES + [vmem] * 3 + [hbm] * 3,
+        in_specs=[smem] * 3 + [hbm] * PIECES + [vmem] * 2 + [hbm] * 3,
         out_specs=vmem,
         scratch_shapes=[
             pltpu.VMEM((16, height, padded), jnp.bfloat16),
+            pltpu.VMEM((16,) + rows[0].shape[1:], jnp.bfloat16),
             pltpu.VMEM((height, cols), jnp.float32),
             pltpu.VMEM((4, cols, width), jnp.float32),
             pltpu.VMEM((4,) + near.shape[1:], jnp.bfloat16),
@@ -186,7 +190,7 @@
         ],
         out_shape=jax.ShapeDtypeStruct((factors, width), jnp.float32),
         compiler_params=pltpu.CompilerParams(vmem_limit_bytes=SCORE_LIMIT),
-    )(order, columns, live, *lhs, right, rows, left, eig_t, near, far)
+    )(order, columns, live, *lhs, *rows, right, left, eig_t, near, far)
 
 
 def local(
@@ -238,13 +242,18 @@
     z_2 = jnp.concatenate(opposite(after(z_1, right_own), after(z_3, right_own), "zhi"), axis=-2)
     far = lax.all_gather(after(v_far, in_z, pair_1, pair_3), ("x", "core"), axis=0, tiled=False)
 
-    in_all = everyone(after(in_z, pair_1, pair_3), "y", 4)
-    in_all = in_all.reshape(feats, SEQ_LEN + factors // 2, width)
+    in_1, in_3 = sides(in_z, "y")
     pair_2 = opposite(pair_1, pair_3, "y")
+    in_2 = opposite(after(in_1, *pair_2), after(in_3, *pair_2), "y")
     far_1, far_3 = sides(z_2, "y")
     far_2 = opposite(far_1, far_3, "y")
 
-    left_other = shift(in_all[:, SEQ_LEN:], "core", 1)
+    in_pieces = (in_z, in_1, *in_2, in_3)
+    in_cut = in_2[0].shape[1]
+    left_own = [in_z[:, SEQ_LEN:], in_1[:, SEQ_LEN:], in_3[:, SEQ_LEN:], in_2[1][:, SEQ_LEN - in_cut :]]
+    left_other = shift(jnp.concatenate(left_own, axis=0), "core", 1)
+    in_y = jnp.repeat(jnp.array((0, 1, 3, 2), jnp.int32), 4)
+    columns = lax.rem(y - in_y + 4, 4) * 4 + lax.rem(block, 4)
 
     pieces = (own, own_1, *own_2, own_3, pair, pair_1, *pair_2, pair_3, z_2, far_1, *far_2, far_3)
     steps = [(k, z) for group in GROUPS for k in (0, 1, 3, 2) for z in group]
@@ -255,7 +264,7 @@
     right_here = jnp.concatenate([right_own, shift(right_own, "core", 1)], axis=0)
     eig_t = jnp.transpose(eigenvalues)
     total = score(
-        numbers, block, lengths, pieces, near, far, right_here, in_all, eig_t, left_other
+        numbers, columns, lengths, pieces, in_pieces, near, far, right_here, eig_t, left_other
     )
     sums = jnp.sum(total, axis=1)
     sums = jnp.where(core == 0, sums, jnp.concatenate([sums[half:], sums[:half]]))

time: 225 us -> 221 us (0.982)
  starting transfers between devices: 60.8 us -> 66.9 us
  waiting for transfers between devices: 76.9 us -> 71.4 us
  local copies, waits for them, and re-layouts: 23.2 us -> 19 us
    ppermute x22 -> x26, starting transfers between devices: 34.1 us -> 44.6 us  [shift(): lax.ppermute(block, axis, [(i, (i + step) % size) for i in range(size)])]
    all_to_all x4 -> x3, waiting for transfers between devices: 8.86 us -> 0.43 us  [everyone(): lax.all_to_all(jnp.broadcast_to(block[None], (size,) + block.shape), axes...]
    ppermute x22 -> x26, waiting for transfers between devices: 57.6 us -> 63.8 us  [shift(): lax.ppermute(block, axis, [(i, (i + step) % size) for i in range(size)])]
    all_to_all x4 -> x3, starting transfers between devices: 24.7 us -> 20.3 us  [everyone(): lax.all_to_all(jnp.broadcast_to(block[None], (size,) + block.shape), axes...]
    ppermute x1, waiting for transfers between devices: 6.54 us -> 3.16 us  [local(): lax.ppermute(right_x, 'x', [(i, i ^ 2) for i in range(4)])]
    broadcast_in_dim x4 -> x3, local copies, waits for them, and re-layouts: 5.04 us -> 3.29 us  [everyone(): jnp.broadcast_to(block[None], (size,) + block.shape)]
    slice x4 -> x5, local copies, waits for them, and re-layouts: 4.68 us -> 3.78 us  [opposite(): three[..., cut:, :]]
    unnamed x36 -> x54, local copies, waits for them, and re-layouts: 6.32 us -> 6.41 us
  transfers between devices with their start and end apart: 31 -> 34, of which waited for: 13 -> 13; matrix products, arithmetic and copies ran while one was open for 9% -> 8% of each run, Pallas kernels for 2% -> 2%
where the time goes in v4:
time: 221 us; the launch traced here: 220 us
  waiting for transfers between devices  71.4 us (32%)
  starting transfers between devices  66.9 us (30%)
  Pallas kernels  27.2 us (12%)
  local copies, waits for them, and re-layouts  19 us (9%)
  blocking collectives  14.5 us (7%)
  between operations  14.2 us (6%)
  other arithmetic  6.48 us (3%)
    ppermute x26, waiting for transfers between devices, shift(): lax.ppermute(block, axis, [(i, (i + step) % size) for i in range(size)])  63.8 us
    ppermute x26, starting transfers between devices, shift(): lax.ppermute(block, axis, [(i, (i + step) % size) for i in range(size)])  44.6 us
    pallas_call x1, Pallas kernels, score(): pl.pallas_call(score_kernel, in_specs=[smem] * 3 + [hbm] * PIECES + [vmem...  22.9 us
    all_to_all x3, starting transfers between devices, everyone(): lax.all_to_all(jnp.broadcast_to(block[None], (size,) + block.shape), axes...  20.3 us
    all_to_all x1, blocking collectives, local(): pieces = lax.all_to_all(partial.reshape(feats, 1, 1), FEAT, 0, 0)  14.5 us
    unnamed x54, local copies, waits for them, and re-layouts  6.41 us
  transfers between devices with their start and end apart: 34, of which 13 were waited for; matrix products, arithmetic and copies ran while one was open for 8% of the time, Pallas kernels for 2%

profile of v4, /device:TPU:4, one launch (start us, length us, event | category | flops | bytes accessed | tf_op | source)
XLA Modules:
  0.0 220.1 jit_solution(15755140761436434459)
XLA Ops:
  8.5 2.0 collective-permute-start.4
  10.5 4.9 %collective-permute-done.4 = bf16[256,384]{1,0:T(8,128)(2,1)S(1)} collective-permute-done((bf16[256,384]{1,0:T(8,128)(2,1)S(1)}, bf16[256,384]{1,0:T(8,128)(2,1)S(1)}, u32[]{:S(2)}, u32[]{:S(2)}) %collective-permute-start.4) | collective-permute-done | bytes 196640 | tf_op jit(solution)/shard_map/ppermute | solution.py:26
  17.8 8.3 %all-to-all-start = ((bf16[4,256,256]{2,1,0:T(8,128)(2,1)}), bf16[4,256,256]{2,1,0:T(8,128)(2,1)S(1)}, u32[]{:S(2)}, u32[]{:S(2)}) async-start(bf16[4,256,256]{2,1,0:T(8,128)(2,1)} %broadcast_in_dim.14), calls=%async_computation | async-start | bytes 1048576 | tf_op jit(solution)/shard_map/all_to_all | solution.py:47
  26.8 1.7 collective-permute-start
  28.5 1.7 collective-permute-start.2
  30.2 9.5 %collective-permute-done.refs_1_ = bf16[1,256,768]{2,1,0:T(8,128)(2,1)S(1)} collective-permute-done((bf16[1,256,768]{2,1,0:T(8,128)(2,1)S(1)}, bf16[1,256,768]{2,1,0:T(8,128)(2,1)S(1)}, u32[]{:S(2)}, u32[]{:S(2)}) %collective-permute-start) | collective-permute-done | bytes 393248 | tf_op jit(solution)/shard_map/ppermute | solution.py:26
  42.4 4.5 %all-to-all-start.1 = ((bf16[4,4,256,256]{3,2,1,0:T(8,128)(2,1)}), bf16[4,4,256,256]{3,2,1,0:T(8,128)(2,1)S(1)}, u32[]{:S(2)}, u32[]{:S(2)}) async-start(bf16[4,4,256,256]{3,2,1,0:T(8,128)(2,1)} %broadcast_in_dim.31), calls=%async_computation.1 | async-start | bytes 4194304 | tf_op jit(solution)/shard_map/all_to_all | solution.py:47
  46.9 2.0 collective-permute-start.12
  49.9 3.2 %collective-permute-start.6 = (bf16[1,256,768]{2,1,0:T(8,128)(2,1)}, bf16[1,256,768]{2,1,0:T(8,128)(2,1)}, u32[]{:S(2)}, u32[]{:S(2)}) collective-permute-start(bf16[1,256,768]{2,1,0:T(8,128)(2,1)} %copy-done.8), channel_id=1, source_target_pairs={{0,3},{1,0},{2,1},{3,2},{4,7},{5,4},{6,5},{7,6},{8,11},{9,8},{10,9... | collective-permute-start | bytes 1179656 | tf_op jit(solution)/shard_map/ppermute | solution.py:26
  53.1 9.5 %collective-permute-done.12 = f32[64,688]{1,0:T(8,128)} collective-permute-done((f32[64,688]{1,0:T(8,128)S(1)}, f32[64,688]{1,0:T(8,128)}, u32[]{:S(2)}, u32[]{:S(2)}) %collective-permute-start.12) | collective-permute-done | bytes 176160 | tf_op jit(solution)/shard_map/ppermute | solution.py:26
  65.8 2.0 collective-permute-start.1
  70.2 3.2 %collective-permute-done.13 = f32[64,688]{1,0:T(8,128)S(1)} collective-permute-done((f32[64,688]{1,0:T(8,128)S(1)}, f32[64,688]{1,0:T(8,128)S(1)}, u32[]{:S(2)}, u32[]{:S(2)}) %collective-permute-start.13) | collective-permute-done | bytes 176160 | tf_op jit(solution)/shard_map/ppermute | solution.py:220
  73.5 2.5 %collective-permute-start.27 = (bf16[688,688]{1,0:T(8,128)(2,1)S(1)}, bf16[688,688]{1,0:T(8,128)(2,1)}, u32[]{:S(2)}, u32[]{:S(2)}) collective-permute-start(bf16[688,688]{1,0:T(8,128)(2,1)S(1)} %copy-done.2), channel_id=1, source_target_pairs={{0,128},{128,0},{1,129},{129,1},{2,130},{130,2},{3,131},{131,3},{4... | collective-permute-start | bytes 2840072 | tf_op jit(solution)/shard_map/ppermute | solution.py:26
  76.8 1.9 copy-done.1
  78.7 4.4 %shard_map.109 = bf16[320,256]{1,0:T(8,128)(2,1)S(1)} custom-call(s32[17]{0:T(128)S(1)} %pad_add_fusion.order, bf16[16,256,256]{2,1,0:T(8,128)(2,1)S(1)} %bitcast.13, bf16[16,256,384]{2,1,0:T(8,128)(2,1)S(1)} %copy-done.1), custom_call_target="tpu_custom_call" | custom-call | tf_op jit(solution)/shard_map/pallas_call | solution.py:79
  83.9 7.6 %all-to-all-start.2 = ((bf16[4,320,256]{2,1,0:T(8,128)(2,1)}), bf16[4,320,256]{2,1,0:T(8,128)(2,1)S(1)}, u32[]{:S(2)}, u32[]{:S(2)}) async-start(bf16[4,320,256]{2,1,0:T(8,128)(2,1)} %broadcast_in_dim.32), calls=%async_computation.2 | async-start | bytes 1310720 | tf_op jit(solution)/shard_map/all_to_all | solution.py:47
  93.7 3.2 %collective-permute-start.9 = (bf16[2,256,768]{2,1,0:T(8,128)(2,1)S(1)}, bf16[2,256,768]{2,1,0:T(8,128)(2,1)}, u32[]{:S(2)}, u32[]{:S(2)}) collective-permute-start(bf16[2,256,768]{2,1,0:T(8,128)(2,1)S(1)} %constant_dynamic-update-slice_fusion.2.refs_5_), channel_id=1, source_target_pairs={{0,12},{4,0},{8,4},{12,8},{1,13},{5,1},{9,5},{13,9},{2,14},{6,2},{... | collective-permute-start | bytes 2359304 | tf_op jit(solution)/shard_map/ppermute | solution.py:26
  96.9 17.2 %collective-permute-done.7.refs_6_ = bf16[2,256,768]{2,1,0:T(8,128)(2,1)S(1)} collective-permute-done((bf16[2,256,768]{2,1,0:T(8,128)(2,1)S(1)}, bf16[2,256,768]{2,1,0:T(8,128)(2,1)S(1)}, u32[]{:S(2)}, u32[]{:S(2)}) %collective-permute-start.7) | collective-permute-done | bytes 786464 | tf_op jit(solution)/shard_map/ppermute | solution.py:26
  114.2 3.1 %collective-permute-start.23 = (bf16[4,320,256]{2,1,0:T(8,128)(2,1)S(1)}, bf16[4,320,256]{2,1,0:T(8,128)(2,1)S(1)}, u32[]{:S(2)}, u32[]{:S(2)}) collective-permute-start(bf16[4,320,256]{2,1,0:T(8,128)(2,1)S(1)} %all-to-all-done.2.refs_15_), channel_id=1, source_target_pairs={{0,12},{4,0},{8,4},{12,8},{1,13},{5,1},{9,5},{13,9},{2,14},{6,2},{... | collective-permute-start | bytes 1966088 | tf_op jit(solution)/shard_map/ppermute | solution.py:26
  119.4 1.8 collective-permute-start.8
  121.3 3.2 %collective-permute-done.14 = f32[64,688]{1,0:T(8,128)S(1)} collective-permute-done((f32[64,688]{1,0:T(8,128)S(1)}, f32[64,688]{1,0:T(8,128)S(1)}, u32[]{:S(2)}, u32[]{:S(2)}) %collective-permute-start.14) | collective-permute-done | bytes 176160 | tf_op jit(solution)/shard_map/ppermute | solution.py:221
  126.1 2.7 %collective-permute-start.15 = (bf16[1,128,768]{2,1,0:T(8,128)(2,1)S(1)}, bf16[1,128,768]{2,1,0:T(8,128)(2,1)S(1)}, u32[]{:S(2)}, u32[]{:S(2)}) collective-permute-start(bf16[1,128,768]{2,1,0:T(8,128)(2,1)S(1)} %slice.74), channel_id=1, source_target_pairs={{0,1},{1,2},{2,3},{3,0},{4,5},{5,6},{6,7},{7,4},{8,9},{9,10},{10,1... | collective-permute-start | bytes 589832 | tf_op jit(solution)/shard_map/ppermute | solution.py:26
  129.8 8.7 %collective-permute-done.10.refs_8_ = bf16[2,128,768]{2,1,0:T(8,128)(2,1)S(1)} collective-permute-done((bf16[2,128,768]{2,1,0:T(8,128)(2,1)S(1)}, bf16[2,128,768]{2,1,0:T(8,128)(2,1)S(1)}, u32[]{:S(2)}, u32[]{:S(2)}) %collective-permute-start.10) | collective-permute-done | bytes 393248 | tf_op jit(solution)/shard_map/ppermute | solution.py:26
  138.5 3.4 %collective-permute-start.16 = (bf16[1,128,768]{2,1,0:T(8,128)(2,1)S(1)}, bf16[1,128,768]{2,1,0:T(8,128)(2,1)S(1)}, u32[]{:S(2)}, u32[]{:S(2)}) collective-permute-start(bf16[1,128,768]{2,1,0:T(8,128)(2,1)S(1)} %slice.75), channel_id=1, source_target_pairs={{0,3},{1,0},{2,1},{3,2},{4,7},{5,4},{6,5},{7,6},{8,11},{9,8},{10,9... | collective-permute-start | bytes 589832 | tf_op jit(solution)/shard_map/ppermute | solution.py:26
  142.8 3.7 %collective-permute-start.24 = (bf16[4,160,256]{2,1,0:T(8,128)(2,1)}, bf16[4,160,256]{2,1,0:T(8,128)(2,1)}, u32[]{:S(2)}, u32[]{:S(2)}) collective-permute-start(bf16[4,160,256]{2,1,0:T(8,128)(2,1)} %slice.79), channel_id=1, source_target_pairs={{0,12},{4,0},{8,4},{12,8},{1,13},{5,1},{9,5},{13,9},{2,14},{6,2},{... | collective-permute-start | bytes 983048 | tf_op jit(solution)/shard_map/ppermute | solution.py:26
  146.6 3.9 %collective-permute-start.19 = (bf16[1,256,768]{2,1,0:T(8,128)(2,1)S(1)}, bf16[1,256,768]{2,1,0:T(8,128)(2,1)S(1)}, u32[]{:S(2)}, u32[]{:S(2)}) collective-permute-start(bf16[1,256,768]{2,1,0:T(8,128)(2,1)S(1)} %constant_dynamic-update-slice_fusion.4.refs_10_), channel_id=1, source_target_pairs={{0,12},{4,0},{8,4},{12,8},{1,13},{5,1},{9,5},{13,9},{2,14},{6,2},{... | collective-permute-start | bytes 1179656 | tf_op jit(solution)/shard_map/ppermute | solution.py:26
  150.6 4.1 %collective-permute-done.24.refs_18_ = bf16[4,160,256]{2,1,0:T(8,128)(2,1)} collective-permute-done((bf16[4,160,256]{2,1,0:T(8,128)(2,1)}, bf16[4,160,256]{2,1,0:T(8,128)(2,1)}, u32[]{:S(2)}, u32[]{:S(2)}) %collective-permute-start.24) | collective-permute-done | bytes 327712 | tf_op jit(solution)/shard_map/ppermute | solution.py:26
  157.3 2.4 %collective-permute-done.19.refs_14_ = bf16[1,256,768]{2,1,0:T(8,128)(2,1)S(1)} collective-permute-done((bf16[1,256,768]{2,1,0:T(8,128)(2,1)S(1)}, bf16[1,256,768]{2,1,0:T(8,128)(2,1)S(1)}, u32[]{:S(2)}, u32[]{:S(2)}) %collective-permute-start.19) | collective-permute-done | bytes 393248 | tf_op jit(solution)/shard_map/ppermute | solution.py:26
  159.7 3.8 %collective-permute-start.20 = (bf16[1,128,768]{2,1,0:T(8,128)(2,1)S(1)}, bf16[1,128,768]{2,1,0:T(8,128)(2,1)S(1)}, u32[]{:S(2)}, u32[]{:S(2)}) collective-permute-start(bf16[1,128,768]{2,1,0:T(8,128)(2,1)S(1)} %slice.93), channel_id=1, source_target_pairs={{0,12},{4,0},{8,4},{12,8},{1,13},{5,1},{9,5},{13,9},{2,14},{6,2},{... | collective-permute-start | bytes 589832 | tf_op jit(solution)/shard_map/ppermute | solution.py:26
  166.7 6.4 %collective-permute-done.22.refs_17_ = bf16[4,160,256]{2,1,0:T(8,128)(2,1)S(1)} collective-permute-done((bf16[4,160,256]{2,1,0:T(8,128)(2,1)S(1)}, bf16[4,160,256]{2,1,0:T(8,128)(2,1)S(1)}, u32[]{:S(2)}, u32[]{:S(2)}) %collective-permute-start.22) | collective-permute-done | bytes 327712 | tf_op jit(solution)/shard_map/ppermute | solution.py:26
  174.0 22.9 %shard_map.110 = f32[128,256]{1,0:T(8,128)} custom-call(s32[16]{0:T(128)} %get-tuple-element.31.order, s32[16]{0:T(128)} %get-tuple-element.32.columns, s32[1]{0:T(128)S(6)} %copy.26.live, bf16[1,256,768]{2,1,0:T(8,128)(2,1)} %copy-done.8, bf16[1,256,768]{2,1,0:T(8,128)(2,1)} %copy-done.9, bf16[1,128,768]{2,1,0:T(8,128)(2,1)} %copy-done.18, ...), custom_call_target="tpu_custom_call" | custom-call | tf_op jit(solution)/shard_map/pallas_call | solution.py:177
  198.4 14.5 %all_to_all.20 = f32[16,1,1]{2,1,0:T(1,128)S(1)} all-to-all(f32[16,1,1]{2,1,0:T(1,128)S(1)} %copy.21), channel_id=1, replica_groups=mesh['zlo'=2,'x'=4,'core'=2,'y'=4,'zhi'=4] {'y','zhi'}, dimensions={0} | all-to-all | bytes 128 | tf_op jit(solution)/shard_map/all_to_all | solution.py:273
  (140 shorter events, 32.2 us)
Async XLA Ops:
  6.5 70.2 %all-gather.6.cloned.1.call-start = ((), (), s32[]{:S(2)}) async-start(), calls=%async_computation.4 | async-start | bytes 3538944 | tf_op jit(solution)/shard_map/all_gather | solution.py:210
  16.2 156.9 %all-gather.8.cloned.1.call-start = ((), (), s32[]{:S(2)}) async-start(), calls=%async_computation.5 | async-start | bytes 9510912 | tf_op jit(solution)/shard_map/all_gather | solution.py:211
  17.8 23.1 %all-to-all-start = ((bf16[4,256,256]{2,1,0:T(8,128)(2,1)}), bf16[4,256,256]{2,1,0:T(8,128)(2,1)S(1)}, u32[]{:S(2)}, u32[]{:S(2)}) async-start(bf16[4,256,256]{2,1,0:T(8,128)(2,1)} %broadcast_in_dim.14), calls=%async_computation | async-start | bytes 1048576 | tf_op jit(solution)/shard_map/all_to_all | solution.py:47
  26.8 12.9 %collective-permute-start = (bf16[1,256,768]{2,1,0:T(8,128)(2,1)S(1)}, bf16[1,256,768]{2,1,0:T(8,128)(2,1)S(1)}, u32[]{:S(2)}, u32[]{:S(2)}) collective-permute-start(bf16[1,256,768]{2,1,0:T(8,128)(2,1)S(1)} %pad_bitcast_fusion.refs_0_), channel_id=1, source_target_pairs={{0,4},{4,8},{8,12},{12,0},{1,5},{5,9},{9,13},{13,1},{2,6},{6,10},{... | collective-permute-start | bytes 1179656 | tf_op jit(solution)/shard_map/ppermute | solution.py:26
  28.5 12.0 %collective-permute-start.2 = (bf16[1,256,768]{2,1,0:T(8,128)(2,1)S(1)}, bf16[1,256,768]{2,1,0:T(8,128)(2,1)}, u32[]{:S(2)}, u32[]{:S(2)}) collective-permute-start(bf16[1,256,768]{2,1,0:T(8,128)(2,1)S(1)} %pad_bitcast_fusion.refs_0_), channel_id=1, source_target_pairs={{0,12},{4,0},{8,4},{12,8},{1,13},{5,1},{9,5},{13,9},{2,14},{6,2},{... | collective-permute-start | bytes 1179656 | tf_op jit(solution)/shard_map/ppermute | solution.py:26
  42.4 34.3 %all-to-all-start.1 = ((bf16[4,4,256,256]{3,2,1,0:T(8,128)(2,1)}), bf16[4,4,256,256]{3,2,1,0:T(8,128)(2,1)S(1)}, u32[]{:S(2)}, u32[]{:S(2)}) async-start(bf16[4,4,256,256]{3,2,1,0:T(8,128)(2,1)} %broadcast_in_dim.31), calls=%async_computation.1 | async-start | bytes 4194304 | tf_op jit(solution)/shard_map/all_to_all | solution.py:47
  46.9 15.7 %collective-permute-start.12 = (f32[64,688]{1,0:T(8,128)S(1)}, f32[64,688]{1,0:T(8,128)}, u32[]{:S(2)}, u32[]{:S(2)}) collective-permute-start(f32[64,688]{1,0:T(8,128)S(1)} %select_add_fusion), channel_id=1, source_target_pairs={{0,128},{128,0},{1,129},{129,1},{2,130},{130,2},{3,131},{131,3},{4... | collective-permute-start | bytes 528392 | tf_op jit(solution)/shard_map/ppermute | solution.py:26
  48.9 24.5 %collective-permute-start.5 = (bf16[1,256,768]{2,1,0:T(8,128)(2,1)}, bf16[1,256,768]{2,1,0:T(8,128)(2,1)}, u32[]{:S(2)}, u32[]{:S(2)}) collective-permute-start(bf16[1,256,768]{2,1,0:T(8,128)(2,1)} %copy-done.8), channel_id=1, source_target_pairs={{0,1},{1,2},{2,3},{3,0},{4,5},{5,6},{6,7},{7,4},{8,9},{9,10},{10,1... | collective-permute-start | bytes 1179656 | tf_op jit(solution)/shard_map/ppermute | solution.py:26
  49.9 23.6 %collective-permute-start.6 = (bf16[1,256,768]{2,1,0:T(8,128)(2,1)}, bf16[1,256,768]{2,1,0:T(8,128)(2,1)}, u32[]{:S(2)}, u32[]{:S(2)}) collective-permute-start(bf16[1,256,768]{2,1,0:T(8,128)(2,1)} %copy-done.8), channel_id=1, source_target_pairs={{0,3},{1,0},{2,1},{3,2},{4,7},{5,4},{6,5},{7,6},{8,11},{9,8},{10,9... | collective-permute-start | bytes 1179656 | tf_op jit(solution)/shard_map/ppermute | solution.py:26
  63.6 9.9 %collective-permute-start.13 = (f32[64,688]{1,0:T(8,128)S(1)}, f32[64,688]{1,0:T(8,128)S(1)}, u32[]{:S(2)}, u32[]{:S(2)}) collective-permute-start(f32[64,688]{1,0:T(8,128)S(1)} %add.54), channel_id=1, source_target_pairs={{0,32},{32,0},{64,96},{96,64},{1,33},{33,1},{65,97},{97,65},{2,34}... | collective-permute-start | bytes 528392 | tf_op jit(solution)/shard_map/ppermute | solution.py:220
  65.8 10.3 %collective-permute-start.1 = (bf16[1,128,768]{2,1,0:T(8,128)(2,1)S(1)}, bf16[1,128,768]{2,1,0:T(8,128)(2,1)S(1)}, u32[]{:S(2)}, u32[]{:S(2)}) collective-permute-start(bf16[1,128,768]{2,1,0:T(8,128)(2,1)S(1)} %slice.86), channel_id=1, source_target_pairs={{0,4},{4,8},{8,12},{12,0},{1,5},{5,9},{9,13},{13,1},{2,6},{6,10},{... | collective-permute-start | bytes 589832 | tf_op jit(solution)/shard_map/ppermute | solution.py:26
  68.7 8.1 %collective-permute-start.3 = (bf16[1,128,768]{2,1,0:T(8,128)(2,1)S(1)}, bf16[1,128,768]{2,1,0:T(8,128)(2,1)}, u32[]{:S(2)}, u32[]{:S(2)}) collective-permute-start(bf16[1,128,768]{2,1,0:T(8,128)(2,1)S(1)} %slice.87), channel_id=1, source_target_pairs={{0,12},{4,0},{8,4},{12,8},{1,13},{5,1},{9,5},{13,9},{2,14},{6,2},{... | collective-permute-start | bytes 589832 | tf_op jit(solution)/shard_map/ppermute | solution.py:26
  73.5 40.7 %collective-permute-start.27 = (bf16[688,688]{1,0:T(8,128)(2,1)S(1)}, bf16[688,688]{1,0:T(8,128)(2,1)}, u32[]{:S(2)}, u32[]{:S(2)}) collective-permute-start(bf16[688,688]{1,0:T(8,128)(2,1)S(1)} %copy-done.2), channel_id=1, source_target_pairs={{0,128},{128,0},{1,129},{129,1},{2,130},{130,2},{3,131},{131,3},{4... | collective-permute-start | bytes 2840072 | tf_op jit(solution)/shard_map/ppermute | solution.py:26
  83.9 30.2 %all-to-all-start.2 = ((bf16[4,320,256]{2,1,0:T(8,128)(2,1)}), bf16[4,320,256]{2,1,0:T(8,128)(2,1)S(1)}, u32[]{:S(2)}, u32[]{:S(2)}) async-start(bf16[4,320,256]{2,1,0:T(8,128)(2,1)} %broadcast_in_dim.32), calls=%async_computation.2 | async-start | bytes 1310720 | tf_op jit(solution)/shard_map/all_to_all | solution.py:47
  91.5 81.6 %all-gather.10.cloned.1.call-start = ((), (), s32[]{:S(2)}) async-start(), calls=%async_computation.6 | async-start | bytes 9510912 | tf_op jit(solution)/shard_map/all_gather | solution.py:243
  93.6 20.5 %collective-permute-start.7 = (bf16[2,256,768]{2,1,0:T(8,128)(2,1)S(1)}, bf16[2,256,768]{2,1,0:T(8,128)(2,1)S(1)}, u32[]{:S(2)}, u32[]{:S(2)}) collective-permute-start(bf16[2,256,768]{2,1,0:T(8,128)(2,1)S(1)} %constant_dynamic-update-slice_fusion.2.refs_5_), channel_id=1, source_target_pairs={{0,4},{4,8},{8,12},{12,0},{1,5},{5,9},{9,13},{13,1},{2,6},{6,10},{... | collective-permute-start | bytes 2359304 | tf_op jit(solution)/shard_map/ppermute | solution.py:26
  93.7 20.4 %collective-permute-start.9 = (bf16[2,256,768]{2,1,0:T(8,128)(2,1)S(1)}, bf16[2,256,768]{2,1,0:T(8,128)(2,1)}, u32[]{:S(2)}, u32[]{:S(2)}) collective-permute-start(bf16[2,256,768]{2,1,0:T(8,128)(2,1)S(1)} %constant_dynamic-update-slice_fusion.2.refs_5_), channel_id=1, source_target_pairs={{0,12},{4,0},{8,4},{12,8},{1,13},{5,1},{9,5},{13,9},{2,14},{6,2},{... | collective-permute-start | bytes 2359304 | tf_op jit(solution)/shard_map/ppermute | solution.py:26
  114.2 27.7 %collective-permute-start.23 = (bf16[4,320,256]{2,1,0:T(8,128)(2,1)S(1)}, bf16[4,320,256]{2,1,0:T(8,128)(2,1)S(1)}, u32[]{:S(2)}, u32[]{:S(2)}) collective-permute-start(bf16[4,320,256]{2,1,0:T(8,128)(2,1)S(1)} %all-to-all-done.2.refs_15_), channel_id=1, source_target_pairs={{0,12},{4,0},{8,4},{12,8},{1,13},{5,1},{9,5},{13,9},{2,14},{6,2},{... | collective-permute-start | bytes 1966088 | tf_op jit(solution)/shard_map/ppermute | solution.py:26
  117.3 7.2 %collective-permute-start.14 = (f32[64,688]{1,0:T(8,128)S(1)}, f32[64,688]{1,0:T(8,128)S(1)}, u32[]{:S(2)}, u32[]{:S(2)}) collective-permute-start(f32[64,688]{1,0:T(8,128)S(1)} %add.55), channel_id=1, source_target_pairs={{0,64},{32,96},{64,0},{96,32},{1,65},{33,97},{65,1},{97,33},{2,66}... | collective-permute-start | bytes 528392 | tf_op jit(solution)/shard_map/ppermute | solution.py:221
  119.0 19.5 %collective-permute-start.10 = (bf16[2,128,768]{2,1,0:T(8,128)(2,1)S(1)}, bf16[2,128,768]{2,1,0:T(8,128)(2,1)S(1)}, u32[]{:S(2)}, u32[]{:S(2)}) collective-permute-start(bf16[2,128,768]{2,1,0:T(8,128)(2,1)S(1)} %slice.89), channel_id=1, source_target_pairs={{0,12},{4,0},{8,4},{12,8},{1,13},{5,1},{9,5},{13,9},{2,14},{6,2},{... | collective-permute-start | bytes 1179656 | tf_op jit(solution)/shard_map/ppermute | solution.py:26
  119.4 22.5 %collective-permute-start.8 = (bf16[2,128,768]{2,1,0:T(8,128)(2,1)S(1)}, bf16[2,128,768]{2,1,0:T(8,128)(2,1)}, u32[]{:S(2)}, u32[]{:S(2)}) collective-permute-start(bf16[2,128,768]{2,1,0:T(8,128)(2,1)S(1)} %slice.88), channel_id=1, source_target_pairs={{0,4},{4,8},{8,12},{12,0},{1,5},{5,9},{9,13},{13,1},{2,6},{6,10},{... | collective-permute-start | bytes 1179656 | tf_op jit(solution)/shard_map/ppermute | solution.py:26
  121.2 29.3 %collective-permute-start.21 = (bf16[4,320,256]{2,1,0:T(8,128)(2,1)S(1)}, bf16[4,320,256]{2,1,0:T(8,128)(2,1)S(1)}, u32[]{:S(2)}, u32[]{:S(2)}) collective-permute-start(bf16[4,320,256]{2,1,0:T(8,128)(2,1)S(1)} %all-to-all-done.2.refs_15_), channel_id=1, source_target_pairs={{0,4},{4,8},{8,12},{12,0},{1,5},{5,9},{9,13},{13,1},{2,6},{6,10},{... | collective-permute-start | bytes 1966088 | tf_op jit(solution)/shard_map/ppermute | solution.py:26
  126.1 20.3 %collective-permute-start.15 = (bf16[1,128,768]{2,1,0:T(8,128)(2,1)S(1)}, bf16[1,128,768]{2,1,0:T(8,128)(2,1)S(1)}, u32[]{:S(2)}, u32[]{:S(2)}) collective-permute-start(bf16[1,128,768]{2,1,0:T(8,128)(2,1)S(1)} %slice.74), channel_id=1, source_target_pairs={{0,1},{1,2},{2,3},{3,0},{4,5},{5,6},{6,7},{7,4},{8,9},{9,10},{10,1... | collective-permute-start | bytes 589832 | tf_op jit(solution)/shard_map/ppermute | solution.py:26
  138.5 8.0 %collective-permute-start.16 = (bf16[1,128,768]{2,1,0:T(8,128)(2,1)S(1)}, bf16[1,128,768]{2,1,0:T(8,128)(2,1)S(1)}, u32[]{:S(2)}, u32[]{:S(2)}) collective-permute-start(bf16[1,128,768]{2,1,0:T(8,128)(2,1)S(1)} %slice.75), channel_id=1, source_target_pairs={{0,3},{1,0},{2,1},{3,2},{4,7},{5,4},{6,5},{7,6},{8,11},{9,8},{10,9... | collective-permute-start | bytes 589832 | tf_op jit(solution)/shard_map/ppermute | solution.py:26
  142.8 11.9 %collective-permute-start.24 = (bf16[4,160,256]{2,1,0:T(8,128)(2,1)}, bf16[4,160,256]{2,1,0:T(8,128)(2,1)}, u32[]{:S(2)}, u32[]{:S(2)}) collective-permute-start(bf16[4,160,256]{2,1,0:T(8,128)(2,1)} %slice.79), channel_id=1, source_target_pairs={{0,12},{4,0},{8,4},{12,8},{1,13},{5,1},{9,5},{13,9},{2,14},{6,2},{... | collective-permute-start | bytes 983048 | tf_op jit(solution)/shard_map/ppermute | solution.py:26
  146.5 10.6 %collective-permute-start.17 = (bf16[1,256,768]{2,1,0:T(8,128)(2,1)S(1)}, bf16[1,256,768]{2,1,0:T(8,128)(2,1)S(1)}, u32[]{:S(2)}, u32[]{:S(2)}) collective-permute-start(bf16[1,256,768]{2,1,0:T(8,128)(2,1)S(1)} %constant_dynamic-update-slice_fusion.4.refs_10_), channel_id=1, source_target_pairs={{0,4},{4,8},{8,12},{12,0},{1,5},{5,9},{9,13},{13,1},{2,6},{6,10},{... | collective-permute-start | bytes 1179656 | tf_op jit(solution)/shard_map/ppermute | solution.py:26
  146.6 13.1 %collective-permute-start.19 = (bf16[1,256,768]{2,1,0:T(8,128)(2,1)S(1)}, bf16[1,256,768]{2,1,0:T(8,128)(2,1)S(1)}, u32[]{:S(2)}, u32[]{:S(2)}) collective-permute-start(bf16[1,256,768]{2,1,0:T(8,128)(2,1)S(1)} %constant_dynamic-update-slice_fusion.4.refs_10_), channel_id=1, source_target_pairs={{0,12},{4,0},{8,4},{12,8},{1,13},{5,1},{9,5},{13,9},{2,14},{6,2},{... | collective-permute-start | bytes 1179656 | tf_op jit(solution)/shard_map/ppermute | solution.py:26
  156.5 16.6 %collective-permute-start.26 = (bf16[16,64,256]{2,1,0:T(8,128)(2,1)}, bf16[16,64,256]{2,1,0:T(8,128)(2,1)S(1)}, u32[]{:S(2)}, u32[]{:S(2)}) collective-permute-start(bf16[16,64,256]{2,1,0:T(8,128)(2,1)} %pad_maximum_fusion), channel_id=1, source_target_pairs={{0,16},{16,0},{1,17},{17,1},{2,18},{18,2},{3,19},{19,3},{4,20},{20... | collective-permute-start | bytes 1572872 | tf_op jit(solution)/shard_map/ppermute | solution.py:26
  156.7 8.4 %collective-permute-start.25 = (bf16[64,688]{1,0:T(8,128)(2,1)S(1)}, bf16[64,688]{1,0:T(8,128)(2,1)S(1)}, u32[]{:S(2)}, u32[]{:S(2)}) collective-permute-start(bf16[64,688]{1,0:T(8,128)(2,1)S(1)} %copy-done.15), channel_id=1, source_target_pairs={{0,16},{16,0},{1,17},{17,1},{2,18},{18,2},{3,19},{19,3},{4,20},{20... | collective-permute-start | bytes 264200 | tf_op jit(solution)/shard_map/ppermute | solution.py:26
  157.2 9.5 %collective-permute-start.18 = (bf16[1,128,768]{2,1,0:T(8,128)(2,1)S(1)}, bf16[1,128,768]{2,1,0:T(8,128)(2,1)S(1)}, u32[]{:S(2)}, u32[]{:S(2)}) collective-permute-start(bf16[1,128,768]{2,1,0:T(8,128)(2,1)S(1)} %slice.92), channel_id=1, source_target_pairs={{0,4},{4,8},{8,12},{12,0},{1,5},{5,9},{9,13},{13,1},{2,6},{6,10},{... | collective-permute-start | bytes 589832 | tf_op jit(solution)/shard_map/ppermute | solution.py:26
  159.7 7.0 %collective-permute-start.20 = (bf16[1,128,768]{2,1,0:T(8,128)(2,1)S(1)}, bf16[1,128,768]{2,1,0:T(8,128)(2,1)S(1)}, u32[]{:S(2)}, u32[]{:S(2)}) collective-permute-start(bf16[1,128,768]{2,1,0:T(8,128)(2,1)S(1)} %slice.93), channel_id=1, source_target_pairs={{0,12},{4,0},{8,4},{12,8},{1,13},{5,1},{9,5},{13,9},{2,14},{6,2},{... | collective-permute-start | bytes 589832 | tf_op jit(solution)/shard_map/ppermute | solution.py:26
  163.5 9.6 %collective-permute-start.22 = (bf16[4,160,256]{2,1,0:T(8,128)(2,1)S(1)}, bf16[4,160,256]{2,1,0:T(8,128)(2,1)S(1)}, u32[]{:S(2)}, u32[]{:S(2)}) collective-permute-start(bf16[4,160,256]{2,1,0:T(8,128)(2,1)S(1)} %slice.78), channel_id=1, source_target_pairs={{0,4},{4,8},{8,12},{12,0},{1,5},{5,9},{9,13},{13,1},{2,6},{6,10},{... | collective-permute-start | bytes 983048 | tf_op jit(solution)/shard_map/ppermute | solution.py:26
  (27 other events, 371.2 us)
Sparse Core Ops, SparseCore 0:
  16.3 31.8 all-gather.5
  50.0 54.8 all-gather.7
  114.3 52.6 all-gather.9

commit v5 on v4

--- a/solution.py
+++ b/solution.py
@@ -218,8 +218,6 @@
     right_core = jnp.where(core == 0, low, high) + shift(jnp.where(core == 0, high, low), "core", 1)
     right_pair = right_core + shift(right_core, "zlo", 1)
     right_x = right_pair + lax.ppermute(right_pair, "x", [(i, i ^ 1) for i in range(4)])
-    right_sum = right_x + lax.ppermute(right_x, "x", [(i, i ^ 2) for i in range(4)])
-    right_own = right_sum.astype(bf16)
 
     act_z = everyone(after(activations, u_far), "zhi", 4)
     padding = -slab % 256
@@ -239,13 +237,15 @@
     pair_1, pair_3 = sides(pair, "y")
     v_far = shift(after(out_basis, z_1, z_3), "zlo", 1)
     in_z = everyone(after(in_rot, right_x), "zhi", 4)
-    z_2 = jnp.concatenate(opposite(after(z_1, right_own), after(z_3, right_own), "zhi"), axis=-2)
-    far = lax.all_gather(after(v_far, in_z, pair_1, pair_3), ("x", "core"), axis=0, tiled=False)
+    z_2 = shift(after(own, in_rot), "zhi", 2)
+    right_sum = right_x + lax.ppermute(after(right_x, in_rot), "x", [(i, i ^ 2) for i in range(4)])
+    right_own = right_sum.astype(bf16)
+    far = lax.all_gather(after(v_far, in_z, pair_1, pair_3, right_own), ("x", "core"), axis=0, tiled=False)
 
     in_1, in_3 = sides(in_z, "y")
     pair_2 = opposite(pair_1, pair_3, "y")
     in_2 = opposite(after(in_1, *pair_2), after(in_3, *pair_2), "y")
-    far_1, far_3 = sides(z_2, "y")
+    far_1, far_3 = sides(after(z_2, in_1, in_3), "y")
     far_2 = opposite(far_1, far_3, "y")
 
     in_pieces = (in_z, in_1, *in_2, in_3)

time: 221 us -> 221 us (level)
  blocking collectives: 14.5 us -> 17.7 us
    ppermute x26 -> x25, waiting for transfers between devices: 63.8 us -> 56.6 us  [shift(): lax.ppermute(block, axis, [(i, (i + step) % size) for i in range(size)])]
    ppermute x1, waiting for transfers between devices: 3.16 us -> 8.4 us  [local(): lax.ppermute(after(right_x, in_rot), 'x', [(i, i ^ 2) for i in range(4)])]
    all_to_all x1, blocking collectives: 14.5 us -> 17.7 us  [local(): pieces = lax.all_to_all(partial.reshape(feats, 1, 1), FEAT, 0, 0)]
    unnamed x54 -> x53, local copies, waits for them, and re-layouts: 6.41 us -> 7.72 us
    ppermute x26 -> x25, starting transfers between devices: 44.6 us -> 45.4 us  [shift(): lax.ppermute(block, axis, [(i, (i + step) % size) for i in range(size)])]
  transfers between devices with their start and end apart: 34 -> 33, of which waited for: 13 -> 13; matrix products, arithmetic and copies ran while one was open for 8% -> 6% of each run, Pallas kernels for 2% -> 2%
where the time goes in v5:
time: 221 us; the launch traced here: 220 us
  waiting for transfers between devices  69.3 us (31%)
  starting transfers between devices  67.7 us (31%)
  Pallas kernels  27.2 us (12%)
  blocking collectives  17.7 us (8%)
  local copies, waits for them, and re-layouts  17.4 us (8%)
  between operations  14.2 us (6%)
  other arithmetic  6.49 us (3%)
    ppermute x25, waiting for transfers between devices, shift(): lax.ppermute(block, axis, [(i, (i + step) % size) for i in range(size)])  56.6 us
    ppermute x25, starting transfers between devices, shift(): lax.ppermute(block, axis, [(i, (i + step) % size) for i in range(size)])  45.4 us
    pallas_call x1, Pallas kernels, score(): pl.pallas_call(score_kernel, in_specs=[smem] * 3 + [hbm] * PIECES + [vmem...  22.8 us
    all_to_all x3, starting transfers between devices, everyone(): lax.all_to_all(jnp.broadcast_to(block[None], (size,) + block.shape), axes...  20.3 us
    all_to_all x1, blocking collectives, local(): pieces = lax.all_to_all(partial.reshape(feats, 1, 1), FEAT, 0, 0)  17.7 us
    ppermute x1, waiting for transfers between devices, local(): lax.ppermute(after(right_x, in_rot), 'x', [(i, i ^ 2) for i in range(4)])  8.4 us
    unnamed x53, local copies, waits for them, and re-layouts  7.72 us
  transfers between devices with their start and end apart: 33, of which 13 were waited for; matrix products, arithmetic and copies ran while one was open for 6% of the time, Pallas kernels for 2%

profile of v5, /device:TPU:4, one launch (start us, length us, event | category | flops | bytes accessed | tf_op | source)
XLA Modules:
  0.0 220.4 jit_solution(17514410297819471766)
XLA Ops:
  8.5 2.0 collective-permute-start.4
  10.5 4.9 %collective-permute-done.4 = bf16[256,384]{1,0:T(8,128)(2,1)S(1)} collective-permute-done((bf16[256,384]{1,0:T(8,128)(2,1)S(1)}, bf16[256,384]{1,0:T(8,128)(2,1)S(1)}, u32[]{:S(2)}, u32[]{:S(2)}) %collective-permute-start.4) | collective-permute-done | bytes 196640 | tf_op jit(solution)/shard_map/ppermute | solution.py:26
  17.9 8.3 %all-to-all-start = ((bf16[4,256,256]{2,1,0:T(8,128)(2,1)}), bf16[4,256,256]{2,1,0:T(8,128)(2,1)S(1)}, u32[]{:S(2)}, u32[]{:S(2)}) async-start(bf16[4,256,256]{2,1,0:T(8,128)(2,1)} %broadcast_in_dim.14), calls=%async_computation | async-start | bytes 1048576 | tf_op jit(solution)/shard_map/all_to_all | solution.py:47
  26.9 1.7 collective-permute-start
  28.5 1.7 collective-permute-start.2
  30.2 9.5 %collective-permute-done.refs_1_ = bf16[1,256,768]{2,1,0:T(8,128)(2,1)S(1)} collective-permute-done((bf16[1,256,768]{2,1,0:T(8,128)(2,1)S(1)}, bf16[1,256,768]{2,1,0:T(8,128)(2,1)S(1)}, u32[]{:S(2)}, u32[]{:S(2)}) %collective-permute-start) | collective-permute-done | bytes 393248 | tf_op jit(solution)/shard_map/ppermute | solution.py:26
  42.5 4.5 %all-to-all-start.1 = ((bf16[4,4,256,256]{3,2,1,0:T(8,128)(2,1)}), bf16[4,4,256,256]{3,2,1,0:T(8,128)(2,1)S(1)}, u32[]{:S(2)}, u32[]{:S(2)}) async-start(bf16[4,4,256,256]{3,2,1,0:T(8,128)(2,1)} %broadcast_in_dim.31), calls=%async_computation.1 | async-start | bytes 4194304 | tf_op jit(solution)/shard_map/all_to_all | solution.py:47
  47.0 2.0 collective-permute-start.12
  49.9 3.2 %collective-permute-start.6 = (bf16[1,256,768]{2,1,0:T(8,128)(2,1)}, bf16[1,256,768]{2,1,0:T(8,128)(2,1)}, u32[]{:S(2)}, u32[]{:S(2)}) collective-permute-start(bf16[1,256,768]{2,1,0:T(8,128)(2,1)} %copy-done.8), channel_id=1, source_target_pairs={{0,3},{1,0},{2,1},{3,2},{4,7},{5,4},{6,5},{7,6},{8,11},{9,8},{10,9... | collective-permute-start | bytes 1179656 | tf_op jit(solution)/shard_map/ppermute | solution.py:26
  53.1 9.5 %collective-permute-done.12 = f32[64,688]{1,0:T(8,128)} collective-permute-done((f32[64,688]{1,0:T(8,128)S(1)}, f32[64,688]{1,0:T(8,128)}, u32[]{:S(2)}, u32[]{:S(2)}) %collective-permute-start.12) | collective-permute-done | bytes 176160 | tf_op jit(solution)/shard_map/ppermute | solution.py:26
  65.8 2.0 collective-permute-start.1
  70.3 3.2 %collective-permute-done.14 = f32[64,688]{1,0:T(8,128)S(1)} collective-permute-done((f32[64,688]{1,0:T(8,128)S(1)}, f32[64,688]{1,0:T(8,128)S(1)}, u32[]{:S(2)}, u32[]{:S(2)}) %collective-permute-start.14) | collective-permute-done | bytes 176160 | tf_op jit(solution)/shard_map/ppermute | solution.py:220
  73.5 2.5 %collective-permute-start.26 = (bf16[688,688]{1,0:T(8,128)(2,1)S(1)}, bf16[688,688]{1,0:T(8,128)(2,1)}, u32[]{:S(2)}, u32[]{:S(2)}) collective-permute-start(bf16[688,688]{1,0:T(8,128)(2,1)S(1)} %copy-done.2), channel_id=1, source_target_pairs={{0,128},{128,0},{1,129},{129,1},{2,130},{130,2},{3,131},{131,3},{4... | collective-permute-start | bytes 2840072 | tf_op jit(solution)/shard_map/ppermute | solution.py:26
  76.8 1.9 copy-done.1
  78.7 4.4 %shard_map.109 = bf16[320,256]{1,0:T(8,128)(2,1)S(1)} custom-call(s32[17]{0:T(128)S(1)} %pad_add_fusion.order, bf16[16,256,256]{2,1,0:T(8,128)(2,1)S(1)} %bitcast.13, bf16[16,256,384]{2,1,0:T(8,128)(2,1)S(1)} %copy-done.1), custom_call_target="tpu_custom_call" | custom-call | tf_op jit(solution)/shard_map/pallas_call | solution.py:79
  84.0 7.6 %all-to-all-start.2 = ((bf16[4,320,256]{2,1,0:T(8,128)(2,1)}), bf16[4,320,256]{2,1,0:T(8,128)(2,1)S(1)}, u32[]{:S(2)}, u32[]{:S(2)}) async-start(bf16[4,320,256]{2,1,0:T(8,128)(2,1)} %broadcast_in_dim.32), calls=%async_computation.2 | async-start | bytes 1310720 | tf_op jit(solution)/shard_map/all_to_all | solution.py:47
  93.7 3.2 %collective-permute-start.9 = (bf16[2,256,768]{2,1,0:T(8,128)(2,1)S(1)}, bf16[2,256,768]{2,1,0:T(8,128)(2,1)}, u32[]{:S(2)}, u32[]{:S(2)}) collective-permute-start(bf16[2,256,768]{2,1,0:T(8,128)(2,1)S(1)} %constant_dynamic-update-slice_fusion.2.refs_5_), channel_id=1, source_target_pairs={{0,12},{4,0},{8,4},{12,8},{1,13},{5,1},{9,5},{13,9},{2,14},{6,2},{... | collective-permute-start | bytes 2359304 | tf_op jit(solution)/shard_map/ppermute | solution.py:26
  97.6 8.4 %collective-permute-done.23 = f32[64,688]{1,0:T(8,128)S(1)} collective-permute-done((f32[64,688]{1,0:T(8,128)S(1)}, f32[64,688]{1,0:T(8,128)S(1)}, u32[]{:S(2)}, u32[]{:S(2)}) %collective-permute-start.23) | collective-permute-done | bytes 176160 | tf_op jit(solution)/shard_map/ppermute | solution.py:241
  106.6 7.4 %collective-permute-done.7.refs_6_ = bf16[2,256,768]{2,1,0:T(8,128)(2,1)S(1)} collective-permute-done((bf16[2,256,768]{2,1,0:T(8,128)(2,1)S(1)}, bf16[2,256,768]{2,1,0:T(8,128)(2,1)S(1)}, u32[]{:S(2)}, u32[]{:S(2)}) %collective-permute-start.7) | collective-permute-done | bytes 786464 | tf_op jit(solution)/shard_map/ppermute | solution.py:26
  114.1 3.3 %collective-permute-start.16 = (bf16[4,320,256]{2,1,0:T(8,128)(2,1)S(1)}, bf16[4,320,256]{2,1,0:T(8,128)(2,1)S(1)}, u32[]{:S(2)}, u32[]{:S(2)}) collective-permute-start(bf16[4,320,256]{2,1,0:T(8,128)(2,1)S(1)} %all-to-all-done.2.refs_15_), channel_id=1, source_target_pairs={{0,12},{4,0},{8,4},{12,8},{1,13},{5,1},{9,5},{13,9},{2,14},{6,2},{... | collective-permute-start | bytes 1966088 | tf_op jit(solution)/shard_map/ppermute | solution.py:26
  118.6 2.1 collective-permute-start.8
  120.8 5.7 %collective-permute-start.13 = (bf16[1,256,768]{2,1,0:T(8,128)(2,1)}, bf16[1,256,768]{2,1,0:T(8,128)(2,1)}, u32[]{:S(2)}, u32[]{:S(2)}) collective-permute-start(bf16[1,256,768]{2,1,0:T(8,128)(2,1)} %copy-done.8), channel_id=1, source_target_pairs={{0,2},{1,3},{2,0},{3,1},{4,6},{5,7},{6,4},{7,5},{8,10},{9,11},{10,... | collective-permute-start | bytes 1179656 | tf_op jit(solution)/shard_map/ppermute | solution.py:26
  126.5 12.0 %collective-permute-done.10.refs_8_ = bf16[2,128,768]{2,1,0:T(8,128)(2,1)S(1)} collective-permute-done((bf16[2,128,768]{2,1,0:T(8,128)(2,1)S(1)}, bf16[2,128,768]{2,1,0:T(8,128)(2,1)S(1)}, u32[]{:S(2)}, u32[]{:S(2)}) %collective-permute-start.10) | collective-permute-done | bytes 393248 | tf_op jit(solution)/shard_map/ppermute | solution.py:26
  140.1 3.7 %collective-permute-start.22 = (bf16[4,160,256]{2,1,0:T(8,128)(2,1)}, bf16[4,160,256]{2,1,0:T(8,128)(2,1)S(1)}, u32[]{:S(2)}, u32[]{:S(2)}) collective-permute-start(bf16[4,160,256]{2,1,0:T(8,128)(2,1)} %slice.71), channel_id=1, source_target_pairs={{0,12},{4,0},{8,4},{12,8},{1,13},{5,1},{9,5},{13,9},{2,14},{6,2},{... | collective-permute-start | bytes 983048 | tf_op jit(solution)/shard_map/ppermute | solution.py:26
  143.9 3.2 %collective-permute-start.19 = (bf16[1,256,768]{2,1,0:T(8,128)(2,1)}, bf16[1,256,768]{2,1,0:T(8,128)(2,1)S(1)}, u32[]{:S(2)}, u32[]{:S(2)}) collective-permute-start(bf16[1,256,768]{2,1,0:T(8,128)(2,1)} %collective-permute-done.13.refs_10_), channel_id=1, source_target_pairs={{0,12},{4,0},{8,4},{12,8},{1,13},{5,1},{9,5},{13,9},{2,14},{6,2},{... | collective-permute-start | bytes 1179656 | tf_op jit(solution)/shard_map/ppermute | solution.py:26
  147.1 5.1 %collective-permute-done.22.refs_18_ = bf16[4,160,256]{2,1,0:T(8,128)(2,1)S(1)} collective-permute-done((bf16[4,160,256]{2,1,0:T(8,128)(2,1)}, bf16[4,160,256]{2,1,0:T(8,128)(2,1)S(1)}, u32[]{:S(2)}, u32[]{:S(2)}) %collective-permute-start.22) | collective-permute-done | bytes 327712 | tf_op jit(solution)/shard_map/ppermute | solution.py:26
  154.0 1.8 collective-permute-start.18
  157.3 3.9 %collective-permute-start.20 = (bf16[1,128,768]{2,1,0:T(8,128)(2,1)S(1)}, bf16[1,128,768]{2,1,0:T(8,128)(2,1)S(1)}, u32[]{:S(2)}, u32[]{:S(2)}) collective-permute-start(bf16[1,128,768]{2,1,0:T(8,128)(2,1)S(1)} %slice.85), channel_id=1, source_target_pairs={{0,12},{4,0},{8,4},{12,8},{1,13},{5,1},{9,5},{13,9},{2,14},{6,2},{... | collective-permute-start | bytes 589832 | tf_op jit(solution)/shard_map/ppermute | solution.py:26
  163.1 2.9 %collective-permute-done.21.refs_17_ = bf16[4,160,256]{2,1,0:T(8,128)(2,1)S(1)} collective-permute-done((bf16[4,160,256]{2,1,0:T(8,128)(2,1)S(1)}, bf16[4,160,256]{2,1,0:T(8,128)(2,1)S(1)}, u32[]{:S(2)}, u32[]{:S(2)}) %collective-permute-start.21) | collective-permute-done | bytes 327712 | tf_op jit(solution)/shard_map/ppermute | solution.py:26
  166.1 3.6 %collective-permute-done.18.refs_12_ = bf16[1,128,768]{2,1,0:T(8,128)(2,1)S(1)} collective-permute-done((bf16[1,128,768]{2,1,0:T(8,128)(2,1)S(1)}, bf16[1,128,768]{2,1,0:T(8,128)(2,1)S(1)}, u32[]{:S(2)}, u32[]{:S(2)}) %collective-permute-start.18) | collective-permute-done | bytes 196640 | tf_op jit(solution)/shard_map/ppermute | solution.py:26
  171.2 22.8 %shard_map.110 = f32[128,256]{1,0:T(8,128)} custom-call(s32[16]{0:T(128)} %get-tuple-element.33.order, s32[16]{0:T(128)} %get-tuple-element.34.columns, s32[1]{0:T(128)S(6)} %copy.25.live, bf16[1,256,768]{2,1,0:T(8,128)(2,1)} %copy-done.8, bf16[1,256,768]{2,1,0:T(8,128)(2,1)} %copy-done.9, bf16[1,128,768]{2,1,0:T(8,128)(2,1)} %copy-done.18, ...), custom_call_target="tpu_custom_call" | custom-call | tf_op jit(solution)/shard_map/pallas_call | solution.py:177
  195.6 17.7 %all_to_all.20 = f32[16,1,1]{2,1,0:T(1,128)S(1)} all-to-all(f32[16,1,1]{2,1,0:T(1,128)S(1)} %copy.21), channel_id=1, replica_groups=mesh['zlo'=2,'x'=4,'core'=2,'y'=4,'zhi'=4] {'y','zhi'}, dimensions={0} | all-to-all | bytes 128 | tf_op jit(solution)/shard_map/all_to_all | solution.py:273
  (134 shorter events, 30.6 us)
Async XLA Ops:
  6.5 70.3 %all-gather.6.cloned.1.call-start = ((), (), s32[]{:S(2)}) async-start(), calls=%async_computation.4 | async-start | bytes 3538944 | tf_op jit(solution)/shard_map/all_gather | solution.py:210
  8.5 6.9 %collective-permute-start.4 = (bf16[256,384]{1,0:T(8,128)(2,1)S(1)}, bf16[256,384]{1,0:T(8,128)(2,1)S(1)}, u32[]{:S(2)}, u32[]{:S(2)}) collective-permute-start(bf16[256,384]{1,0:T(8,128)(2,1)S(1)} %constant_dynamic-update-slice_fusion), channel_id=1, source_target_pairs={{0,128},{128,0},{1,129},{129,1},{2,130},{130,2},{3,131},{131,3},{4... | collective-permute-start | bytes 589832 | tf_op jit(solution)/shard_map/ppermute | solution.py:26
  16.2 154.1 %all-gather.8.cloned.1.call-start = ((), (), s32[]{:S(2)}) async-start(), calls=%async_computation.5 | async-start | bytes 9510912 | tf_op jit(solution)/shard_map/all_gather | solution.py:211
  17.9 23.1 %all-to-all-start = ((bf16[4,256,256]{2,1,0:T(8,128)(2,1)}), bf16[4,256,256]{2,1,0:T(8,128)(2,1)S(1)}, u32[]{:S(2)}, u32[]{:S(2)}) async-start(bf16[4,256,256]{2,1,0:T(8,128)(2,1)} %broadcast_in_dim.14), calls=%async_computation | async-start | bytes 1048576 | tf_op jit(solution)/shard_map/all_to_all | solution.py:47
  26.9 12.9 %collective-permute-start = (bf16[1,256,768]{2,1,0:T(8,128)(2,1)S(1)}, bf16[1,256,768]{2,1,0:T(8,128)(2,1)S(1)}, u32[]{:S(2)}, u32[]{:S(2)}) collective-permute-start(bf16[1,256,768]{2,1,0:T(8,128)(2,1)S(1)} %pad_bitcast_fusion.refs_0_), channel_id=1, source_target_pairs={{0,4},{4,8},{8,12},{12,0},{1,5},{5,9},{9,13},{13,1},{2,6},{6,10},{... | collective-permute-start | bytes 1179656 | tf_op jit(solution)/shard_map/ppermute | solution.py:26
  28.5 12.0 %collective-permute-start.2 = (bf16[1,256,768]{2,1,0:T(8,128)(2,1)S(1)}, bf16[1,256,768]{2,1,0:T(8,128)(2,1)}, u32[]{:S(2)}, u32[]{:S(2)}) collective-permute-start(bf16[1,256,768]{2,1,0:T(8,128)(2,1)S(1)} %pad_bitcast_fusion.refs_0_), channel_id=1, source_target_pairs={{0,12},{4,0},{8,4},{12,8},{1,13},{5,1},{9,5},{13,9},{2,14},{6,2},{... | collective-permute-start | bytes 1179656 | tf_op jit(solution)/shard_map/ppermute | solution.py:26
  42.5 34.3 %all-to-all-start.1 = ((bf16[4,4,256,256]{3,2,1,0:T(8,128)(2,1)}), bf16[4,4,256,256]{3,2,1,0:T(8,128)(2,1)S(1)}, u32[]{:S(2)}, u32[]{:S(2)}) async-start(bf16[4,4,256,256]{3,2,1,0:T(8,128)(2,1)} %broadcast_in_dim.31), calls=%async_computation.1 | async-start | bytes 4194304 | tf_op jit(solution)/shard_map/all_to_all | solution.py:47
  47.0 15.7 %collective-permute-start.12 = (f32[64,688]{1,0:T(8,128)S(1)}, f32[64,688]{1,0:T(8,128)}, u32[]{:S(2)}, u32[]{:S(2)}) collective-permute-start(f32[64,688]{1,0:T(8,128)S(1)} %select_add_fusion), channel_id=1, source_target_pairs={{0,128},{128,0},{1,129},{129,1},{2,130},{130,2},{3,131},{131,3},{4... | collective-permute-start | bytes 528392 | tf_op jit(solution)/shard_map/ppermute | solution.py:26
  49.0 24.5 %collective-permute-start.5 = (bf16[1,256,768]{2,1,0:T(8,128)(2,1)}, bf16[1,256,768]{2,1,0:T(8,128)(2,1)}, u32[]{:S(2)}, u32[]{:S(2)}) collective-permute-start(bf16[1,256,768]{2,1,0:T(8,128)(2,1)} %copy-done.8), channel_id=1, source_target_pairs={{0,1},{1,2},{2,3},{3,0},{4,5},{5,6},{6,7},{7,4},{8,9},{9,10},{10,1... | collective-permute-start | bytes 1179656 | tf_op jit(solution)/shard_map/ppermute | solution.py:26
  49.9 23.6 %collective-permute-start.6 = (bf16[1,256,768]{2,1,0:T(8,128)(2,1)}, bf16[1,256,768]{2,1,0:T(8,128)(2,1)}, u32[]{:S(2)}, u32[]{:S(2)}) collective-permute-start(bf16[1,256,768]{2,1,0:T(8,128)(2,1)} %copy-done.8), channel_id=1, source_target_pairs={{0,3},{1,0},{2,1},{3,2},{4,7},{5,4},{6,5},{7,6},{8,11},{9,8},{10,9... | collective-permute-start | bytes 1179656 | tf_op jit(solution)/shard_map/ppermute | solution.py:26
  63.6 9.9 %collective-permute-start.14 = (f32[64,688]{1,0:T(8,128)S(1)}, f32[64,688]{1,0:T(8,128)S(1)}, u32[]{:S(2)}, u32[]{:S(2)}) collective-permute-start(f32[64,688]{1,0:T(8,128)S(1)} %add.57), channel_id=1, source_target_pairs={{0,32},{32,0},{64,96},{96,64},{1,33},{33,1},{65,97},{97,65},{2,34}... | collective-permute-start | bytes 528392 | tf_op jit(solution)/shard_map/ppermute | solution.py:220
  65.8 10.3 %collective-permute-start.1 = (bf16[1,128,768]{2,1,0:T(8,128)(2,1)S(1)}, bf16[1,128,768]{2,1,0:T(8,128)(2,1)S(1)}, u32[]{:S(2)}, u32[]{:S(2)}) collective-permute-start(bf16[1,128,768]{2,1,0:T(8,128)(2,1)S(1)} %slice.78), channel_id=1, source_target_pairs={{0,4},{4,8},{8,12},{12,0},{1,5},{5,9},{9,13},{13,1},{2,6},{6,10},{... | collective-permute-start | bytes 589832 | tf_op jit(solution)/shard_map/ppermute | solution.py:26
  68.7 8.0 %collective-permute-start.3 = (bf16[1,128,768]{2,1,0:T(8,128)(2,1)S(1)}, bf16[1,128,768]{2,1,0:T(8,128)(2,1)}, u32[]{:S(2)}, u32[]{:S(2)}) collective-permute-start(bf16[1,128,768]{2,1,0:T(8,128)(2,1)S(1)} %slice.79), channel_id=1, source_target_pairs={{0,12},{4,0},{8,4},{12,8},{1,13},{5,1},{9,5},{13,9},{2,14},{6,2},{... | collective-permute-start | bytes 589832 | tf_op jit(solution)/shard_map/ppermute | solution.py:26
  73.5 40.6 %collective-permute-start.26 = (bf16[688,688]{1,0:T(8,128)(2,1)S(1)}, bf16[688,688]{1,0:T(8,128)(2,1)}, u32[]{:S(2)}, u32[]{:S(2)}) collective-permute-start(bf16[688,688]{1,0:T(8,128)(2,1)S(1)} %copy-done.2), channel_id=1, source_target_pairs={{0,128},{128,0},{1,129},{129,1},{2,130},{130,2},{3,131},{131,3},{4... | collective-permute-start | bytes 2840072 | tf_op jit(solution)/shard_map/ppermute | solution.py:26
  84.0 30.1 %all-to-all-start.2 = ((bf16[4,320,256]{2,1,0:T(8,128)(2,1)}), bf16[4,320,256]{2,1,0:T(8,128)(2,1)S(1)}, u32[]{:S(2)}, u32[]{:S(2)}) async-start(bf16[4,320,256]{2,1,0:T(8,128)(2,1)} %broadcast_in_dim.32), calls=%async_computation.2 | async-start | bytes 1310720 | tf_op jit(solution)/shard_map/all_to_all | solution.py:47
  91.6 78.8 %all-gather.10.cloned.1.call-start = ((), (), s32[]{:S(2)}) async-start(), calls=%async_computation.6 | async-start | bytes 9510912 | tf_op jit(solution)/shard_map/all_gather | solution.py:243
  93.6 20.4 %collective-permute-start.7 = (bf16[2,256,768]{2,1,0:T(8,128)(2,1)S(1)}, bf16[2,256,768]{2,1,0:T(8,128)(2,1)S(1)}, u32[]{:S(2)}, u32[]{:S(2)}) collective-permute-start(bf16[2,256,768]{2,1,0:T(8,128)(2,1)S(1)} %constant_dynamic-update-slice_fusion.2.refs_5_), channel_id=1, source_target_pairs={{0,4},{4,8},{8,12},{12,0},{1,5},{5,9},{9,13},{13,1},{2,6},{6,10},{... | collective-permute-start | bytes 2359304 | tf_op jit(solution)/shard_map/ppermute | solution.py:26
  93.7 20.3 %collective-permute-start.9 = (bf16[2,256,768]{2,1,0:T(8,128)(2,1)S(1)}, bf16[2,256,768]{2,1,0:T(8,128)(2,1)}, u32[]{:S(2)}, u32[]{:S(2)}) collective-permute-start(bf16[2,256,768]{2,1,0:T(8,128)(2,1)S(1)} %constant_dynamic-update-slice_fusion.2.refs_5_), channel_id=1, source_target_pairs={{0,12},{4,0},{8,4},{12,8},{1,13},{5,1},{9,5},{13,9},{2,14},{6,2},{... | collective-permute-start | bytes 2359304 | tf_op jit(solution)/shard_map/ppermute | solution.py:26
  96.9 9.0 %collective-permute-start.23 = (f32[64,688]{1,0:T(8,128)S(1)}, f32[64,688]{1,0:T(8,128)S(1)}, u32[]{:S(2)}, u32[]{:S(2)}) collective-permute-start(f32[64,688]{1,0:T(8,128)S(1)} %add.58), channel_id=1, source_target_pairs={{0,64},{32,96},{64,0},{96,32},{1,65},{33,97},{65,1},{97,33},{2,66}... | collective-permute-start | bytes 528392 | tf_op jit(solution)/shard_map/ppermute | solution.py:241
  114.1 24.4 %collective-permute-start.16 = (bf16[4,320,256]{2,1,0:T(8,128)(2,1)S(1)}, bf16[4,320,256]{2,1,0:T(8,128)(2,1)S(1)}, u32[]{:S(2)}, u32[]{:S(2)}) collective-permute-start(bf16[4,320,256]{2,1,0:T(8,128)(2,1)S(1)} %all-to-all-done.2.refs_15_), channel_id=1, source_target_pairs={{0,12},{4,0},{8,4},{12,8},{1,13},{5,1},{9,5},{13,9},{2,14},{6,2},{... | collective-permute-start | bytes 1966088 | tf_op jit(solution)/shard_map/ppermute | solution.py:26
  118.4 20.0 %collective-permute-start.10 = (bf16[2,128,768]{2,1,0:T(8,128)(2,1)S(1)}, bf16[2,128,768]{2,1,0:T(8,128)(2,1)S(1)}, u32[]{:S(2)}, u32[]{:S(2)}) collective-permute-start(bf16[2,128,768]{2,1,0:T(8,128)(2,1)S(1)} %slice.81), channel_id=1, source_target_pairs={{0,12},{4,0},{8,4},{12,8},{1,13},{5,1},{9,5},{13,9},{2,14},{6,2},{... | collective-permute-start | bytes 1179656 | tf_op jit(solution)/shard_map/ppermute | solution.py:26
  118.6 19.9 %collective-permute-start.8 = (bf16[2,128,768]{2,1,0:T(8,128)(2,1)S(1)}, bf16[2,128,768]{2,1,0:T(8,128)(2,1)}, u32[]{:S(2)}, u32[]{:S(2)}) collective-permute-start(bf16[2,128,768]{2,1,0:T(8,128)(2,1)S(1)} %slice.80), channel_id=1, source_target_pairs={{0,4},{4,8},{8,12},{12,0},{1,5},{5,9},{9,13},{13,1},{2,6},{6,10},{... | collective-permute-start | bytes 1179656 | tf_op jit(solution)/shard_map/ppermute | solution.py:26
  120.7 23.1 %collective-permute-start.15 = (bf16[4,320,256]{2,1,0:T(8,128)(2,1)S(1)}, bf16[4,320,256]{2,1,0:T(8,128)(2,1)S(1)}, u32[]{:S(2)}, u32[]{:S(2)}) collective-permute-start(bf16[4,320,256]{2,1,0:T(8,128)(2,1)S(1)} %all-to-all-done.2.refs_15_), channel_id=1, source_target_pairs={{0,4},{4,8},{8,12},{12,0},{1,5},{5,9},{9,13},{13,1},{2,6},{6,10},{... | collective-permute-start | bytes 1966088 | tf_op jit(solution)/shard_map/ppermute | solution.py:26
  120.8 23.0 %collective-permute-start.13 = (bf16[1,256,768]{2,1,0:T(8,128)(2,1)}, bf16[1,256,768]{2,1,0:T(8,128)(2,1)}, u32[]{:S(2)}, u32[]{:S(2)}) collective-permute-start(bf16[1,256,768]{2,1,0:T(8,128)(2,1)} %copy-done.8), channel_id=1, source_target_pairs={{0,2},{1,3},{2,0},{3,1},{4,6},{5,7},{6,4},{7,5},{8,10},{9,11},{10,... | collective-permute-start | bytes 1179656 | tf_op jit(solution)/shard_map/ppermute | solution.py:26
  140.1 12.2 %collective-permute-start.22 = (bf16[4,160,256]{2,1,0:T(8,128)(2,1)}, bf16[4,160,256]{2,1,0:T(8,128)(2,1)S(1)}, u32[]{:S(2)}, u32[]{:S(2)}) collective-permute-start(bf16[4,160,256]{2,1,0:T(8,128)(2,1)} %slice.71), channel_id=1, source_target_pairs={{0,12},{4,0},{8,4},{12,8},{1,13},{5,1},{9,5},{13,9},{2,14},{6,2},{... | collective-permute-start | bytes 983048 | tf_op jit(solution)/shard_map/ppermute | solution.py:26
  143.8 10.2 %collective-permute-start.17 = (bf16[1,256,768]{2,1,0:T(8,128)(2,1)}, bf16[1,256,768]{2,1,0:T(8,128)(2,1)S(1)}, u32[]{:S(2)}, u32[]{:S(2)}) collective-permute-start(bf16[1,256,768]{2,1,0:T(8,128)(2,1)} %collective-permute-done.13.refs_10_), channel_id=1, source_target_pairs={{0,4},{4,8},{8,12},{12,0},{1,5},{5,9},{9,13},{13,1},{2,6},{6,10},{... | collective-permute-start | bytes 1179656 | tf_op jit(solution)/shard_map/ppermute | solution.py:26
  143.9 13.4 %collective-permute-start.19 = (bf16[1,256,768]{2,1,0:T(8,128)(2,1)}, bf16[1,256,768]{2,1,0:T(8,128)(2,1)S(1)}, u32[]{:S(2)}, u32[]{:S(2)}) collective-permute-start(bf16[1,256,768]{2,1,0:T(8,128)(2,1)} %collective-permute-done.13.refs_10_), channel_id=1, source_target_pairs={{0,12},{4,0},{8,4},{12,8},{1,13},{5,1},{9,5},{13,9},{2,14},{6,2},{... | collective-permute-start | bytes 1179656 | tf_op jit(solution)/shard_map/ppermute | solution.py:26
  153.2 17.2 %collective-permute-start.25 = (bf16[16,64,256]{2,1,0:T(8,128)(2,1)}, bf16[16,64,256]{2,1,0:T(8,128)(2,1)S(1)}, u32[]{:S(2)}, u32[]{:S(2)}) collective-permute-start(bf16[16,64,256]{2,1,0:T(8,128)(2,1)} %pad_maximum_fusion), channel_id=1, source_target_pairs={{0,16},{16,0},{1,17},{17,1},{2,18},{18,2},{3,19},{19,3},{4,20},{20... | collective-permute-start | bytes 1572872 | tf_op jit(solution)/shard_map/ppermute | solution.py:26
  153.3 9.1 %collective-permute-start.24 = (bf16[64,688]{1,0:T(8,128)(2,1)S(1)}, bf16[64,688]{1,0:T(8,128)(2,1)S(1)}, u32[]{:S(2)}, u32[]{:S(2)}) collective-permute-start(bf16[64,688]{1,0:T(8,128)(2,1)S(1)} %copy-done.15), channel_id=1, source_target_pairs={{0,16},{16,0},{1,17},{17,1},{2,18},{18,2},{3,19},{19,3},{4,20},{20... | collective-permute-start | bytes 264200 | tf_op jit(solution)/shard_map/ppermute | solution.py:26
  153.9 12.2 %collective-permute-start.21 = (bf16[4,160,256]{2,1,0:T(8,128)(2,1)S(1)}, bf16[4,160,256]{2,1,0:T(8,128)(2,1)S(1)}, u32[]{:S(2)}, u32[]{:S(2)}) collective-permute-start(bf16[4,160,256]{2,1,0:T(8,128)(2,1)S(1)} %slice.70), channel_id=1, source_target_pairs={{0,4},{4,8},{8,12},{12,0},{1,5},{5,9},{9,13},{13,1},{2,6},{6,10},{... | collective-permute-start | bytes 983048 | tf_op jit(solution)/shard_map/ppermute | solution.py:26
  154.0 15.6 %collective-permute-start.18 = (bf16[1,128,768]{2,1,0:T(8,128)(2,1)S(1)}, bf16[1,128,768]{2,1,0:T(8,128)(2,1)S(1)}, u32[]{:S(2)}, u32[]{:S(2)}) collective-permute-start(bf16[1,128,768]{2,1,0:T(8,128)(2,1)S(1)} %slice.84), channel_id=1, source_target_pairs={{0,4},{4,8},{8,12},{12,0},{1,5},{5,9},{9,13},{13,1},{2,6},{6,10},{... | collective-permute-start | bytes 589832 | tf_op jit(solution)/shard_map/ppermute | solution.py:26
  157.3 12.3 %collective-permute-start.20 = (bf16[1,128,768]{2,1,0:T(8,128)(2,1)S(1)}, bf16[1,128,768]{2,1,0:T(8,128)(2,1)S(1)}, u32[]{:S(2)}, u32[]{:S(2)}) collective-permute-start(bf16[1,128,768]{2,1,0:T(8,128)(2,1)S(1)} %slice.85), channel_id=1, source_target_pairs={{0,12},{4,0},{8,4},{12,8},{1,13},{5,1},{9,5},{13,9},{2,14},{6,2},{... | collective-permute-start | bytes 589832 | tf_op jit(solution)/shard_map/ppermute | solution.py:26
  (26 other events, 403.9 us)
Sparse Core Ops, SparseCore 0:
  16.3 31.8 all-gather.5
  50.0 58.5 all-gather.7
  114.2 52.7 all-gather.9

commit v6 on v5

--- a/solution.py
+++ b/solution.py
@@ -182,11 +182,11 @@
             pltpu.VMEM((16, height, padded), jnp.bfloat16),
             pltpu.VMEM((16,) + rows[0].shape[1:], jnp.bfloat16),
             pltpu.VMEM((height, cols), jnp.float32),
-            pltpu.VMEM((4, cols, width), jnp.float32),
-            pltpu.VMEM((4,) + near.shape[1:], jnp.bfloat16),
+            pltpu.VMEM((8, cols, width), jnp.float32),
+            pltpu.VMEM((8,) + near.shape[1:], jnp.bfloat16),
             pltpu.SemaphoreType.DMA((PIECES,)),
-            pltpu.SemaphoreType.DMA((4,)),
-            pltpu.SemaphoreType.DMA((4,)),
+            pltpu.SemaphoreType.DMA((8,)),
+            pltpu.SemaphoreType.DMA((8,)),
         ],
         out_shape=jax.ShapeDtypeStruct((factors, width), jnp.float32),
         compiler_params=pltpu.CompilerParams(vmem_limit_bytes=SCORE_LIMIT),

time: 221 us -> 221 us (level)
  no operation moved by 1% of the time
where the time goes in v6:
time: 221 us; the launch traced here: 220 us
  waiting for transfers between devices  69.3 us (31%)
  starting transfers between devices  67.7 us (31%)
  Pallas kernels  26.9 us (12%)
  blocking collectives  17.8 us (8%)
  local copies, waits for them, and re-layouts  17.4 us (8%)
  between operations  14.2 us (6%)
  other arithmetic  6.49 us (3%)
    ppermute x25, waiting for transfers between devices, shift(): lax.ppermute(block, axis, [(i, (i + step) % size) for i in range(size)])  56.6 us
    ppermute x25, starting transfers between devices, shift(): lax.ppermute(block, axis, [(i, (i + step) % size) for i in range(size)])  45.4 us
    pallas_call x1, Pallas kernels, score(): pl.pallas_call(score_kernel, in_specs=[smem] * 3 + [hbm] * PIECES + [vmem...  22.5 us
    all_to_all x3, starting transfers between devices, everyone(): lax.all_to_all(jnp.broadcast_to(block[None], (size,) + block.shape), axes...  20.3 us
    all_to_all x1, blocking collectives, local(): pieces = lax.all_to_all(partial.reshape(feats, 1, 1), FEAT, 0, 0)  17.8 us
    ppermute x1, waiting for transfers between devices, local(): lax.ppermute(after(right_x, in_rot), 'x', [(i, i ^ 2) for i in range(4)])  8.4 us
    unnamed x53, local copies, waits for them, and re-layouts  7.72 us
  transfers between devices with their start and end apart: 33, of which 13 were waited for; matrix products, arithmetic and copies ran while one was open for 6% of the time, Pallas kernels for 2%

profile of v6, /device:TPU:4, one launch (start us, length us, event | category | flops | bytes accessed | tf_op | source)
XLA Modules:
  0.0 220.2 jit_solution(9881344988359481930)
XLA Ops:
  8.5 2.0 collective-permute-start.4
  10.5 4.9 %collective-permute-done.4 = bf16[256,384]{1,0:T(8,128)(2,1)S(1)} collective-permute-done((bf16[256,384]{1,0:T(8,128)(2,1)S(1)}, bf16[256,384]{1,0:T(8,128)(2,1)S(1)}, u32[]{:S(2)}, u32[]{:S(2)}) %collective-permute-start.4) | collective-permute-done | bytes 196640 | tf_op jit(solution)/shard_map/ppermute | solution.py:26
  17.9 8.3 %all-to-all-start = ((bf16[4,256,256]{2,1,0:T(8,128)(2,1)}), bf16[4,256,256]{2,1,0:T(8,128)(2,1)S(1)}, u32[]{:S(2)}, u32[]{:S(2)}) async-start(bf16[4,256,256]{2,1,0:T(8,128)(2,1)} %broadcast_in_dim.14), calls=%async_computation | async-start | bytes 1048576 | tf_op jit(solution)/shard_map/all_to_all | solution.py:47
  26.9 1.7 collective-permute-start
  28.5 1.7 collective-permute-start.2
  30.2 9.5 %collective-permute-done.refs_1_ = bf16[1,256,768]{2,1,0:T(8,128)(2,1)S(1)} collective-permute-done((bf16[1,256,768]{2,1,0:T(8,128)(2,1)S(1)}, bf16[1,256,768]{2,1,0:T(8,128)(2,1)S(1)}, u32[]{:S(2)}, u32[]{:S(2)}) %collective-permute-start) | collective-permute-done | bytes 393248 | tf_op jit(solution)/shard_map/ppermute | solution.py:26
  42.5 4.5 %all-to-all-start.1 = ((bf16[4,4,256,256]{3,2,1,0:T(8,128)(2,1)}), bf16[4,4,256,256]{3,2,1,0:T(8,128)(2,1)S(1)}, u32[]{:S(2)}, u32[]{:S(2)}) async-start(bf16[4,4,256,256]{3,2,1,0:T(8,128)(2,1)} %broadcast_in_dim.31), calls=%async_computation.1 | async-start | bytes 4194304 | tf_op jit(solution)/shard_map/all_to_all | solution.py:47
  47.0 2.0 collective-permute-start.12
  49.9 3.2 %collective-permute-start.6 = (bf16[1,256,768]{2,1,0:T(8,128)(2,1)}, bf16[1,256,768]{2,1,0:T(8,128)(2,1)}, u32[]{:S(2)}, u32[]{:S(2)}) collective-permute-start(bf16[1,256,768]{2,1,0:T(8,128)(2,1)} %copy-done.8), channel_id=1, source_target_pairs={{0,3},{1,0},{2,1},{3,2},{4,7},{5,4},{6,5},{7,6},{8,11},{9,8},{10,9... | collective-permute-start | bytes 1179656 | tf_op jit(solution)/shard_map/ppermute | solution.py:26
  53.1 9.5 %collective-permute-done.12 = f32[64,688]{1,0:T(8,128)} collective-permute-done((f32[64,688]{1,0:T(8,128)S(1)}, f32[64,688]{1,0:T(8,128)}, u32[]{:S(2)}, u32[]{:S(2)}) %collective-permute-start.12) | collective-permute-done | bytes 176160 | tf_op jit(solution)/shard_map/ppermute | solution.py:26
  65.8 2.0 collective-permute-start.1
  70.3 3.2 %collective-permute-done.14 = f32[64,688]{1,0:T(8,128)S(1)} collective-permute-done((f32[64,688]{1,0:T(8,128)S(1)}, f32[64,688]{1,0:T(8,128)S(1)}, u32[]{:S(2)}, u32[]{:S(2)}) %collective-permute-start.14) | collective-permute-done | bytes 176160 | tf_op jit(solution)/shard_map/ppermute | solution.py:220
  73.5 2.5 %collective-permute-start.26 = (bf16[688,688]{1,0:T(8,128)(2,1)S(1)}, bf16[688,688]{1,0:T(8,128)(2,1)}, u32[]{:S(2)}, u32[]{:S(2)}) collective-permute-start(bf16[688,688]{1,0:T(8,128)(2,1)S(1)} %copy-done.2), channel_id=1, source_target_pairs={{0,128},{128,0},{1,129},{129,1},{2,130},{130,2},{3,131},{131,3},{4... | collective-permute-start | bytes 2840072 | tf_op jit(solution)/shard_map/ppermute | solution.py:26
  76.8 1.9 copy-done.1
  78.7 4.4 %shard_map.109 = bf16[320,256]{1,0:T(8,128)(2,1)S(1)} custom-call(s32[17]{0:T(128)S(1)} %pad_add_fusion.order, bf16[16,256,256]{2,1,0:T(8,128)(2,1)S(1)} %bitcast.13, bf16[16,256,384]{2,1,0:T(8,128)(2,1)S(1)} %copy-done.1), custom_call_target="tpu_custom_call" | custom-call | tf_op jit(solution)/shard_map/pallas_call | solution.py:79
  84.0 7.6 %all-to-all-start.2 = ((bf16[4,320,256]{2,1,0:T(8,128)(2,1)}), bf16[4,320,256]{2,1,0:T(8,128)(2,1)S(1)}, u32[]{:S(2)}, u32[]{:S(2)}) async-start(bf16[4,320,256]{2,1,0:T(8,128)(2,1)} %broadcast_in_dim.32), calls=%async_computation.2 | async-start | bytes 1310720 | tf_op jit(solution)/shard_map/all_to_all | solution.py:47
  93.7 3.2 %collective-permute-start.9 = (bf16[2,256,768]{2,1,0:T(8,128)(2,1)S(1)}, bf16[2,256,768]{2,1,0:T(8,128)(2,1)}, u32[]{:S(2)}, u32[]{:S(2)}) collective-permute-start(bf16[2,256,768]{2,1,0:T(8,128)(2,1)S(1)} %constant_dynamic-update-slice_fusion.2.refs_5_), channel_id=1, source_target_pairs={{0,12},{4,0},{8,4},{12,8},{1,13},{5,1},{9,5},{13,9},{2,14},{6,2},{... | collective-permute-start | bytes 2359304 | tf_op jit(solution)/shard_map/ppermute | solution.py:26
  97.6 8.4 %collective-permute-done.23 = f32[64,688]{1,0:T(8,128)S(1)} collective-permute-done((f32[64,688]{1,0:T(8,128)S(1)}, f32[64,688]{1,0:T(8,128)S(1)}, u32[]{:S(2)}, u32[]{:S(2)}) %collective-permute-start.23) | collective-permute-done | bytes 176160 | tf_op jit(solution)/shard_map/ppermute | solution.py:241
  106.6 7.4 %collective-permute-done.7.refs_6_ = bf16[2,256,768]{2,1,0:T(8,128)(2,1)S(1)} collective-permute-done((bf16[2,256,768]{2,1,0:T(8,128)(2,1)S(1)}, bf16[2,256,768]{2,1,0:T(8,128)(2,1)S(1)}, u32[]{:S(2)}, u32[]{:S(2)}) %collective-permute-start.7) | collective-permute-done | bytes 786464 | tf_op jit(solution)/shard_map/ppermute | solution.py:26
  114.1 3.3 %collective-permute-start.16 = (bf16[4,320,256]{2,1,0:T(8,128)(2,1)S(1)}, bf16[4,320,256]{2,1,0:T(8,128)(2,1)S(1)}, u32[]{:S(2)}, u32[]{:S(2)}) collective-permute-start(bf16[4,320,256]{2,1,0:T(8,128)(2,1)S(1)} %all-to-all-done.2.refs_15_), channel_id=1, source_target_pairs={{0,12},{4,0},{8,4},{12,8},{1,13},{5,1},{9,5},{13,9},{2,14},{6,2},{... | collective-permute-start | bytes 1966088 | tf_op jit(solution)/shard_map/ppermute | solution.py:26
  118.6 2.1 collective-permute-start.8
  120.8 5.7 %collective-permute-start.13 = (bf16[1,256,768]{2,1,0:T(8,128)(2,1)}, bf16[1,256,768]{2,1,0:T(8,128)(2,1)}, u32[]{:S(2)}, u32[]{:S(2)}) collective-permute-start(bf16[1,256,768]{2,1,0:T(8,128)(2,1)} %copy-done.8), channel_id=1, source_target_pairs={{0,2},{1,3},{2,0},{3,1},{4,6},{5,7},{6,4},{7,5},{8,10},{9,11},{10,... | collective-permute-start | bytes 1179656 | tf_op jit(solution)/shard_map/ppermute | solution.py:26
  126.5 12.0 %collective-permute-done.10.refs_8_ = bf16[2,128,768]{2,1,0:T(8,128)(2,1)S(1)} collective-permute-done((bf16[2,128,768]{2,1,0:T(8,128)(2,1)S(1)}, bf16[2,128,768]{2,1,0:T(8,128)(2,1)S(1)}, u32[]{:S(2)}, u32[]{:S(2)}) %collective-permute-start.10) | collective-permute-done | bytes 393248 | tf_op jit(solution)/shard_map/ppermute | solution.py:26
  140.1 3.7 %collective-permute-start.22 = (bf16[4,160,256]{2,1,0:T(8,128)(2,1)}, bf16[4,160,256]{2,1,0:T(8,128)(2,1)S(1)}, u32[]{:S(2)}, u32[]{:S(2)}) collective-permute-start(bf16[4,160,256]{2,1,0:T(8,128)(2,1)} %slice.71), channel_id=1, source_target_pairs={{0,12},{4,0},{8,4},{12,8},{1,13},{5,1},{9,5},{13,9},{2,14},{6,2},{... | collective-permute-start | bytes 983048 | tf_op jit(solution)/shard_map/ppermute | solution.py:26
  143.9 3.2 %collective-permute-start.19 = (bf16[1,256,768]{2,1,0:T(8,128)(2,1)}, bf16[1,256,768]{2,1,0:T(8,128)(2,1)S(1)}, u32[]{:S(2)}, u32[]{:S(2)}) collective-permute-start(bf16[1,256,768]{2,1,0:T(8,128)(2,1)} %collective-permute-done.13.refs_10_), channel_id=1, source_target_pairs={{0,12},{4,0},{8,4},{12,8},{1,13},{5,1},{9,5},{13,9},{2,14},{6,2},{... | collective-permute-start | bytes 1179656 | tf_op jit(solution)/shard_map/ppermute | solution.py:26
  147.1 5.1 %collective-permute-done.22.refs_18_ = bf16[4,160,256]{2,1,0:T(8,128)(2,1)S(1)} collective-permute-done((bf16[4,160,256]{2,1,0:T(8,128)(2,1)}, bf16[4,160,256]{2,1,0:T(8,128)(2,1)S(1)}, u32[]{:S(2)}, u32[]{:S(2)}) %collective-permute-start.22) | collective-permute-done | bytes 327712 | tf_op jit(solution)/shard_map/ppermute | solution.py:26
  154.0 1.8 collective-permute-start.18
  157.3 3.9 %collective-permute-start.20 = (bf16[1,128,768]{2,1,0:T(8,128)(2,1)S(1)}, bf16[1,128,768]{2,1,0:T(8,128)(2,1)S(1)}, u32[]{:S(2)}, u32[]{:S(2)}) collective-permute-start(bf16[1,128,768]{2,1,0:T(8,128)(2,1)S(1)} %slice.85), channel_id=1, source_target_pairs={{0,12},{4,0},{8,4},{12,8},{1,13},{5,1},{9,5},{13,9},{2,14},{6,2},{... | collective-permute-start | bytes 589832 | tf_op jit(solution)/shard_map/ppermute | solution.py:26
  163.1 2.9 %collective-permute-done.21.refs_17_ = bf16[4,160,256]{2,1,0:T(8,128)(2,1)S(1)} collective-permute-done((bf16[4,160,256]{2,1,0:T(8,128)(2,1)S(1)}, bf16[4,160,256]{2,1,0:T(8,128)(2,1)S(1)}, u32[]{:S(2)}, u32[]{:S(2)}) %collective-permute-start.21) | collective-permute-done | bytes 327712 | tf_op jit(solution)/shard_map/ppermute | solution.py:26
  166.1 3.6 %collective-permute-done.18.refs_12_ = bf16[1,128,768]{2,1,0:T(8,128)(2,1)S(1)} collective-permute-done((bf16[1,128,768]{2,1,0:T(8,128)(2,1)S(1)}, bf16[1,128,768]{2,1,0:T(8,128)(2,1)S(1)}, u32[]{:S(2)}, u32[]{:S(2)}) %collective-permute-start.18) | collective-permute-done | bytes 196640 | tf_op jit(solution)/shard_map/ppermute | solution.py:26
  171.2 22.5 %shard_map.110 = f32[128,256]{1,0:T(8,128)} custom-call(s32[16]{0:T(128)} %get-tuple-element.33.order, s32[16]{0:T(128)} %get-tuple-element.34.columns, s32[1]{0:T(128)S(6)} %copy.25.live, bf16[1,256,768]{2,1,0:T(8,128)(2,1)} %copy-done.8, bf16[1,256,768]{2,1,0:T(8,128)(2,1)} %copy-done.9, bf16[1,128,768]{2,1,0:T(8,128)(2,1)} %copy-done.18, ...), custom_call_target="tpu_custom_call" | custom-call | tf_op jit(solution)/shard_map/pallas_call | solution.py:177
  195.2 17.8 %all_to_all.20 = f32[16,1,1]{2,1,0:T(1,128)S(1)} all-to-all(f32[16,1,1]{2,1,0:T(1,128)S(1)} %copy.21), channel_id=1, replica_groups=mesh['zlo'=2,'x'=4,'core'=2,'y'=4,'zhi'=4] {'y','zhi'}, dimensions={0} | all-to-all | bytes 128 | tf_op jit(solution)/shard_map/all_to_all | solution.py:273
  (134 shorter events, 30.6 us)
Async XLA Ops:
  6.5 70.3 %all-gather.6.cloned.1.call-start = ((), (), s32[]{:S(2)}) async-start(), calls=%async_computation.4 | async-start | bytes 3538944 | tf_op jit(solution)/shard_map/all_gather | solution.py:210
  8.5 6.9 %collective-permute-start.4 = (bf16[256,384]{1,0:T(8,128)(2,1)S(1)}, bf16[256,384]{1,0:T(8,128)(2,1)S(1)}, u32[]{:S(2)}, u32[]{:S(2)}) collective-permute-start(bf16[256,384]{1,0:T(8,128)(2,1)S(1)} %constant_dynamic-update-slice_fusion), channel_id=1, source_target_pairs={{0,128},{128,0},{1,129},{129,1},{2,130},{130,2},{3,131},{131,3},{4... | collective-permute-start | bytes 589832 | tf_op jit(solution)/shard_map/ppermute | solution.py:26
  16.2 154.1 %all-gather.8.cloned.1.call-start = ((), (), s32[]{:S(2)}) async-start(), calls=%async_computation.5 | async-start | bytes 9510912 | tf_op jit(solution)/shard_map/all_gather | solution.py:211
  17.9 23.1 %all-to-all-start = ((bf16[4,256,256]{2,1,0:T(8,128)(2,1)}), bf16[4,256,256]{2,1,0:T(8,128)(2,1)S(1)}, u32[]{:S(2)}, u32[]{:S(2)}) async-start(bf16[4,256,256]{2,1,0:T(8,128)(2,1)} %broadcast_in_dim.14), calls=%async_computation | async-start | bytes 1048576 | tf_op jit(solution)/shard_map/all_to_all | solution.py:47
  26.9 12.9 %collective-permute-start = (bf16[1,256,768]{2,1,0:T(8,128)(2,1)S(1)}, bf16[1,256,768]{2,1,0:T(8,128)(2,1)S(1)}, u32[]{:S(2)}, u32[]{:S(2)}) collective-permute-start(bf16[1,256,768]{2,1,0:T(8,128)(2,1)S(1)} %pad_bitcast_fusion.refs_0_), channel_id=1, source_target_pairs={{0,4},{4,8},{8,12},{12,0},{1,5},{5,9},{9,13},{13,1},{2,6},{6,10},{... | collective-permute-start | bytes 1179656 | tf_op jit(solution)/shard_map/ppermute | solution.py:26
  28.5 12.0 %collective-permute-start.2 = (bf16[1,256,768]{2,1,0:T(8,128)(2,1)S(1)}, bf16[1,256,768]{2,1,0:T(8,128)(2,1)}, u32[]{:S(2)}, u32[]{:S(2)}) collective-permute-start(bf16[1,256,768]{2,1,0:T(8,128)(2,1)S(1)} %pad_bitcast_fusion.refs_0_), channel_id=1, source_target_pairs={{0,12},{4,0},{8,4},{12,8},{1,13},{5,1},{9,5},{13,9},{2,14},{6,2},{... | collective-permute-start | bytes 1179656 | tf_op jit(solution)/shard_map/ppermute | solution.py:26
  42.5 34.3 %all-to-all-start.1 = ((bf16[4,4,256,256]{3,2,1,0:T(8,128)(2,1)}), bf16[4,4,256,256]{3,2,1,0:T(8,128)(2,1)S(1)}, u32[]{:S(2)}, u32[]{:S(2)}) async-start(bf16[4,4,256,256]{3,2,1,0:T(8,128)(2,1)} %broadcast_in_dim.31), calls=%async_computation.1 | async-start | bytes 4194304 | tf_op jit(solution)/shard_map/all_to_all | solution.py:47
  47.0 15.7 %collective-permute-start.12 = (f32[64,688]{1,0:T(8,128)S(1)}, f32[64,688]{1,0:T(8,128)}, u32[]{:S(2)}, u32[]{:S(2)}) collective-permute-start(f32[64,688]{1,0:T(8,128)S(1)} %select_add_fusion), channel_id=1, source_target_pairs={{0,128},{128,0},{1,129},{129,1},{2,130},{130,2},{3,131},{131,3},{4... | collective-permute-start | bytes 528392 | tf_op jit(solution)/shard_map/ppermute | solution.py:26
  49.0 24.5 %collective-permute-start.5 = (bf16[1,256,768]{2,1,0:T(8,128)(2,1)}, bf16[1,256,768]{2,1,0:T(8,128)(2,1)}, u32[]{:S(2)}, u32[]{:S(2)}) collective-permute-start(bf16[1,256,768]{2,1,0:T(8,128)(2,1)} %copy-done.8), channel_id=1, source_target_pairs={{0,1},{1,2},{2,3},{3,0},{4,5},{5,6},{6,7},{7,4},{8,9},{9,10},{10,1... | collective-permute-start | bytes 1179656 | tf_op jit(solution)/shard_map/ppermute | solution.py:26
  49.9 23.6 %collective-permute-start.6 = (bf16[1,256,768]{2,1,0:T(8,128)(2,1)}, bf16[1,256,768]{2,1,0:T(8,128)(2,1)}, u32[]{:S(2)}, u32[]{:S(2)}) collective-permute-start(bf16[1,256,768]{2,1,0:T(8,128)(2,1)} %copy-done.8), channel_id=1, source_target_pairs={{0,3},{1,0},{2,1},{3,2},{4,7},{5,4},{6,5},{7,6},{8,11},{9,8},{10,9... | collective-permute-start | bytes 1179656 | tf_op jit(solution)/shard_map/ppermute | solution.py:26
  63.6 9.9 %collective-permute-start.14 = (f32[64,688]{1,0:T(8,128)S(1)}, f32[64,688]{1,0:T(8,128)S(1)}, u32[]{:S(2)}, u32[]{:S(2)}) collective-permute-start(f32[64,688]{1,0:T(8,128)S(1)} %add.57), channel_id=1, source_target_pairs={{0,32},{32,0},{64,96},{96,64},{1,33},{33,1},{65,97},{97,65},{2,34}... | collective-permute-start | bytes 528392 | tf_op jit(solution)/shard_map/ppermute | solution.py:220
  65.8 10.3 %collective-permute-start.1 = (bf16[1,128,768]{2,1,0:T(8,128)(2,1)S(1)}, bf16[1,128,768]{2,1,0:T(8,128)(2,1)S(1)}, u32[]{:S(2)}, u32[]{:S(2)}) collective-permute-start(bf16[1,128,768]{2,1,0:T(8,128)(2,1)S(1)} %slice.78), channel_id=1, source_target_pairs={{0,4},{4,8},{8,12},{12,0},{1,5},{5,9},{9,13},{13,1},{2,6},{6,10},{... | collective-permute-start | bytes 589832 | tf_op jit(solution)/shard_map/ppermute | solution.py:26
  68.7 8.0 %collective-permute-start.3 = (bf16[1,128,768]{2,1,0:T(8,128)(2,1)S(1)}, bf16[1,128,768]{2,1,0:T(8,128)(2,1)}, u32[]{:S(2)}, u32[]{:S(2)}) collective-permute-start(bf16[1,128,768]{2,1,0:T(8,128)(2,1)S(1)} %slice.79), channel_id=1, source_target_pairs={{0,12},{4,0},{8,4},{12,8},{1,13},{5,1},{9,5},{13,9},{2,14},{6,2},{... | collective-permute-start | bytes 589832 | tf_op jit(solution)/shard_map/ppermute | solution.py:26
  73.5 40.6 %collective-permute-start.26 = (bf16[688,688]{1,0:T(8,128)(2,1)S(1)}, bf16[688,688]{1,0:T(8,128)(2,1)}, u32[]{:S(2)}, u32[]{:S(2)}) collective-permute-start(bf16[688,688]{1,0:T(8,128)(2,1)S(1)} %copy-done.2), channel_id=1, source_target_pairs={{0,128},{128,0},{1,129},{129,1},{2,130},{130,2},{3,131},{131,3},{4... | collective-permute-start | bytes 2840072 | tf_op jit(solution)/shard_map/ppermute | solution.py:26
  84.0 30.1 %all-to-all-start.2 = ((bf16[4,320,256]{2,1,0:T(8,128)(2,1)}), bf16[4,320,256]{2,1,0:T(8,128)(2,1)S(1)}, u32[]{:S(2)}, u32[]{:S(2)}) async-start(bf16[4,320,256]{2,1,0:T(8,128)(2,1)} %broadcast_in_dim.32), calls=%async_computation.2 | async-start | bytes 1310720 | tf_op jit(solution)/shard_map/all_to_all | solution.py:47
  91.6 78.8 %all-gather.10.cloned.1.call-start = ((), (), s32[]{:S(2)}) async-start(), calls=%async_computation.6 | async-start | bytes 9510912 | tf_op jit(solution)/shard_map/all_gather | solution.py:243
  93.6 20.4 %collective-permute-start.7 = (bf16[2,256,768]{2,1,0:T(8,128)(2,1)S(1)}, bf16[2,256,768]{2,1,0:T(8,128)(2,1)S(1)}, u32[]{:S(2)}, u32[]{:S(2)}) collective-permute-start(bf16[2,256,768]{2,1,0:T(8,128)(2,1)S(1)} %constant_dynamic-update-slice_fusion.2.refs_5_), channel_id=1, source_target_pairs={{0,4},{4,8},{8,12},{12,0},{1,5},{5,9},{9,13},{13,1},{2,6},{6,10},{... | collective-permute-start | bytes 2359304 | tf_op jit(solution)/shard_map/ppermute | solution.py:26
  93.7 20.3 %collective-permute-start.9 = (bf16[2,256,768]{2,1,0:T(8,128)(2,1)S(1)}, bf16[2,256,768]{2,1,0:T(8,128)(2,1)}, u32[]{:S(2)}, u32[]{:S(2)}) collective-permute-start(bf16[2,256,768]{2,1,0:T(8,128)(2,1)S(1)} %constant_dynamic-update-slice_fusion.2.refs_5_), channel_id=1, source_target_pairs={{0,12},{4,0},{8,4},{12,8},{1,13},{5,1},{9,5},{13,9},{2,14},{6,2},{... | collective-permute-start | bytes 2359304 | tf_op jit(solution)/shard_map/ppermute | solution.py:26
  96.9 9.0 %collective-permute-start.23 = (f32[64,688]{1,0:T(8,128)S(1)}, f32[64,688]{1,0:T(8,128)S(1)}, u32[]{:S(2)}, u32[]{:S(2)}) collective-permute-start(f32[64,688]{1,0:T(8,128)S(1)} %add.58), channel_id=1, source_target_pairs={{0,64},{32,96},{64,0},{96,32},{1,65},{33,97},{65,1},{97,33},{2,66}... | collective-permute-start | bytes 528392 | tf_op jit(solution)/shard_map/ppermute | solution.py:241
  114.1 24.4 %collective-permute-start.16 = (bf16[4,320,256]{2,1,0:T(8,128)(2,1)S(1)}, bf16[4,320,256]{2,1,0:T(8,128)(2,1)S(1)}, u32[]{:S(2)}, u32[]{:S(2)}) collective-permute-start(bf16[4,320,256]{2,1,0:T(8,128)(2,1)S(1)} %all-to-all-done.2.refs_15_), channel_id=1, source_target_pairs={{0,12},{4,0},{8,4},{12,8},{1,13},{5,1},{9,5},{13,9},{2,14},{6,2},{... | collective-permute-start | bytes 1966088 | tf_op jit(solution)/shard_map/ppermute | solution.py:26
  118.4 20.0 %collective-permute-start.10 = (bf16[2,128,768]{2,1,0:T(8,128)(2,1)S(1)}, bf16[2,128,768]{2,1,0:T(8,128)(2,1)S(1)}, u32[]{:S(2)}, u32[]{:S(2)}) collective-permute-start(bf16[2,128,768]{2,1,0:T(8,128)(2,1)S(1)} %slice.81), channel_id=1, source_target_pairs={{0,12},{4,0},{8,4},{12,8},{1,13},{5,1},{9,5},{13,9},{2,14},{6,2},{... | collective-permute-start | bytes 1179656 | tf_op jit(solution)/shard_map/ppermute | solution.py:26
  118.6 19.9 %collective-permute-start.8 = (bf16[2,128,768]{2,1,0:T(8,128)(2,1)S(1)}, bf16[2,128,768]{2,1,0:T(8,128)(2,1)}, u32[]{:S(2)}, u32[]{:S(2)}) collective-permute-start(bf16[2,128,768]{2,1,0:T(8,128)(2,1)S(1)} %slice.80), channel_id=1, source_target_pairs={{0,4},{4,8},{8,12},{12,0},{1,5},{5,9},{9,13},{13,1},{2,6},{6,10},{... | collective-permute-start | bytes 1179656 | tf_op jit(solution)/shard_map/ppermute | solution.py:26
  120.7 23.1 %collective-permute-start.15 = (bf16[4,320,256]{2,1,0:T(8,128)(2,1)S(1)}, bf16[4,320,256]{2,1,0:T(8,128)(2,1)S(1)}, u32[]{:S(2)}, u32[]{:S(2)}) collective-permute-start(bf16[4,320,256]{2,1,0:T(8,128)(2,1)S(1)} %all-to-all-done.2.refs_15_), channel_id=1, source_target_pairs={{0,4},{4,8},{8,12},{12,0},{1,5},{5,9},{9,13},{13,1},{2,6},{6,10},{... | collective-permute-start | bytes 1966088 | tf_op jit(solution)/shard_map/ppermute | solution.py:26
  120.8 23.0 %collective-permute-start.13 = (bf16[1,256,768]{2,1,0:T(8,128)(2,1)}, bf16[1,256,768]{2,1,0:T(8,128)(2,1)}, u32[]{:S(2)}, u32[]{:S(2)}) collective-permute-start(bf16[1,256,768]{2,1,0:T(8,128)(2,1)} %copy-done.8), channel_id=1, source_target_pairs={{0,2},{1,3},{2,0},{3,1},{4,6},{5,7},{6,4},{7,5},{8,10},{9,11},{10,... | collective-permute-start | bytes 1179656 | tf_op jit(solution)/shard_map/ppermute | solution.py:26
  140.1 12.2 %collective-permute-start.22 = (bf16[4,160,256]{2,1,0:T(8,128)(2,1)}, bf16[4,160,256]{2,1,0:T(8,128)(2,1)S(1)}, u32[]{:S(2)}, u32[]{:S(2)}) collective-permute-start(bf16[4,160,256]{2,1,0:T(8,128)(2,1)} %slice.71), channel_id=1, source_target_pairs={{0,12},{4,0},{8,4},{12,8},{1,13},{5,1},{9,5},{13,9},{2,14},{6,2},{... | collective-permute-start | bytes 983048 | tf_op jit(solution)/shard_map/ppermute | solution.py:26
  143.8 10.2 %collective-permute-start.17 = (bf16[1,256,768]{2,1,0:T(8,128)(2,1)}, bf16[1,256,768]{2,1,0:T(8,128)(2,1)S(1)}, u32[]{:S(2)}, u32[]{:S(2)}) collective-permute-start(bf16[1,256,768]{2,1,0:T(8,128)(2,1)} %collective-permute-done.13.refs_10_), channel_id=1, source_target_pairs={{0,4},{4,8},{8,12},{12,0},{1,5},{5,9},{9,13},{13,1},{2,6},{6,10},{... | collective-permute-start | bytes 1179656 | tf_op jit(solution)/shard_map/ppermute | solution.py:26
  143.9 13.4 %collective-permute-start.19 = (bf16[1,256,768]{2,1,0:T(8,128)(2,1)}, bf16[1,256,768]{2,1,0:T(8,128)(2,1)S(1)}, u32[]{:S(2)}, u32[]{:S(2)}) collective-permute-start(bf16[1,256,768]{2,1,0:T(8,128)(2,1)} %collective-permute-done.13.refs_10_), channel_id=1, source_target_pairs={{0,12},{4,0},{8,4},{12,8},{1,13},{5,1},{9,5},{13,9},{2,14},{6,2},{... | collective-permute-start | bytes 1179656 | tf_op jit(solution)/shard_map/ppermute | solution.py:26
  153.2 17.2 %collective-permute-start.25 = (bf16[16,64,256]{2,1,0:T(8,128)(2,1)}, bf16[16,64,256]{2,1,0:T(8,128)(2,1)S(1)}, u32[]{:S(2)}, u32[]{:S(2)}) collective-permute-start(bf16[16,64,256]{2,1,0:T(8,128)(2,1)} %pad_maximum_fusion), channel_id=1, source_target_pairs={{0,16},{16,0},{1,17},{17,1},{2,18},{18,2},{3,19},{19,3},{4,20},{20... | collective-permute-start | bytes 1572872 | tf_op jit(solution)/shard_map/ppermute | solution.py:26
  153.3 9.1 %collective-permute-start.24 = (bf16[64,688]{1,0:T(8,128)(2,1)S(1)}, bf16[64,688]{1,0:T(8,128)(2,1)S(1)}, u32[]{:S(2)}, u32[]{:S(2)}) collective-permute-start(bf16[64,688]{1,0:T(8,128)(2,1)S(1)} %copy-done.15), channel_id=1, source_target_pairs={{0,16},{16,0},{1,17},{17,1},{2,18},{18,2},{3,19},{19,3},{4,20},{20... | collective-permute-start | bytes 264200 | tf_op jit(solution)/shard_map/ppermute | solution.py:26
  153.9 12.2 %collective-permute-start.21 = (bf16[4,160,256]{2,1,0:T(8,128)(2,1)S(1)}, bf16[4,160,256]{2,1,0:T(8,128)(2,1)S(1)}, u32[]{:S(2)}, u32[]{:S(2)}) collective-permute-start(bf16[4,160,256]{2,1,0:T(8,128)(2,1)S(1)} %slice.70), channel_id=1, source_target_pairs={{0,4},{4,8},{8,12},{12,0},{1,5},{5,9},{9,13},{13,1},{2,6},{6,10},{... | collective-permute-start | bytes 983048 | tf_op jit(solution)/shard_map/ppermute | solution.py:26
  154.0 15.6 %collective-permute-start.18 = (bf16[1,128,768]{2,1,0:T(8,128)(2,1)S(1)}, bf16[1,128,768]{2,1,0:T(8,128)(2,1)S(1)}, u32[]{:S(2)}, u32[]{:S(2)}) collective-permute-start(bf16[1,128,768]{2,1,0:T(8,128)(2,1)S(1)} %slice.84), channel_id=1, source_target_pairs={{0,4},{4,8},{8,12},{12,0},{1,5},{5,9},{9,13},{13,1},{2,6},{6,10},{... | collective-permute-start | bytes 589832 | tf_op jit(solution)/shard_map/ppermute | solution.py:26
  157.3 12.3 %collective-permute-start.20 = (bf16[1,128,768]{2,1,0:T(8,128)(2,1)S(1)}, bf16[1,128,768]{2,1,0:T(8,128)(2,1)S(1)}, u32[]{:S(2)}, u32[]{:S(2)}) collective-permute-start(bf16[1,128,768]{2,1,0:T(8,128)(2,1)S(1)} %slice.85), channel_id=1, source_target_pairs={{0,12},{4,0},{8,4},{12,8},{1,13},{5,1},{9,5},{13,9},{2,14},{6,2},{... | collective-permute-start | bytes 589832 | tf_op jit(solution)/shard_map/ppermute | solution.py:26
  (26 other events, 403.9 us)
Sparse Core Ops, SparseCore 0:
  16.3 31.8 all-gather.5
  50.0 58.5 all-gather.7
  114.2 52.7 all-gather.9
